TPU v7x, 128 devices: a whole 4x4x4 slice. The times are simulated.
128 devices in a mesh: seq: 8 (over x_lo, z), ctx: 16 (over y, x_hi, core).
Axes of the slice: x: 4 (x_hi: 2, x_lo: 2; x = x_hi * 2 + x_lo), y: 4, z: 4, core: 2. Of those that a mesh axis runs over, the one named last changes fastest.
Arguments:
- block_in: bfloat16 [8, 2048, 1536], P('seq', 'ctx'), may hold values from -6 to 6
- routes: int32 [8, 2048, 8], P('seq', 'ctx'), may hold values from 0 to 31, all different within a row; in each aligned block of 128 rows (0 to 127, 128 to 255, ..., all dimensions but the last counted through in order) at most 48 rows name the same one
- cotangent: bfloat16 [8, 2048, 1536], P('seq', 'ctx'), may hold values from -6 to 6
- gain_attn: bfloat16 [1536], P(('seq', 'ctx')), may hold values from 0.099609375 to 1.8984375
- w_query: bfloat16 [1536, 1536], P(('seq', 'ctx')), may hold values from -0.21875 to 0.21875
- key_weight: bfloat16 [1536, 512], P(('seq', 'ctx')), may hold values from -0.21875 to 0.21875
- value_weight: bfloat16 [1536, 512], P(('seq', 'ctx')), may hold values from -0.15625 to 0.15625
- w_out: bfloat16 [1536, 1536], P(('seq', 'ctx')), may hold values from -1.75 to 1.75
- gain_ffn: bfloat16 [1536], P(('seq', 'ctx')), may hold values from 0.099609375 to 1.8984375
- w_router: bfloat16 [1536, 32], P(('seq', 'ctx')), may hold values from -0.078125 to 0.078125
- w_gate: bfloat16 [32, 1536, 512], P('ctx', 'seq'), may hold values from -0.15625 to 0.15625
- w_up: bfloat16 [32, 1536, 512], P('ctx', 'seq'), may hold values from -0.15625 to 0.15625
- w_down: bfloat16 [32, 512, 1536], P('ctx', 'seq'), may hold values from -1 to 1
Outputs:
- block_out: bfloat16 [8, 2048, 1536], P('seq', 'ctx')
- grad_in: float32 [8, 2048, 1536], P('seq', 'ctx')
- grad_gain_attn: float32 [1536], P(('seq', 'ctx'))
- grad_query: float32 [1536, 1536], P(('seq', 'ctx'))
- key_weight_gradient: float32 [1536, 512], P(('seq', 'ctx'))
- value_weight_gradient: float32 [1536, 512], P(('seq', 'ctx'))
- grad_out: float32 [1536, 1536], P(('seq', 'ctx'))
- grad_gain_ffn: float32 [1536], P(('seq', 'ctx'))
- grad_router: float32 [1536, 32], P(('seq', 'ctx'))
- grad_gate: float32 [32, 1536, 512], P('ctx', 'seq')
- grad_up: float32 [32, 1536, 512], P('ctx', 'seq')
- grad_down: float32 [32, 512, 1536], P('ctx', 'seq')
Inputs may be any that keep to these rules, and one draw needn't show every extreme that they name: `routes`: each token names 8 different experts. Within the rows of one device (aligned blocks of 128 tokens) no expert is named by more than 48 tokens, a bound that some block reaches of one device in every draw.
All inputs are finite; a program needn't handle non-finite values.
Results may differ from a plain program's by a relative error of at most 0.02.
The roundings to bfloat16 on the way count: a program that leaves them out, or rounds other values in their place, can miss the bound.
Values may be sent and summed in bfloat16 or wider, within the bound.
A program may use at most 192 MiB of HBM per device.

v0:
```python
import math

import jax
import jax.numpy as jnp
from jax import lax
from jax.sharding import PartitionSpec as P

QUERY_HEADS = 24
KEY_VALUE_HEADS = 8
HEAD_WIDTH = 64
TOPK = 8


EPSILON = 1e-06
HIGHEST = lax.Precision.HIGHEST


def sent_together(arrays, axis, dim, along):
    columns = [a.reshape(*a.shape[:along], -1) for a in arrays]
    both = jnp.concatenate(columns, axis=along)
    result, at, finished = (lax.all_gather(both, axis, axis=dim, tiled=True), 0, [])
    for a, column in zip(arrays, columns):
        share = result[..., at : at + column.shape[along]]
        finished.append(share.reshape(*share.shape[:along], *a.shape[along:]))
        at += column.shape[along]
    return tuple(finished)


def in_one_piece(arrays, axis, dim, along):
    ends, at = ([], 0)
    for a in arrays[:-1]:
        at += a.shape[along]
        ends.append(at)
    both = jnp.concatenate(arrays, axis=along)
    return tuple(jnp.split(lax.all_gather(both, axis, axis=dim, tiled=True), ends, axis=along))


def in_one_piece_2(arrays, axis, dim, along):
    ends, at = ([], 0)
    for a in arrays[:-1]:
        at += a.shape[along]
        ends.append(at)
    both = jnp.concatenate(arrays, axis=along)
    return tuple(
        jnp.split(lax.psum_scatter(both, axis, scatter_dimension=dim, tiled=True), ends, axis=along)
    )


def in_blocks(value, dim, peers):
    dims = value.shape
    parts = value.reshape(*dims[:dim], peers, dims[dim] // peers, *dims[dim + 1 :])
    return jnp.moveaxis(parts, dim, 0)


def one_scatter(arrays, axis, dims):
    peers = lax.axis_size(axis)
    parts = [in_blocks(a, dim, peers) for a, dim in zip(arrays, dims)]
    lines = jnp.concatenate([b.reshape(peers, -1) for b in parts], axis=1)
    span = max(16, -(-lines.shape[1] // 1024) * 8)
    lines = jnp.pad(lines, ((0, 0), (0, span * 128 - lines.shape[1]))).reshape(-1, 128)
    flat, at, finished = (lax.psum_scatter(lines, axis, tiled=True).reshape(-1), 0, [])
    for b in parts:
        part = b[0]
        finished.append(flat[at : at + part.size].reshape(part.shape))
        at += part.size
    return tuple(finished)


def elementwise_product(left_side, right_side):
    return jnp.dot(left_side, right_side, preferred_element_type=jnp.float32)


def rope_tables(positions, head_size):
    half_size = head_size // 2
    frequency = jnp.exp(
        jnp.arange(half_size, dtype=jnp.float32) * (-2.0 * math.log(10000.0) / head_size)
    )
    angles = positions.astype(jnp.float32)[:, None] * frequency[None, :]
    return (jnp.cos(angles)[:, None, :], jnp.sin(angles)[:, None, :])


def apply_rotary(vector, cosine_lookup, sine_lookup):
    half_size = vector.shape[-1] // 2
    first_half = vector[..., :half_size]
    second_half = vector[..., half_size:]
    return jnp.concatenate(
        [
            first_half * cosine_lookup - second_half * sine_lookup,
            second_half * cosine_lookup + first_half * sine_lookup,
        ],
        -1,
    )


def norm_forward(values, gain_vec):
    inverse = lax.rsqrt(jnp.mean(values * values, -1, keepdims=True) + EPSILON)
    normed = values * inverse
    return (normed, inverse, (normed * gain_vec.astype(jnp.float32)).astype(jnp.bfloat16))


def norm_backward(grad_rows, normed, inverse, gain_vec):
    scaled = grad_rows * gain_vec.astype(jnp.float32)
    grad_gain = jnp.sum(grad_rows * normed, 0)
    grad_values = inverse * (scaled - normed * jnp.mean(scaled * normed, -1, keepdims=True))
    return (grad_values, grad_gain)


def soft_scores(query_pair, key_pair, query_pos, key_pos):
    scores = jnp.einsum(
        "tjgd,sjd->jgts", query_pair, key_pair, preferred_element_type=jnp.float32
    ) * HEAD_WIDTH ** (-0.5)
    allowed = key_pos[None, :] <= query_pos[:, None]
    scores = jnp.where(allowed[None, None], scores, -1e30)
    top_score = jnp.max(scores, -1, keepdims=True)
    raised = jnp.exp(scores - top_score)
    return raised / jnp.sum(raised, -1, keepdims=True)


def split_pairs(rotated_query, keys_all, values_all):
    count_of_rows = rotated_query.shape[0]
    sequence_length = keys_all.shape[0]
    count_of_pairs = KEY_VALUE_HEADS // 2
    pairs_of_query = jnp.moveaxis(
        rotated_query.reshape(
            count_of_rows, count_of_pairs, 2, QUERY_HEADS // KEY_VALUE_HEADS, HEAD_WIDTH
        ),
        1,
        0,
    )
    key_pairs = jnp.moveaxis(keys_all.reshape(sequence_length, count_of_pairs, 2, HEAD_WIDTH), 1, 0)
    value_pairs = jnp.moveaxis(
        values_all.reshape(sequence_length, count_of_pairs, 2, HEAD_WIDTH), 1, 0
    )
    return (pairs_of_query, key_pairs, value_pairs)


def attend(rotated_query, keys_all, values_all, positions, key_pos):
    count_of_rows = rotated_query.shape[0]
    pairs_of_query, key_pairs, value_pairs = split_pairs(rotated_query, keys_all, values_all)

    def one_pair(operand):
        query_pair, key_pair, value_pair = operand
        shares = soft_scores(query_pair, key_pair, positions, key_pos)
        mixed_pair = jnp.einsum(
            "jgts,sjd->tjgd",
            shares.astype(jnp.bfloat16),
            value_pair,
            preferred_element_type=jnp.float32,
        )
        return mixed_pair.astype(jnp.bfloat16)

    mixed_heads = lax.map(one_pair, (pairs_of_query, key_pairs, value_pairs))
    return jnp.moveaxis(mixed_heads, 0, 1).reshape(count_of_rows, QUERY_HEADS * HEAD_WIDTH)


def attend_back(rotated_query, keys_all, values_all, mixed_gradient, positions, key_pos):
    count_of_rows = rotated_query.shape[0]
    sequence_length = keys_all.shape[0]
    pairs_of_query, key_pairs, value_pairs = split_pairs(rotated_query, keys_all, values_all)
    pair_gradients = jnp.moveaxis(
        mixed_gradient.reshape(
            count_of_rows, KEY_VALUE_HEADS // 2, 2, QUERY_HEADS // KEY_VALUE_HEADS, HEAD_WIDTH
        ),
        1,
        0,
    )

    def one_pair(operand):
        query_pair, key_pair, value_pair, grad_pair = operand
        shares = soft_scores(query_pair, key_pair, positions, key_pos)
        grad_shares = jnp.einsum(
            "tjgd,sjd->jgts", grad_pair, value_pair, preferred_element_type=jnp.float32
        )
        value_weight_gradient = jnp.einsum(
            "jgts,tjgd->sjd",
            shares.astype(jnp.bfloat16),
            grad_pair,
            preferred_element_type=jnp.float32,
        )
        centre = jnp.sum(shares * grad_shares, -1, keepdims=True)
        grad_scores = (shares * (grad_shares - centre)).astype(jnp.bfloat16)
        grad_query = jnp.einsum(
            "jgts,sjd->tjgd", grad_scores, key_pair, preferred_element_type=jnp.float32
        ) * HEAD_WIDTH ** (-0.5)
        key_weight_gradient = jnp.einsum(
            "jgts,tjgd->sjd", grad_scores, query_pair, preferred_element_type=jnp.float32
        ) * HEAD_WIDTH ** (-0.5)
        return (grad_query, key_weight_gradient, value_weight_gradient)

    grad_query, key_weight_gradient, value_weight_gradient = lax.map(
        one_pair, (pairs_of_query, key_pairs, value_pairs, pair_gradients)
    )
    grad_query = jnp.moveaxis(grad_query, 0, 1).reshape(count_of_rows, QUERY_HEADS * HEAD_WIDTH)
    key_weight_gradient = jnp.moveaxis(key_weight_gradient, 0, 1).reshape(
        sequence_length, KEY_VALUE_HEADS * HEAD_WIDTH
    )
    value_weight_gradient = jnp.moveaxis(value_weight_gradient, 0, 1).reshape(
        sequence_length, KEY_VALUE_HEADS * HEAD_WIDTH
    )
    return (grad_query, key_weight_gradient, value_weight_gradient)


def body(
    block_in,
    routes,
    cotangent,
    gain_attn,
    w_query,
    key_weight,
    value_weight,
    w_out,
    gain_ffn,
    w_router,
    w_gate,
    w_up,
    w_down,
):
    fetched = sent_together(
        (gain_attn, w_query, key_weight, value_weight, w_out, gain_ffn, w_router),
        ("seq", "ctx"),
        0,
        1,
    )
    expert_full = (
        *in_one_piece((w_gate, w_up), "seq", 1, 0),
        lax.all_gather(w_down, "seq", axis=1, tiled=True),
    )
    full_gain_attn, full_query, complete_key, full_value, full_out, full_gain_ffn, full_router = (
        fetched
    )
    gate_full, up_full, down_full = expert_full
    tokens = block_in[0].astype(jnp.float32)
    count_of_rows = tokens.shape[0]
    width = tokens.shape[1]
    ctx_count = lax.axis_size("ctx")
    local_experts = w_gate.shape[0]
    expert_count = local_experts * ctx_count
    capacity = 3 * count_of_rows * TOPK // (2 * expert_count)
    positions = lax.axis_index("ctx") * count_of_rows + jnp.arange(count_of_rows, dtype=jnp.int32)
    key_pos = jnp.arange(count_of_rows * ctx_count, dtype=jnp.int32)
    cosine_lookup, sine_lookup = rope_tables(positions, HEAD_WIDTH)
    normed_one, inverse_one, first_hidden = norm_forward(tokens, full_gain_attn)
    rotated_query = apply_rotary(
        elementwise_product(first_hidden, full_query).reshape(
            count_of_rows, QUERY_HEADS, HEAD_WIDTH
        ),
        cosine_lookup,
        sine_lookup,
    )
    rotated_query = rotated_query.astype(jnp.bfloat16).reshape(
        count_of_rows, QUERY_HEADS * HEAD_WIDTH
    )
    rotated_key = apply_rotary(
        elementwise_product(first_hidden, complete_key).reshape(
            count_of_rows, KEY_VALUE_HEADS, HEAD_WIDTH
        ),
        cosine_lookup,
        sine_lookup,
    )
    rotated_key = rotated_key.astype(jnp.bfloat16).reshape(
        count_of_rows, KEY_VALUE_HEADS * HEAD_WIDTH
    )
    value_low = elementwise_product(first_hidden, full_value).astype(jnp.bfloat16)
    keys_all, values_all = in_one_piece((rotated_key, value_low), "ctx", 0, 1)
    mixed_heads = attend(rotated_query, keys_all, values_all, positions, key_pos)
    middle = tokens + elementwise_product(mixed_heads, full_out)
    normed_two, inverse_two, hidden_two = norm_forward(middle, full_gain_ffn)
    logits = elementwise_product(hidden_two, full_router)
    route_rows = routes[0]
    expert_ids = jnp.arange(expert_count, dtype=jnp.int32)
    route_hot = (route_rows[:, :, None] == expert_ids[None, None, :]).astype(jnp.float32)
    picked = jnp.sum(route_hot * logits[:, None, :], -1)
    top_logit = jnp.max(picked, -1, keepdims=True)
    raised = jnp.exp(picked - top_logit)
    gate_share = raised / jnp.sum(raised, -1, keepdims=True)
    flat_routes = route_rows.reshape(-1)
    flat_hot = (flat_routes[:, None] == expert_ids[None, :]).astype(jnp.int32)
    slot_rank = jnp.sum((jnp.cumsum(flat_hot, 0) - flat_hot) * flat_hot, -1)
    slot_index = flat_routes * capacity + slot_rank
    copies = jnp.repeat(hidden_two, TOPK, axis=0)
    outgoing = jnp.zeros((expert_count * capacity, width), jnp.bfloat16).at[slot_index].set(copies)
    arrived = lax.all_to_all(outgoing, "ctx", split_axis=0, concat_axis=0, tiled=True).reshape(
        ctx_count, local_experts, capacity, width
    )
    gate_act = jnp.einsum("cxtd,xdf->cxtf", arrived, gate_full, preferred_element_type=jnp.float32)
    up_act = jnp.einsum("cxtd,xdf->cxtf", arrived, up_full, preferred_element_type=jnp.float32)
    inner_act = (jax.nn.silu(gate_act) * up_act).astype(jnp.bfloat16)
    result = jnp.einsum(
        "cxtf,xfd->cxtd", inner_act, down_full, preferred_element_type=jnp.float32
    ).astype(jnp.bfloat16)
    returned = lax.all_to_all(
        result.reshape(expert_count * capacity, width),
        "ctx",
        split_axis=0,
        concat_axis=0,
        tiled=True,
    )
    route_out = returned[slot_index].reshape(count_of_rows, TOPK, width).astype(jnp.float32)
    block_out = (middle + jnp.sum(gate_share[:, :, None] * route_out, 1)).astype(jnp.bfloat16)
    back_fetched = sent_together(
        (gain_attn, w_query, key_weight, value_weight, w_out, gain_ffn, w_router),
        ("seq", "ctx"),
        0,
        1,
    )
    back_experts = (
        *in_one_piece((w_gate, w_up), "seq", 1, 0),
        lax.all_gather(w_down, "seq", axis=1, tiled=True),
    )
    keys_back, values_back = in_one_piece((rotated_key, value_low), "ctx", 0, 1)
    back_gain_attn, back_query, back_key, back_value, back_out, back_gain_ffn, back_router = (
        back_fetched
    )
    back_gate, back_up, back_down = back_experts
    grad_rows = cotangent[0].astype(jnp.float32)
    grad_routed = (
        (gate_share[:, :, None] * grad_rows[:, None, :])
        .astype(jnp.bfloat16)
        .reshape(count_of_rows * TOPK, width)
    )
    grad_gates = jnp.sum(grad_rows[:, None, :] * route_out, -1)
    grad_outgoing = (
        jnp.zeros((expert_count * capacity, width), jnp.bfloat16).at[slot_index].set(grad_routed)
    )
    grad_arrived = lax.all_to_all(
        grad_outgoing, "ctx", split_axis=0, concat_axis=0, tiled=True
    ).reshape(ctx_count, local_experts, capacity, width)
    grad_inner = jnp.einsum(
        "cxtd,xfd->cxtf", grad_arrived, back_down, preferred_element_type=jnp.float32
    )
    grad_down_w = jnp.einsum(
        "cxtf,cxtd->xfd", inner_act, grad_arrived, preferred_element_type=jnp.float32
    )
    sigmoid_gate = jax.nn.sigmoid(gate_act)
    grad_gate_act = (
        grad_inner * up_act * (sigmoid_gate * (1.0 + gate_act * (1.0 - sigmoid_gate)))
    ).astype(jnp.bfloat16)
    grad_up_act = (grad_inner * (gate_act * sigmoid_gate)).astype(jnp.bfloat16)
    grad_gate_w = jnp.einsum(
        "cxtd,cxtf->xdf", arrived, grad_gate_act, preferred_element_type=jnp.float32
    )
    grad_up_w = jnp.einsum(
        "cxtd,cxtf->xdf", arrived, grad_up_act, preferred_element_type=jnp.float32
    )
    grad_arrival = jnp.einsum(
        "cxtf,xdf->cxtd", grad_gate_act, back_gate, preferred_element_type=jnp.float32
    )
    grad_arrival = grad_arrival + jnp.einsum(
        "cxtf,xdf->cxtd", grad_up_act, back_up, preferred_element_type=jnp.float32
    )
    grad_back = lax.all_to_all(
        grad_arrival.astype(jnp.bfloat16).reshape(expert_count * capacity, width),
        "ctx",
        split_axis=0,
        concat_axis=0,
        tiled=True,
    )
    grad_hidden_two = jnp.sum(
        grad_back[slot_index].reshape(count_of_rows, TOPK, width).astype(jnp.float32), 1
    )
    grad_picked = gate_share * (grad_gates - jnp.sum(gate_share * grad_gates, -1, keepdims=True))
    grad_logits = jnp.sum(grad_picked[:, :, None] * route_hot, 1)
    grad_router_w = jnp.dot(
        hidden_two.astype(jnp.float32).T,
        grad_logits,
        precision=HIGHEST,
        preferred_element_type=jnp.float32,
    )
    grad_hidden_two = grad_hidden_two + jnp.dot(
        grad_logits,
        back_router.astype(jnp.float32).T,
        precision=HIGHEST,
        preferred_element_type=jnp.float32,
    )
    grad_middle, grad_gain_two = norm_backward(
        grad_hidden_two, normed_two, inverse_two, back_gain_ffn
    )
    grad_middle = grad_middle + grad_rows
    grad_middle_low = grad_middle.astype(jnp.bfloat16)
    grad_out_w = elementwise_product(mixed_heads.T, grad_middle_low)
    mixed_gradient = elementwise_product(grad_middle_low, back_out.T).astype(jnp.bfloat16)
    grad_query_rot, grad_key_all, grad_value_all = attend_back(
        rotated_query, keys_back, values_back, mixed_gradient, positions, key_pos
    )
    rotated_key_gradient, grad_value_rows = tuple(
        (
            part.astype(jnp.float32)
            for part in in_one_piece_2(
                (grad_key_all.astype(jnp.bfloat16), grad_value_all.astype(jnp.bfloat16)),
                "ctx",
                0,
                1,
            )
        )
    )
    grad_query_low = (
        apply_rotary(
            grad_query_rot.reshape(count_of_rows, QUERY_HEADS, HEAD_WIDTH),
            cosine_lookup,
            -sine_lookup,
        )
        .astype(jnp.bfloat16)
        .reshape(count_of_rows, QUERY_HEADS * HEAD_WIDTH)
    )
    grad_key_low = (
        apply_rotary(
            rotated_key_gradient.reshape(count_of_rows, KEY_VALUE_HEADS, HEAD_WIDTH),
            cosine_lookup,
            -sine_lookup,
        )
        .astype(jnp.bfloat16)
        .reshape(count_of_rows, KEY_VALUE_HEADS * HEAD_WIDTH)
    )
    grad_value_low = grad_value_rows.astype(jnp.bfloat16)
    grad_query_w = elementwise_product(first_hidden.T, grad_query_low)
    grad_key_w = elementwise_product(first_hidden.T, grad_key_low)
    grad_value_w = elementwise_product(first_hidden.T, grad_value_low)
    grad_hidden_one = (
        elementwise_product(grad_query_low, back_query.T)
        + elementwise_product(grad_key_low, back_key.T)
        + elementwise_product(grad_value_low, back_value.T)
    )
    grad_tokens, grad_gain_one = norm_backward(
        grad_hidden_one, normed_one, inverse_one, back_gain_attn
    )
    grad_tokens = grad_tokens + grad_middle
    owned = one_scatter(
        (
            grad_gain_one,
            grad_query_w,
            grad_key_w,
            grad_value_w,
            grad_out_w,
            grad_gain_two,
            grad_router_w,
        ),
        ("seq", "ctx"),
        (0, 0, 0, 0, 0, 0, 0),
    )
    expert_owned = (
        *tuple(
            (
                part.astype(jnp.float32)
                for part in in_one_piece_2(
                    (grad_gate_w.astype(jnp.bfloat16), grad_up_w.astype(jnp.bfloat16)), "seq", 1, 0
                )
            )
        ),
        lax.psum_scatter(
            grad_down_w.astype(jnp.bfloat16), "seq", scatter_dimension=1, tiled=True
        ).astype(jnp.float32),
    )
    return (
        block_out[None],
        grad_tokens[None],
        owned[0],
        owned[1],
        owned[2],
        owned[3],
        owned[4],
        owned[5],
        owned[6],
        expert_owned[0],
        expert_owned[1],
        expert_owned[2],
    )


def solution(mesh):
    placed = (
        P("seq", "ctx", None),
        P("seq", "ctx", None),
        P("seq", "ctx", None),
        P(("seq", "ctx")),
        P(("seq", "ctx"), None),
        P(("seq", "ctx"), None),
        P(("seq", "ctx"), None),
        P(("seq", "ctx"), None),
        P(("seq", "ctx")),
        P(("seq", "ctx"), None),
        P("ctx", "seq", None),
        P("ctx", "seq", None),
        P("ctx", "seq", None),
    )
    return jax.shard_map(
        body,
        mesh=mesh,
        in_specs=placed,
        out_specs=(
            P("seq", "ctx", None),
            P("seq", "ctx", None),
            P(("seq", "ctx")),
            P(("seq", "ctx"), None),
            P(("seq", "ctx"), None),
            P(("seq", "ctx"), None),
            P(("seq", "ctx"), None),
            P(("seq", "ctx")),
            P(("seq", "ctx"), None),
            P("ctx", "seq", None),
            P("ctx", "seq", None),
            P("ctx", "seq", None),
        ),
        check_vma=False,
    )
```

profile of v0, /device:TPU:1, one launch (start us, length us, event | category | flops | bytes accessed | tf_op | source)
XLA Modules:
  0.0 1723.3 jit_solution(8401089198220815974)
XLA Ops:
  12.9 215.9 %all-gather.12.cloned.1.call-done = bf16[128,12,4130]{2,1,0:T(8,128)(2,1)} async-done(((bf16[1,12,4130]{2,1,0:T(8,128)(2,1)}), bf16[128,12,4130]{2,1,0:T(8,128)(2,1)}) %all-gather.12.cloned.1.call-update) | async-done | bytes 12687376 | tf_op jit(solution)/shard_map/all_gather | solution.py:21
  228.8 20.0 %reshape.605 = bf16[1536,4130]{1,0:T(8,128)(2,1)} reshape(bf16[128,12,4130]{2,1,0:T(8,128)(2,1)} %all-gather.12.cloned.1.call-done) | data formatting | bytes 25374720
  260.1 9.0 reduce-window.6
  270.3 7.4 slice_bitcast_fusion
  277.6 6.7 copy.133
  288.3 24.4 %all-gather.6.cloned.1.call-done = bf16[2048,1024]{1,0:T(8,128)(2,1)} async-done(((bf16[128,1024]{1,0:T(8,128)(2,1)}), bf16[2048,1024]{1,0:T(8,128)(2,1)}) %all-gather.6.cloned.1.call-update) | async-done | bytes 4194320 | tf_op jit(solution)/shard_map/all_gather | solution.py:35
  322.1 34.3 %while.26 = (s32[]{:T(128)}, bf16[4,128,2,3,64]{1,4,3,2,0:T(8,128)(2,1)S(1)}, bf16[4,2048,2,64]{1,3,2,0:T(8,128)(2,1)}, bf16[4,2048,2,64]{1,3,2,0:T(8,128)(2,1)S...) while((s32[]{:T(128)}, bf16[4,128,2,3,64]{1,4,3,2,0:T(8,128)(2,1)S(1)}, ...), condition=%wide.region_4.5_spmd.clone, body=%wide.region_1.4_spmd.clone.sunk | while | flops 412403840 | bytes 14362713 | solution.py:152
  330.8 4.7 fusion.275
  339.4 4.7 fusion.275
  356.4 5.4 multiply_reduce_fusion.2
  362.8 8.7 scatter_custom_fusion
  379.0 8.7 scatter_custom_fusion.1
  387.7 78.2 %all-to-all-done = bf16[16,96,1536]{2,1,0:T(8,128)(2,1)} async-done(((bf16[16,96,1536]{2,1,0:T(8,128)(2,1)}), bf16[16,96,1536]{2,1,0:T(8,128)(2,1)}, u32[]{:S(2)}, u32[]{:S(2)}) %all-to-all-start) | async-done | bytes 4718624 | tf_op jit(solution)/shard_map/all_to_all | solution.py:282
  465.9 5.2 all-to-all-start.2
  471.2 7.7 fusion.124
  478.9 6.6 fusion.122
  485.5 42.3 %all-to-all-done.2 = bf16[16,96,1536]{2,1,0:T(8,128)(2,1)} async-done(((bf16[16,96,1536]{2,1,0:T(8,128)(2,1)}), bf16[16,96,1536]{2,1,0:T(8,128)(2,1)}, u32[]{:S(2)}, u32[]{:S(2)}) %all-to-all-start.2) | async-done | bytes 4718624 | tf_op jit(solution)/shard_map/all_to_all | solution.py:325
  527.8 10.0 fusion.131
  537.8 5.7 fusion.150
  543.5 4.9 fusion.126
  550.8 5.3 all-to-all-start.3
  556.2 4.7 convert_bitcast_fusion
  563.3 49.6 %all-to-all-done.3 = bf16[16,96,1536]{2,1,0:T(8,128)(2,1)} async-done(((bf16[16,96,1536]{2,1,0:T(8,128)(2,1)}), bf16[16,96,1536]{2,1,0:T(8,128)(2,1)}, u32[]{:S(2)}, u32[]{:S(2)}) %all-to-all-start.3) | async-done | bytes 4718624 | tf_op jit(solution)/shard_map/all_to_all | solution.py:351
  613.0 5.7 all-to-all-start.1
  619.3 9.7 gather_fusion.1
  632.0 43.5 %all-to-all-done.1 = bf16[16,96,1536]{2,1,0:T(8,128)(2,1)} async-done(((bf16[16,96,1536]{2,1,0:T(8,128)(2,1)}), bf16[16,96,1536]{2,1,0:T(8,128)(2,1)}, u32[]{:S(2)}, u32[]{:S(2)}) %all-to-all-start.1) | async-done | bytes 4718624 | tf_op jit(solution)/shard_map/all_to_all | solution.py:291
  675.5 9.7 gather_fusion
  698.4 5.5 fusion.147
  705.8 66.0 %while.27 = (s32[]{:T(128)}, f32[4,128,2,3,64]{1,4,3,2,0:T(8,128)S(1)}, bf16[4,2048,2,64]{1,3,2,0:T(8,128)(2,1)}, bf16[4,2048,2,64]{1,3,2,0:T(8,128)(2,1)}, bf16...) while((s32[]{:T(128)}, ...), condition=%wide.region_24.25_spmd.clone, body=%wide.region_20.24_spmd.clone.sunk | while | flops 1027655040 | bytes 93938880 | solution.py:190
  771.8 4.8 pad_maximum_fusion.1
  776.6 6.4 copy.168
  783.0 7.4 bitcast_convert_fusion
  790.5 6.7 bitcast_convert_fusion.1
  797.2 6.5 bitcast_convert_fusion.2
  808.0 5.1 fusion.186
  813.1 11.9 reshape_reshape.21
  825.1 4.9 fusion.191
  830.0 11.7 reshape_reshape.24
  843.9 4.9 fusion.117
  848.8 11.0 reduce-scatter.14.cloned.1.call-done
  876.5 4.9 reshape_reshape.23
  883.1 33.9 %dynamic-update-slice.1 = f32[128,49560]{1,0:T(8,128)} dynamic-update-slice(f32[128,49560]{1,0:T(8,128)} %dynamic-update-slice, f32[128,18432]{1,0:T(8,128)} %reshape_reshape.21, s32[]{} %constant.108, s32[]{} %constant.109) | dynamic-update-slice | bytes 18874372
  917.0 12.6 dynamic-update-slice.2
  929.5 13.7 dynamic-update-slice.3
  943.2 33.0 %dynamic-update-slice.4 = f32[128,49560]{1,0:T(8,128)} dynamic-update-slice(f32[128,49560]{1,0:T(8,128)} %dynamic-update-slice.3, f32[128,18432]{1,0:T(8,128)} %reshape_reshape.24, s32[]{} %constant.108, s32[]{} %constant.112) | dynamic-update-slice | bytes 18874372
  979.9 17.2 pad.4
  997.2 23.5 %reshape.557 = f32[50176,128]{1,0:T(8,128)} reshape(f32[128,50176]{1,0:T(8,128)} %pad.4) | data formatting | bytes 51380224 | tf_op jit(solution)/shard_map/reshape | solution.py:60
  1026.4 682.7 %reduce-scatter.16.cloned.1.call-done = f32[392,128]{1,0:T(8,128)} async-done(((f32[50176,128]{1,0:T(8,128)}), f32[392,128]{1,0:T(8,128)}) %reduce-scatter.16.cloned.1.call-update) | async-done | bytes 200720
  (281 shorter events, 194.9 us)
Async XLA Ops:
  7.2 221.6 %all-gather.12.cloned.1.call-start = ((), (), s32[]{:S(2)}) async-start(), calls=%async_computation.13 | async-start | bytes 17436672 | tf_op jit(solution)/shard_map/all_gather | solution.py:21
  10.4 302.3 %all-gather.6.cloned.1.call-start = ((), (), s32[]{:S(2)}) async-start(), calls=%async_computation.8 | async-start | bytes 4456448 | tf_op jit(solution)/shard_map/all_gather | solution.py:35
  248.8 4.7 copy-start.1
  250.4 33.9 %copy-start.24 = (f32[1536]{0:T(1024)}, f32[1536]{0:T(1024)S(1)}, u32[]{:S(2)}) copy-start(f32[1536]{0:T(1024)S(1)} %get-tuple-element.146) | copy-start | bytes 18436
  253.5 5.1 copy-start.28
  253.5 5.1 copy-start.29
  253.5 6.1 copy-start.36
  258.1 213.1 %all-gather.8.cloned.1.call-start = ((), (), s32[]{:S(2)}) async-start(), calls=%async_computation.9 | async-start | bytes 7077888 | tf_op jit(solution)/shard_map/all_gather | solution.py:35
  277.6 6.7 copy-start.39
  356.4 5.4 copy-start.21
  356.4 15.1 copy-start.3
  361.8 9.7 copy-start.44
  362.8 14.0 copy-start.10
  371.5 5.2 copy-start.16
  371.5 7.1 copy-start.37
  371.5 7.5 copy-start.41
  371.5 94.4 %all-to-all-start = ((bf16[16,96,1536]{2,1,0:T(8,128)(2,1)}), bf16[16,96,1536]{2,1,0:T(8,128)(2,1)}, u32[]{:S(2)}, u32[]{:S(2)}) async-start(bf16[16,96,1536]{2,1,0:T(8,128)(2,1)} %bitcast.417), calls=%async_computation | async-start | bytes 9437184 | tf_op jit(solution)/shard_map/all_to_all | solution.py:282
  376.1 109.4 %all-gather.10.cloned.1.call-start = ((), (), s32[]{:S(2)}) async-start(), calls=%async_computation.10 | async-start | bytes 3538944 | tf_op jit(solution)/shard_map/all_gather | solution.py:226
  376.8 89.1 %copy-start.5 = (f32[128,1536]{1,0:T(8,128)}, f32[128,1536]{1,0:T(8,128)S(1)}, u32[]{:S(2)}) copy-start(f32[128,1536]{1,0:T(8,128)S(1)} %bitcast_convert_fusion.3) | copy-start | bytes 2359300
  378.7 87.2 %copy-start.42 = (f32[128]{0:T(128)}, f32[128]{0:T(128)S(1)}, u32[]{:S(2)}) copy-start(f32[128]{0:T(128)S(1)} %reduce_max.27) | copy-start | bytes 1540
  378.7 87.2 %copy-start.43 = (f32[128]{0:T(128)}, f32[128]{0:T(128)S(1)}, u32[]{:S(2)}) copy-start(f32[128]{0:T(128)S(1)} %fusion.205) | copy-start | bytes 1540
  378.9 87.0 %copy-start.23 = (f32[128,8]{1,0:T(8,128)}, f32[128,8]{1,0:T(8,128)S(1)}, u32[]{:S(2)}) copy-start(f32[128,8]{1,0:T(8,128)S(1)} %copy.134) | copy-start | bytes 12292
  465.9 61.9 %all-to-all-start.2 = ((bf16[16,96,1536]{2,1,0:T(8,128)(2,1)}), bf16[16,96,1536]{2,1,0:T(8,128)(2,1)}, u32[]{:S(2)}, u32[]{:S(2)}) async-start(bf16[16,96,1536]{2,1,0:T(8,128)(2,1)} %bitcast.419), calls=%async_computation.2 | async-start | bytes 9437184 | tf_op jit(solution)/shard_map/all_to_all | solution.py:325
  471.2 7.7 copy-start.17
  537.8 5.7 copy-start.45
  537.8 5.7 copy-start.12
  550.8 5.3 copy-start.47
  550.8 62.1 %all-to-all-start.3 = ((bf16[16,96,1536]{2,1,0:T(8,128)(2,1)}), bf16[16,96,1536]{2,1,0:T(8,128)(2,1)}, u32[]{:S(2)}, u32[]{:S(2)}) async-start(bf16[16,96,1536]{2,1,0:T(8,128)(2,1)} %bitcast.420), calls=%async_computation.3 | async-start | bytes 9437184 | tf_op jit(solution)/shard_map/all_to_all | solution.py:351
  613.0 62.5 %all-to-all-start.1 = ((bf16[16,96,1536]{2,1,0:T(8,128)(2,1)}), bf16[16,96,1536]{2,1,0:T(8,128)(2,1)}, u32[]{:S(2)}, u32[]{:S(2)}) async-start(bf16[16,96,1536]{2,1,0:T(8,128)(2,1)} %bitcast.418), calls=%async_computation.1 | async-start | bytes 9437184 | tf_op jit(solution)/shard_map/all_to_all | solution.py:291
  618.7 241.1 %reduce-scatter.14.cloned.1.call-start = ((), (), s32[]{:S(2)}) async-start(), calls=%async_computation.14 | async-start | bytes 4456448
  697.5 8.3 copy-start.4
  697.5 8.3 copy-start.18
  710.9 4.8 copy-start
  727.3 4.8 copy-start
  743.8 4.8 copy-start
  760.2 4.8 copy-start
  783.0 7.5 copy-start.13
  783.0 237.7 %reduce-scatter.12.cloned.1.call-start = ((), (), s32[]{:S(2)}) async-start(), calls=%async_computation.12 | async-start | bytes 3538944 | tf_op jit(solution)/shard_map/reduce_scatter | solution.py:449
  790.4 233.5 %reduce-scatter.10.cloned.1.call-start = ((), (), s32[]{:S(2)}) async-start(), calls=%async_computation.11 | async-start | bytes 7077888 | tf_op jit(solution)/shard_map/reduce_scatter | solution.py:45
  790.5 6.7 copy-start.46
  807.0 902.1 %reduce-scatter.16.cloned.1.call-start = ((), (), s32[]{:S(2)}) async-start(), calls=%async_computation.15 | async-start | bytes 25890816
  813.1 11.9 copy-start.8
  813.1 11.9 copy-start.22
  830.0 11.7 copy-start.38
  830.0 12.5 copy-start.11
  830.0 12.5 copy-start.33
  943.2 33.1 %copy-start.31 = (f32[128,12]{1,0:T(8,128)S(1)}, f32[128,12]{1,0:T(8,128)}, u32[]{:S(2)}) copy-start(f32[128,12]{1,0:T(8,128)} %reshape.556) | copy-start | bytes 18436
  943.2 34.8 %copy-start.20 = (f32[128,384]{1,0:T(8,128)S(1)}, f32[128,384]{1,0:T(8,128)}, u32[]{:S(2)}) copy-start(f32[128,384]{1,0:T(8,128)} %reshape_reshape.25) | copy-start | bytes 589828
  (21 other events, 40.4 us)
Sparse Core Ops, SparseCore 0:
  10.5 218.1 all-gather.11
  258.2 54.4 all-gather.5
  315.0 73.9 all-gather.7
  390.4 70.6 all-gather.9
  783.1 76.6 reduce-scatter.13
  862.2 42.6 reduce-scatter.11
  907.4 76.5 reduce-scatter.9
  1020.8 688.2 reduce-scatter.15
where the time goes:
time: 1740 us; the launch traced here: 1720 us
  waiting for transfers between devices  1150 us (66%)
  local copies, waits for them, and re-layouts  285 us (16%)
  matrix products  197 us (11%)
  other arithmetic  55.3 us (3%)
  starting transfers between devices  21.7 us (1%)
    unnamed x10, waiting for transfers between devices  694 us
    all_gather x1, waiting for transfers between devices, sent_together(): lax.all_gather(both, axis, axis=dim, tiled=True)  216 us
    unnamed x100, local copies, waits for them, and re-layouts  126 us
    all_to_all x1, waiting for transfers between devices, body(): lax.all_to_all(outgoing, 'ctx', split_axis=0, concat_axis=0, tiled=True)  78.2 us
    all_to_all x1, waiting for transfers between devices, body(): lax.all_to_all(grad_arrival.astype(jnp.bfloat16).reshape(expert_count * c...  49.6 us
    dot_general x13, matrix products, elementwise_product(): return jnp.dot(left_side, right_side, preferred_element_type=jnp.float32)  46.3 us
    all_to_all x1, waiting for transfers between devices, body(): lax.all_to_all(result.reshape(expert_count * capacity, width), 'ctx', spl...  43.5 us
    all_to_all x1, waiting for transfers between devices, body(): lax.all_to_all(grad_outgoing, 'ctx', split_axis=0, concat_axis=0, tiled=T...  42.3 us
  transfers between devices with their start and end apart: 12, of which 8 were waited for; matrix products, arithmetic and copies ran while one was open for 21% of the time, Pallas kernels for 0%

commit v1 on v0

v1 whole, which is shorter than its diff:
```python
import functools
import math

import jax
import jax.numpy as jnp
import numpy as np
from jax import lax
from jax.experimental import pallas as pl
from jax.experimental.pallas import tpu as pltpu
from jax.sharding import PartitionSpec as P

WIDTH = 1536
HEADS = 24
KV_HEADS = 8
HEAD = 64
TOPK = 8
ROWS = 128
LENGTH = 2048
EXPERTS = 32
FF = 512
CAP = 48
EPSILON = 1e-06

BF = jnp.bfloat16
F32 = jnp.float32
MESH = pl.DeviceIdType.MESH
VMEM_BYTES = 60 << 20

QUARTER = 1152
HALF = 2 * QUARTER
COL_K, COL_V, COL_O, COL_M, COL_END = 768, 1024, 1280, 2048, 2176
TALL = WIDTH + 128


def vm():
    return pl.BlockSpec(memory_space=pltpu.VMEM)


def hbm():
    return pl.BlockSpec(memory_space=pl.ANY)


def shape(dims, dtype=BF):
    return jax.ShapeDtypeStruct(dims, dtype)


def place():
    seq, ctx = lax.axis_index("seq"), lax.axis_index("ctx")
    return (ctx // 2 % 2 * 2 + seq // 4, ctx // 4, seq % 4, ctx % 2)


def device(x, y, z, core):
    return (x % 2 * 4 + z, (y * 2 + x // 2) * 2 + core)


def ring(at, dim, step):
    x, y, z, core = at
    if dim == 0:
        return ((x + step) % 4, y, z, core)
    if dim == 1:
        return (x, (y + step) % 4, z, core)
    return (x, y, (z + step) % 4, core)


def sibling(at):
    return (at[0], at[1], at[2], 1 - at[3])


def greet(peers):
    barrier = pltpu.get_barrier_semaphore()
    for peer in peers:
        pl.semaphore_signal(barrier, inc=1, device_id=device(*peer), device_id_type=MESH)
    pl.semaphore_wait(barrier, len(peers))


class Wires:
    def __init__(self, send, recv):
        self.send, self.recv, self.used, self.open = send, recv, 0, []

    def go(self, src, dst, peer):
        n = self.used
        self.used += 1
        copy = pltpu.make_async_remote_copy(
            src_ref=src,
            dst_ref=dst,
            send_sem=self.send.at[n],
            recv_sem=self.recv.at[n],
            device_id=device(*peer),
            device_id_type=MESH,
        )
        copy.start()
        self.open.append(copy)
        return copy

    def close(self):
        for copy in self.open:
            copy.wait_send()


def wire_sems(n):
    return [pltpu.SemaphoreType.DMA((n,)), pltpu.SemaphoreType.DMA((n,))]


def got(copies):
    for copy in copies:
        copy.wait_recv()


def dot(a, b):
    return jnp.dot(a, b, preferred_element_type=F32)


def dot_t(a, b):
    return lax.dot_general(a, b, (((1,), (1,)), ((), ())), preferred_element_type=F32)


def t_dot(a, b):
    return lax.dot_general(a, b, (((0,), (0,)), ((), ())), preferred_element_type=F32)


def iota(dims, axis):
    return lax.broadcasted_iota(jnp.int32, dims, axis)


def turn(block, cosine, sine):
    low = iota((block.shape[0], 128), 1) % HEAD < HEAD // 2
    parts = []
    for i in range(block.shape[1] // 128):
        unit = block[:, 128 * i : 128 * i + 128]
        other = jnp.where(low, pltpu.roll(unit, 96, 1), pltpu.roll(unit, 32, 1))
        parts.append(unit * cosine + other * sine)
    return jnp.concatenate(parts, 1)


def regroup():
    r, c = iota((48, 64), 0), iota((48, 64), 1)
    owner = c // 16 % 2 * 2 + c // 32
    hit = (r == owner * 12 + c % 16) & (c % 16 < 12)
    return hit.astype(F32).astype(BF)


def regroup_back():
    r, c = iota((64, 48), 0), iota((64, 48), 1)
    hit = (c == r // 16 * 12 + r % 16) & (r % 16 < 12)
    return hit.astype(F32).astype(BF)


ORDERS = ((0, 1, 2), (1, 2, 0), (2, 0, 1))


def block_of(ref, part, fixed, at):
    x, y, z, _ = at
    whole = slice(None)
    columns = (
        pl.ds(pl.multiple_of(x // 2 * QUARTER, 128), QUARTER) if 0 in fixed else pl.ds(0, HALF)
    )
    return (
        x % 2 if 0 in fixed else whole,
        z if 2 in fixed else whole,
        y if 1 in fixed else whole,
        part,
        whole,
        columns,
    )


def spread(ref, wires, at):
    waits = [[], [], []]
    for phase in range(3):
        for part in range(3):
            got(waits[part])
            waits[part] = []
            fixed = ORDERS[part][phase:]
            spot = ref.at[block_of(ref, part, fixed, at)]
            for step in (1, 2, 3):
                waits[part].append(wires.go(spot, spot, ring(at, fixed[0], step)))
    for part in range(3):
        got(waits[part])


def ctx_peers(at):
    return [ring(at, 1, 1), ring(at, 1, 2), ring(at, 1, 3), ring(at, 0, 2)]


def all_peers(at):
    return [ring(at, d, s) for d in range(3) for s in (1, 2, 3)]


def first_kernel(
    stage, x, cosine, sine,
    weights, wo, rows, router, q, kv, h1t,
    both, slots, cos_v, sin_v, ssem, rsem, lsem,
):
    at = place()
    xx, y, z, core = at
    xh, chip = xx // 2, y * 2 + xx // 2
    diagonal = sibling(ring(at, 0, 2))
    greet(all_peers(at) + [sibling(at), diagonal])
    wires = Wires(ssem, rsem)
    tables = [
        pltpu.make_async_copy(src.at[pl.ds(pl.multiple_of(chip * 256, 256), 256)], dst, lsem.at[i])
        for i, (src, dst) in enumerate(((cosine, cos_v), (sine, sin_v)))
    ]
    for copy in tables:
        copy.start()
    mine = core * 2 + xh
    first = [
        wires.go(stage.at[peer[3] * 2 + peer[0] // 2], slots.at[mine], peer)
        for peer in (sibling(at), ring(at, 0, 2), diagonal)
    ]
    tokens = wires.go(x, both.at[core], sibling(at))
    slots[mine] = stage[mine]
    both[core] = x[...]
    got(first)
    unit = dot(regroup(), slots[...].reshape(64, QUARTER)).astype(BF)
    lanes = pl.ds(pl.multiple_of(xh * QUARTER, 128), QUARTER)
    for part in range(3):
        weights[xx % 2, z, y, part, :, lanes] = unit[16 * part : 16 * part + 16]
    spread(weights, wires, at)

    out_columns = slice(COL_O, COL_M)
    swap = wires.go(
        weights.at[1 - core, :, :, :, :, out_columns],
        wo.at[:, :, :, :, pl.ds(pl.multiple_of(core * 768, 128), 768)],
        sibling(at),
    )
    for i in range(4):
        wo[i, :, :, :, pl.ds(pl.multiple_of(core * 768, 128), 768)] = weights[core, i, :, :, :, out_columns]
    small = weights[:, :, :, :, :, COL_M:COL_END].reshape(WIDTH, 128)
    router[...] = small
    turned = jnp.transpose(small.astype(F32))
    rows[...] = turned[32:40]
    got([tokens])
    values = both[...].reshape(256, WIDTH).astype(F32)
    inverse = lax.rsqrt(jnp.mean(values * values, -1, keepdims=True) + EPSILON)
    hidden = (values * inverse * turned[32:33]).astype(BF)
    made = dot(hidden, weights[:, :, :, :, :, 0:COL_O].reshape(WIDTH, COL_O))
    for copy in tables:
        copy.wait()
    cos, sin = cos_v[...], sin_v[...]
    key = turn(made[:, COL_K:COL_V], cos, sin).astype(BF)
    value = made[:, COL_V:COL_O].astype(BF)
    for part in range(2):
        kv[y, xh, part, :, 0:256] = key[128 * part : 128 * part + 128]
        kv[y, xh, part, :, 256:512] = value[128 * part : 128 * part + 128]
    own = [kv.at[y, xh, 0], kv.at[y, xh, 1]]
    a = [wires.go(own[0], own[0], ring(at, 1, s)) for s in (1, 2, 3)]
    b = [wires.go(own[1], own[1], ring(at, 0, 2))]
    q[...] = turn(made[:, 0:COL_K], cos, sin).astype(BF)
    got(a)
    column = kv.at[:, xh, 0]
    a = [wires.go(column, column, ring(at, 0, 2))]
    got(b)
    pair = kv.at[y, :, 1]
    b = [wires.go(pair, pair, ring(at, 1, s)) for s in (1, 2, 3)]
    h1t[...] = jnp.transpose(hidden.astype(F32)).astype(BF)
    got(a)
    got(b)
    got([swap])
    wires.close()


def first_call(stage, x, cosine, sine):
    return pl.pallas_call(
        first_kernel,
        out_shape=[
            shape((2, 4, 4, 3, 16, HALF)),
            shape((4, 4, 3, 16, WIDTH)),
            shape((8, WIDTH), F32),
            shape((WIDTH, 128)),
            shape((256, 768)),
            shape((4, 2, 2, 128, 512)),
            shape((WIDTH, 256)),
        ],
        in_specs=[vm(), vm(), hbm(), hbm()],
        out_specs=[vm()] * 7,
        scratch_shapes=[
            pltpu.VMEM((2, 128, WIDTH), BF),
            pltpu.VMEM((4, 16, QUARTER), BF),
            pltpu.VMEM((256, 128), F32),
            pltpu.VMEM((256, 128), F32),
            *wire_sems(48),
            pltpu.SemaphoreType.DMA((2,)),
        ],
        compiler_params=pltpu.CompilerParams(
            collective_id=1, has_side_effects=True, vmem_limit_bytes=VMEM_BYTES
        ),
        name="weights_qkv",
    )(stage, x, cosine, sine)


def attend_kernel(q, kv, o, ot, lse, scores, vt, qt, qz, out_t):
    at = place()
    chip = at[1] * 2 + at[0] // 2
    qt[...] = jnp.transpose(q[...].astype(F32) * 0.125).astype(BF)
    for kb in range(8):
        vt[kb] = jnp.transpose(kv[256 * kb : 256 * kb + 256, 256:512].astype(F32)).astype(BF)
    allowed = iota((256, 768), 0) <= iota((256, 768), 1) % 256
    for j in range(4):
        u, half = j // 2, j % 2
        qz[...] = jnp.zeros_like(qz)
        for g in range(3):
            h = 3 * j + g
            qz[64 * half : 64 * half + 64, 256 * g : 256 * g + 256] = qt[64 * h : 64 * h + 64]

        def score(kb):
            rows = pl.ds(pl.multiple_of(kb * 256, 256), 256)
            return rows, dot(kv[rows, 128 * u : 128 * u + 128], qz[...])

        def top(kb, most):
            rows, s = score(kb)
            scores[rows] = s
            return jnp.maximum(most, jnp.max(s.reshape(32, 8, 768), 0))

        most = lax.fori_loop(0, chip, top, jnp.full((8, 768), -1e30, F32))
        rows, s = score(chip)
        s = jnp.where(allowed, s, -1e30)
        scores[rows] = s
        most = jnp.maximum(most, jnp.max(s.reshape(32, 8, 768), 0))
        most = jnp.max(most, 0, keepdims=True)

        def raise_(kb, total):
            rows = pl.ds(pl.multiple_of(kb * 256, 256), 256)
            e = jnp.exp(scores[rows] - most)
            scores[rows] = e
            return total + jnp.sum(e.reshape(32, 8, 768), 0)

        total = lax.fori_loop(0, chip + 1, raise_, jnp.zeros((8, 768), F32))
        total = jnp.sum(total, 0, keepdims=True)
        lse[j] = jnp.broadcast_to(most + jnp.log(total), (8, 768))
        inverse = 1.0 / total

        def mix(kb, acc):
            rows = pl.ds(pl.multiple_of(kb * 256, 256), 256)
            p = (scores[rows] * inverse).astype(BF)
            return acc + dot(vt[kb, 64 * j : 64 * j + 64], p)

        acc = lax.fori_loop(0, chip + 1, mix, jnp.zeros((64, 768), F32))
        for g in range(3):
            h = 3 * j + g
            out_t[64 * h : 64 * h + 64] = acc[:, 256 * g : 256 * g + 256]
    ot[...] = out_t[...].astype(BF)
    o[...] = jnp.transpose(out_t[...]).astype(BF)


def attend_call(q, kv):
    return pl.pallas_call(
        attend_kernel,
        out_shape=[shape((256, 768)), shape((768, 256)), shape((4, 8, 768), F32)],
        in_specs=[vm(), vm()],
        out_specs=[vm()] * 3,
        scratch_shapes=[
            pltpu.VMEM((LENGTH, 768), F32),
            pltpu.VMEM((8, 256, 256), BF),
            pltpu.VMEM((768, 256), BF),
            pltpu.VMEM((128, 768), BF),
            pltpu.VMEM((768, 256), F32),
        ],
        compiler_params=pltpu.CompilerParams(vmem_limit_bytes=VMEM_BYTES),
        name="attend",
    )(q, kv)


def attend_back_kernel(
    q, kv, d_o, lse, cosine, sine,
    dq, dkv,
    probs, grads, kt, qt, dot_, qz, oz, acc, dqt, cos_v, sin_v, lsem,
):
    at = place()
    chip = at[1] * 2 + at[0] // 2
    tables = [
        pltpu.make_async_copy(src.at[pl.ds(pl.multiple_of(chip * 256, 256), 256)], dst, lsem.at[i])
        for i, (src, dst) in enumerate(((cosine, cos_v), (sine, sin_v)))
    ]
    for copy in tables:
        copy.start()
    qt[...] = jnp.transpose(q[...].astype(F32) * 0.125).astype(BF)
    dot_[...] = jnp.transpose(d_o[...].astype(F32)).astype(BF)
    for kb in range(8):
        kt[kb] = jnp.transpose(kv[256 * kb : 256 * kb + 256, 0:256].astype(F32)).astype(BF)
    acc[...] = jnp.zeros_like(acc)
    allowed = iota((256, 768), 0) <= iota((256, 768), 1) % 256
    for j in range(4):
        u, half = j // 2, j % 2
        qz[...] = jnp.zeros_like(qz)
        oz[...] = jnp.zeros_like(oz)
        for g in range(3):
            h = 3 * j + g
            qz[64 * half : 64 * half + 64, 256 * g : 256 * g + 256] = qt[64 * h : 64 * h + 64]
            oz[64 * half : 64 * half + 64, 256 * g : 256 * g + 256] = dot_[64 * h : 64 * h + 64]
        level = lse[j, 0:1]

        def share(kb, centre, masked):
            rows = pl.ds(pl.multiple_of(kb * 256, 256), 256)
            p = jnp.exp(dot(kv[rows, 128 * u : 128 * u + 128], qz[...]) - level)
            if masked:
                p = jnp.where(allowed, p, 0.0)
            probs[rows] = p
            dp = dot(kv[rows, 256 + 128 * u : 384 + 128 * u], oz[...])
            grads[rows] = dp
            acc[rows, 256 + 128 * u : 384 + 128 * u] += dot_t(p.astype(BF), oz[...])
            return centre + jnp.sum((p * dp).reshape(32, 8, 768), 0)

        centre = lax.fori_loop(
            0, chip, functools.partial(share, masked=False), jnp.zeros((8, 768), F32)
        )
        centre = share(chip, centre, True)
        centre = jnp.sum(centre, 0, keepdims=True)

        def back(kb, total):
            rows = pl.ds(pl.multiple_of(kb * 256, 256), 256)
            ds = (probs[rows] * (grads[rows] - centre)).astype(BF)
            acc[rows, 128 * u : 128 * u + 128] += dot_t(ds, qz[...])
            return total + dot(kt[kb, 64 * j : 64 * j + 64], ds)

        total = lax.fori_loop(0, chip + 1, back, jnp.zeros((64, 768), F32))
        for g in range(3):
            h = 3 * j + g
            dqt[64 * h : 64 * h + 64] = total[:, 256 * g : 256 * g + 256] * 0.125
    for kb in range(8):
        for part in range(2):
            at_row = 256 * kb + 128 * part
            dkv[part, kb] = acc[at_row : at_row + 128].astype(BF)
    for copy in tables:
        copy.wait()
    dq[...] = turn(jnp.transpose(dqt[...]), cos_v[...], -sin_v[...]).astype(BF)


def attend_back_call(q, kv, d_o, lse, cosine, sine):
    return pl.pallas_call(
        attend_back_kernel,
        out_shape=[shape((256, 768)), shape((2, 8, 128, 512))],
        in_specs=[vm()] * 4 + [hbm()] * 2,
        out_specs=[vm()] * 2,
        scratch_shapes=[
            pltpu.VMEM((LENGTH, 768), F32),
            pltpu.VMEM((LENGTH, 768), F32),
            pltpu.VMEM((8, 256, 256), BF),
            pltpu.VMEM((768, 256), BF),
            pltpu.VMEM((768, 256), BF),
            pltpu.VMEM((128, 768), BF),
            pltpu.VMEM((128, 768), BF),
            pltpu.VMEM((LENGTH, 512), F32),
            pltpu.VMEM((768, 256), F32),
            pltpu.VMEM((256, 128), F32),
            pltpu.VMEM((256, 128), F32),
            pltpu.SemaphoreType.DMA((2,)),
        ],
        compiler_params=pltpu.CompilerParams(vmem_limit_bytes=VMEM_BYTES),
        name="attend_back",
    )(q, kv, d_o, lse, cosine, sine)


def share_rows(ref, wires, at):
    x, y, _, core = at
    xh = x // 2
    near, far = sibling(at), ring(at, 0, 2)

    def pass_on(spot, peer):
        return wires.go(spot, spot, peer)

    inner = [pass_on(ref.at[y, xh, core], near)]
    a = [pass_on(ref.at[y, xh, core, 0], ring(at, 1, s)) for s in (1, 2, 3)]
    b = [pass_on(ref.at[y, xh, core, 1], far)]
    yield
    got(b)
    b = [pass_on(ref.at[y, :, core, 1], ring(at, 1, s)) for s in (1, 2, 3)]
    got(a)
    a = [pass_on(ref.at[:, xh, core, 0], far)]
    inner.append(pass_on(ref.at[y, 1 - xh, core, 1], near))
    for s in (1, 2, 3):
        inner.append(pass_on(ref.at[(y + s) % 4, xh, core, 0], near))
    yield
    got(a)
    inner.append(pass_on(ref.at[:, 1 - xh, core, 0], near))
    got(b)
    for s in (1, 2, 3):
        inner.append(pass_on(ref.at[(y + s) % 4, :, core, 1], near))
    yield
    got(inner)


def ctx_and_sibling(at):
    return ctx_peers(at) + [sibling(at)]


def share_kernel(rows, all_rows, ssem, rsem, lsem):
    at = place()
    x, y, _, core = at
    greet(ctx_and_sibling(at))
    wires = Wires(ssem, rsem)
    own = pltpu.make_async_copy(rows, all_rows.at[y, x // 2, core], lsem)
    own.start()
    own.wait()
    for _ in share_rows(all_rows, wires, at):
        pass
    wires.close()


def share_call(rows):
    return pl.pallas_call(
        share_kernel,
        out_shape=shape((4, 2, 2, 2, 64, WIDTH)),
        in_specs=[hbm()],
        out_specs=hbm(),
        scratch_shapes=[*wire_sems(24), pltpu.SemaphoreType.DMA],
        compiler_params=pltpu.CompilerParams(collective_id=2, has_side_effects=True),
        name="share_cotangent",
    )(rows)


def normed(values):
    inverse = lax.rsqrt(jnp.mean(values * values, -1, keepdims=True) + EPSILON)
    return values * inverse, inverse


def middle_kernel(
    o, wo, x, routes, rows, router,
    middle, gates, tall,
    product, arrived, ssem, rsem,
):
    at = place()
    xx, y, _, core = at
    near = sibling(at)
    greet(ctx_and_sibling(at))
    wires = Wires(ssem, rsem)
    full = wo[...].reshape(768, WIDTH)
    product[0] = dot(o[1 - core], full)
    swap = wires.go(product.at[0], arrived, near)
    product[1] = dot(o[core], full)
    lane = iota((ROWS, 128), 1)
    named = routes[:, 0:1] == lane
    for i in range(1, TOPK):
        named = named | (routes[:, i : i + 1] == lane)
    got([swap])
    mid = x[...].astype(F32) + product[1] + arrived[...]
    middle[...] = mid
    hidden = (normed(mid)[0] * rows[1:2]).astype(BF)
    logits = jnp.where(named, dot(hidden, router[...]), -jnp.inf)
    raised = jnp.exp(logits - jnp.max(logits, -1, keepdims=True))
    gate = raised / jnp.sum(raised, -1, keepdims=True)
    gates[...] = gate
    high = gate.astype(BF).astype(F32)
    both = high + pltpu.roll(gate - high, EXPERTS, 1)
    for part in range(2):
        cut = slice(64 * part, 64 * part + 64)
        tall[y, xx // 2, core, part, :, 0:WIDTH] = hidden[cut]
        tall[y, xx // 2, core, part, :, WIDTH:TALL] = both[cut].astype(BF)
    for _ in share_rows(tall, wires, at):
        pass
    wires.close()


def middle_call(o, wo, x, routes, rows, router):
    return pl.pallas_call(
        middle_kernel,
        out_shape=[
            shape((ROWS, WIDTH), F32),
            shape((ROWS, 128), F32),
            shape((4, 2, 2, 2, 64, TALL)),
        ],
        in_specs=[vm()] * 6,
        out_specs=[vm()] * 3,
        scratch_shapes=[
            pltpu.VMEM((2, ROWS, WIDTH), F32),
            pltpu.VMEM((ROWS, WIDTH), F32),
            *wire_sems(24),
        ],
        compiler_params=pltpu.CompilerParams(
            collective_id=3, has_side_effects=True, vmem_limit_bytes=VMEM_BYTES
        ),
        name="middle",
    )(o.reshape(2, ROWS, 768), wo, x, routes, rows, router)


def expert_kernel(
    tall, dy, w_gate, w_up, w_down,
    out_rows, d_rows, g_gate, g_up, g_down,
    big, wide, a_rows, y_rows, r_rows, back, wg, wu, wd, gg, gu, gd, m_s, dg_s, du_s, slot_t, sem,
):
    ctx = lax.axis_index("ctx")
    loads = [
        pltpu.make_async_copy(src, dst, sem.at[i])
        for i, (src, dst) in enumerate(
            ((tall, big), (dy, wide), (w_gate, wg), (w_up, wu), (w_down, wd))
        )
    ]
    for copy in loads:
        copy.start()
    lane = iota((128, 128), 1)
    earlier = (iota((128, 128), 1) < iota((128, 128), 0)).astype(F32).astype(BF)
    slots = iota((CAP, 128), 0).astype(F32)
    loads[0].wait()
    loads[1].wait()

    def collect(b, _):
        rows = pl.ds(pl.multiple_of(b * 128, 128), 128)
        packed = pl.ds(pl.multiple_of(b * CAP, CAP), CAP)
        both = big[rows, WIDTH:TALL].astype(F32)
        gate = both + pltpu.roll(both, 128 - EXPERTS, 1)
        hot = (gate > 0.0) & (lane < EXPERTS)
        rank = dot(earlier, hot.astype(F32).astype(BF))
        slot = jnp.where(hot, rank, -1.0)
        slot_t[...] = jnp.transpose(slot)
        picks = [
            (slot_t[pl.ds(2 * ctx + i, 1), :] == slots).astype(F32).astype(BF) for i in range(2)
        ]
        pick = jnp.concatenate(picks, 0)
        found = dot(pick, big[rows, :]).astype(BF)
        grads = dot(pick, wide[rows, :]).astype(BF)
        for i in range(2):
            a_rows[i, packed] = found[CAP * i : CAP * i + CAP]
            y_rows[i, packed] = grads[CAP * i : CAP * i + CAP]
        column = [
            jnp.sum(jnp.where(lane == 2 * ctx + i, slot, 0.0), 1, keepdims=True) for i in range(2)
        ]
        spot = lane.astype(F32)
        put = jnp.where(lane < CAP, column[0], column[1] + CAP) == spot
        back[b] = put.astype(F32).astype(BF)
        return 0

    lax.fori_loop(0, 16, collect, 0)
    for copy in loads[2:]:
        copy.wait()
    stores = []
    for e in range(2):
        number = 2 * ctx + e

        def forward(c, _):
            rows = pl.ds(pl.multiple_of(c * 384, 384), 384)
            a = a_rows[e, rows, 0:WIDTH]
            ag, au = dot(a, wg[e]), dot(a, wu[e])
            sg = jax.nn.sigmoid(ag)
            act = ag * sg
            m = (act * au).astype(BF)
            r = dot(m, wd[e]).astype(BF).astype(F32)
            lanes = iota((384, 128), 1)
            hits = (lanes == number) | (lanes == number + EXPERTS)
            gate = jnp.sum(
                jnp.where(hits, a_rows[e, rows, WIDTH:TALL].astype(F32), 0.0), 1, keepdims=True
            )
            y = y_rows[e, rows].astype(F32)
            d_gate = jnp.sum(y * r, 1, keepdims=True)
            r_rows[e, rows] = (gate * r).astype(BF)
            gr = (gate * y).astype(BF)
            y_rows[e, rows] = gr
            dm = dot_t(gr, wd[e])
            m_s[rows] = m
            dg_s[rows] = (dm * au * (sg * (1.0 + ag * (1.0 - sg)))).astype(BF)
            du_s[rows] = (dm * act).astype(BF)
            high = d_gate.astype(BF).astype(F32)
            d_both = jnp.where(
                lanes == number, high, jnp.where(lanes == number + EXPERTS, d_gate - high, 0.0)
            )
            a_rows[e, rows, WIDTH:TALL] = d_both.astype(BF)
            return 0

        lax.fori_loop(0, 2, forward, 0)
        gd[e] = t_dot(m_s[...], y_rows[e]).astype(BF)
        gg[e] = t_dot(a_rows[e, :, 0:WIDTH], dg_s[...]).astype(BF)
        gu[e] = t_dot(a_rows[e, :, 0:WIDTH], du_s[...]).astype(BF)
        for i, (src, dst) in enumerate(((gd, g_down), (gg, g_gate), (gu, g_up))):
            copy = pltpu.make_async_copy(src.at[e], dst.at[e], sem.at[5 + 3 * e + i])
            copy.start()
            stores.append(copy)

        def to_tokens(c, _):
            rows = pl.ds(pl.multiple_of(c * 384, 384), 384)
            back_rows = dot_t(dg_s[rows], wg[e]) + dot_t(du_s[rows], wu[e])
            a_rows[e, rows, 0:WIDTH] = back_rows.astype(BF)
            return 0

        lax.fori_loop(0, 2, to_tokens, 0)

    def hand_back(b, _):
        rows = pl.ds(pl.multiple_of(b * 128, 128), 128)
        packed = pl.ds(pl.multiple_of(b * CAP, CAP), CAP)
        put = back[b][:, 0 : 2 * CAP]
        big[rows, :] = dot(put, jnp.concatenate([a_rows[0, packed], a_rows[1, packed]], 0)).astype(BF)
        wide[rows, :] = dot(put, jnp.concatenate([r_rows[0, packed], r_rows[1, packed]], 0)).astype(BF)
        return 0

    lax.fori_loop(0, 16, hand_back, 0)
    for i, (src, dst) in enumerate(((big, d_rows), (wide, out_rows))):
        copy = pltpu.make_async_copy(src, dst, sem.at[i])
        copy.start()
        stores.append(copy)
    for copy in stores:
        copy.wait()


def expert_call(tall, dy, w_gate, w_up, w_down):
    slots = 16 * CAP
    return pl.pallas_call(
        expert_kernel,
        out_shape=[
            shape((LENGTH, WIDTH)),
            shape((LENGTH, TALL)),
            shape((2, WIDTH, FF)),
            shape((2, WIDTH, FF)),
            shape((2, FF, WIDTH)),
        ],
        in_specs=[hbm()] * 5,
        out_specs=[hbm()] * 5,
        scratch_shapes=[
            pltpu.VMEM((LENGTH, TALL), BF),
            pltpu.VMEM((LENGTH, WIDTH), BF),
            pltpu.VMEM((2, slots, TALL), BF),
            pltpu.VMEM((2, slots, WIDTH), BF),
            pltpu.VMEM((2, slots, WIDTH), BF),
            pltpu.VMEM((16, 128, 128), BF),
            pltpu.VMEM((2, WIDTH, FF), BF),
            pltpu.VMEM((2, WIDTH, FF), BF),
            pltpu.VMEM((2, FF, WIDTH), BF),
            pltpu.VMEM((2, WIDTH, FF), BF),
            pltpu.VMEM((2, WIDTH, FF), BF),
            pltpu.VMEM((2, FF, WIDTH), BF),
            pltpu.VMEM((slots, FF), BF),
            pltpu.VMEM((slots, FF), BF),
            pltpu.VMEM((slots, FF), BF),
            pltpu.VMEM((128, 128), F32),
            pltpu.SemaphoreType.DMA((11,)),
        ],
        compiler_params=pltpu.CompilerParams(vmem_limit_bytes=VMEM_BYTES),
        name="experts",
    )(tall.reshape(LENGTH, TALL), dy.reshape(LENGTH, WIDTH), w_gate, w_up, w_down)


def sum_scratch(rows, columns):
    return [
        pltpu.VMEM((4, rows, columns), BF),
        pltpu.VMEM((3, 2, rows, columns), BF),
        pltpu.VMEM((4, rows, columns), BF),
        pltpu.VMEM((2, rows, columns), BF),
        pltpu.VMEM((3, rows, columns), BF),
        pltpu.VMEM((1, rows, columns), BF),
    ]


def sum_chips(source, scratch, wires, at):
    e0, e1, t0, t1, f0, f1 = scratch
    x, y, _, _ = at
    xh = x // 2
    far = ring(at, 0, 2)
    a = [wires.go(source.at[0, :, 1 - xh], e0, far)]
    b = [
        wires.go(source.at[1, (y + s) % 4], e1.at[s - 1], ring(at, 1, s)) for s in (1, 2, 3)
    ]
    yield None
    got(a)
    for i in range(4):
        t0[i] = (source[0, i, xh].astype(F32) + e0[i].astype(F32)).astype(BF)
    a = [wires.go(t0.at[(y + s) % 4], f0.at[s - 1], ring(at, 1, s)) for s in (1, 2, 3)]
    got(b)
    for i in range(2):
        total = source[1, y, i].astype(F32)
        for s in range(3):
            total += e1[s, i].astype(F32)
        t1[i] = total.astype(BF)
    b = [wires.go(t1.at[1 - xh], f1.at[0], far)]
    yield None
    got(a)
    first = t0[y].astype(F32)
    for s in range(3):
        first += f0[s].astype(F32)
    got(b)
    yield first, t1[xh].astype(F32) + f1[0].astype(F32)


def sum_rows_scratch(columns):
    return [
        pltpu.VMEM((2, 4, 2, 64, columns), BF),
        pltpu.VMEM((2, 4, 2, 64, columns), BF),
        *sum_scratch(64, columns),
    ]


def sum_rows(rows, scratch, wires, at):
    landed, own, rest = scratch[0], scratch[1], scratch[2:]
    core = at[3]
    copies = [
        wires.go(rows.at[:, :, 1 - core, part], landed.at[part], sibling(at)) for part in range(2)
    ]
    yield None
    for part in range(2):
        got([copies[part]])
        for i in range(4):
            for h in range(2):
                own[part, i, h] = (
                    rows[i, h, core, part].astype(F32) + landed[part, i, h].astype(F32)
                ).astype(BF)
    for result in sum_chips(own, rest, wires, at):
        yield result


def final(steps):
    result = None
    for result in steps:
        pass
    return result


def block_out_kernel(rows, middle, out, *rest):
    scratch, (ssem, rsem) = rest[:-2], rest[-2:]
    at = place()
    greet(ctx_and_sibling(at))
    wires = Wires(ssem, rsem)
    parts = final(sum_rows(rows, scratch, wires, at))
    for part in range(2):
        cut = slice(64 * part, 64 * part + 64)
        out[cut] = (middle[cut] + parts[part]).astype(BF)
    wires.close()


def block_out_call(rows, middle):
    return pl.pallas_call(
        block_out_kernel,
        out_shape=shape((ROWS, WIDTH)),
        in_specs=[vm()] * 2,
        out_specs=vm(),
        scratch_shapes=[*sum_rows_scratch(WIDTH), *wire_sems(16)],
        compiler_params=pltpu.CompilerParams(
            collective_id=5, has_side_effects=True, vmem_limit_bytes=VMEM_BYTES
        ),
        name="block_out",
    )(rows.reshape(4, 2, 2, 2, 64, WIDTH), middle)


def split_dot(left, right, form):
    high = left.astype(BF)
    low = (left - high.astype(F32)).astype(BF)
    return form(high, right) + form(low, right)


def norm_back(grad, gain, n, inverse):
    scaled = grad * gain
    return inverse * (scaled - n * jnp.mean(scaled * n, -1, keepdims=True))


def token_grad_kernel(
    d_rows, middle, gates, dy, rows, router, wo, ot,
    d_mid, d_o, small, g_out,
    low, product, *rest,
):
    scratch, (ssem, rsem) = rest[:-2], rest[-2:]
    at = place()
    core = at[3]
    near = sibling(at)
    greet(ctx_and_sibling(at))
    wires = Wires(ssem, rsem)
    steps = sum_rows(d_rows, scratch, wires, at)
    next(steps)
    next(steps)
    n, inverse = normed(middle[...])
    hidden = (n * rows[1:2]).astype(BF)
    parts = final(steps)
    total = jnp.concatenate(parts, 0)
    d_hidden = total[:, 0:WIDTH]
    both = total[:, WIDTH:TALL]
    gate = gates[...]
    lane = iota((ROWS, 128), 1)
    d_gate = jnp.where(lane < EXPERTS, both + pltpu.roll(both, 128 - EXPERTS, 1), 0.0)
    centre = jnp.sum(gate * d_gate, -1, keepdims=True)
    d_logits = gate * (d_gate - centre)
    d_hidden += split_dot(d_logits, router[...], dot_t)
    d_middle = norm_back(d_hidden, rows[1:2], n, inverse) + dy[...].astype(F32)
    d_low = d_middle.astype(BF)
    low[core] = d_low
    swap = wires.go(low.at[core], low.at[core], near)
    d_mid[...] = d_middle
    grads = split_dot(jnp.transpose(d_logits), hidden, dot)
    line = jnp.sum(d_hidden * n, 0, keepdims=True)
    small[...] = grads + jnp.where(iota((128, WIDTH), 0) == EXPERTS + 1, line, 0.0)
    got([swap])
    chip_rows = low[...].reshape(256, WIDTH)
    d_o[...] = dot_t(chip_rows, wo[...].reshape(768, WIDTH)).astype(BF)
    product[...] = dot(ot[...], chip_rows).astype(BF).reshape(4, 4, 3, 16, WIDTH)
    lanes = pl.ds(pl.multiple_of((1 - core) * 768, 128), 768)
    mine = pl.ds(pl.multiple_of(core * 768, 128), 768)
    swap = wires.go(product.at[:, :, :, :, lanes], g_out.at[core], near)
    for i in range(4):
        g_out[core, i] = product[i, :, :, :, mine]
    got([swap])
    wires.close()


def token_grad_call(d_rows, middle, gates, dy, rows, router, wo, ot):
    return pl.pallas_call(
        token_grad_kernel,
        out_shape=[
            shape((ROWS, WIDTH), F32),
            shape((256, 768)),
            shape((128, WIDTH), F32),
            shape((2, 4, 4, 3, 16, 768)),
        ],
        in_specs=[vm()] * 8,
        out_specs=[vm()] * 4,
        scratch_shapes=[
            pltpu.VMEM((2, ROWS, WIDTH), BF),
            pltpu.VMEM((4, 4, 3, 16, WIDTH), BF),
            *sum_rows_scratch(TALL),
            *wire_sems(16),
        ],
        compiler_params=pltpu.CompilerParams(
            collective_id=4, has_side_effects=True, vmem_limit_bytes=VMEM_BYTES
        ),
        name="token_grad",
    )(d_rows.reshape(4, 2, 2, 2, 64, TALL), middle, gates, dy, rows, router, wo, ot)


def gather_sums(ref, landings, wires, at):
    orders = tuple(order[::-1] for order in ORDERS)
    waits = [[], [], []]

    def send(part, phase):
        fixed = orders[part][: phase + 1]
        dim = fixed[-1]
        for step in (1, 2, 3):
            peer = ring(at, dim, step)
            spot = ref.at[block_of(ref, part, fixed, peer)]
            waits[part].append(wires.go(spot, landings[part][phase].at[step - 1], peer))

    def add(part, phase):
        got(waits[part])
        waits[part] = []
        fixed = orders[part][: phase + 1]
        index = block_of(ref, part, fixed, at)
        total = ref[index].astype(F32)
        for step in range(3):
            total += landings[part][phase][step].astype(F32)
        ref[index] = total.astype(BF)

    for part in range(3):
        send(part, 0)
    yield
    for phase in range(3):
        for part in range(3):
            add(part, phase)
            if phase < 2:
                send(part, phase + 1)
        yield


def landing_shapes():
    sizes = {0: 2, 1: 4, 2: 4}
    found = []
    for order in ORDERS:
        back = order[::-1]
        for phase in range(3):
            fixed = back[: phase + 1]
            dims = [
                size
                for size, dim in ((2, 0), (4, 2), (4, 1))
                if dim not in fixed
            ]
            found.append(
                pltpu.VMEM((3, *dims, 16, QUARTER if 0 in fixed else HALF), BF)
            )
    return found


def last_kernel(
    dkv, dq, h1t, weights, g_out, small, x, d_mid, rows, cosine, sine,
    grad_in, g_q, g_k, g_v, g_o, g_m,
    whole, product, arrived, slots, taken, cos_v, sin_v, *rest,
):
    landings = [rest[3 * i : 3 * i + 3] for i in range(3)]
    chips = rest[9:15]
    ssem, rsem, lsem = rest[15:]
    at = place()
    xx, y, z, core = at
    xh, chip = xx // 2, y * 2 + xx // 2
    near = sibling(at)
    diagonal = sibling(ring(at, 0, 2))
    greet(all_peers(at) + [near, diagonal])
    wires = Wires(ssem, rsem)
    tables = [
        pltpu.make_async_copy(src.at[pl.ds(pl.multiple_of(chip * 256, 256), 256)], dst, lsem.at[i])
        for i, (src, dst) in enumerate(((cosine, cos_v), (sine, sin_v)))
    ]
    for copy in tables:
        copy.start()
    steps = sum_chips(dkv, chips, wires, at)
    next(steps)
    whole[:, :, :, :, :, COL_O:COL_M] = g_out[...]
    n, inverse = normed(x[...].astype(F32))
    parts = final(steps)
    for copy in tables:
        copy.wait()
    total = jnp.concatenate(parts, 0)
    dk = turn(total[:, 0:256], cos_v[...], -sin_v[...]).astype(BF)
    grads = jnp.concatenate([dq[...], dk, total[:, 256:512].astype(BF)], 1)
    into = weights[:, :, :, :, :, 0:COL_O].reshape(WIDTH, COL_O)
    back = dot_t(grads, into)
    product[0] = back[0:128]
    product[1] = back[128:256]
    swap = wires.go(product.at[1 - core], arrived, near)
    whole[:, :, :, :, :, 0:COL_O] = dot(h1t[...], grads).astype(BF).reshape(2, 4, 4, 3, 16, COL_O)
    got([swap])
    d_hidden = product[core] + arrived[...]
    line = jnp.sum(d_hidden * n, 0, keepdims=True)
    tiny = small[...] + jnp.where(iota((128, WIDTH), 0) == EXPERTS, line, 0.0)
    whole[:, :, :, :, :, COL_M:COL_END] = (
        jnp.transpose(tiny).astype(BF).reshape(2, 4, 4, 3, 16, 128)
    )
    whole[:, :, :, :, :, COL_END:HALF] = jnp.zeros((2, 4, 4, 3, 16, HALF - COL_END), BF)
    sums = gather_sums(whole, landings, wires, at)
    next(sums)
    grad_in[...] = d_mid[...] + norm_back(d_hidden, rows[0:1], n, inverse)
    for _ in sums:
        pass
    lanes = pl.ds(pl.multiple_of(xh * QUARTER, 128), QUARTER)
    unit = jnp.concatenate([whole[xx % 2, z, y, part, :, lanes] for part in range(3)], 0)
    slots[...] = dot(regroup_back(), unit).astype(BF).reshape(4, 16, QUARTER)
    mine = core * 2 + xh
    copies = [
        wires.go(slots.at[peer[0] // 2 * 2 + peer[3]], taken.at[mine], peer)
        for peer in (near, ring(at, 0, 2), diagonal)
    ]
    taken[mine] = slots[xh * 2 + core]
    got(copies)
    halves = [
        jnp.concatenate([taken[2 * i], taken[2 * i + 1]], 1).astype(F32)[0:12] for i in range(2)
    ]
    for i, half in enumerate(halves):
        g_q[:, 768 * i : 768 * i + 768] = half[:, 0:COL_K]
        g_k[:, 256 * i : 256 * i + 256] = half[:, COL_K:COL_V]
        g_v[:, 256 * i : 256 * i + 256] = half[:, COL_V:COL_O]
        g_o[:, 768 * i : 768 * i + 768] = half[:, COL_O:COL_M]
    g_m[...] = halves[0][:, COL_M:COL_END] + halves[1][:, COL_M:COL_END]
    wires.close()


def last_call(dkv, dq, h1t, weights, g_out, small, x, d_mid, rows, cosine, sine):
    return pl.pallas_call(
        last_kernel,
        out_shape=[
            shape((ROWS, WIDTH), F32),
            shape((12, WIDTH), F32),
            shape((12, 512), F32),
            shape((12, 512), F32),
            shape((12, WIDTH), F32),
            shape((12, 128), F32),
        ],
        in_specs=[vm()] * 9 + [hbm()] * 2,
        out_specs=[vm()] * 6,
        scratch_shapes=[
            pltpu.VMEM((2, 4, 4, 3, 16, HALF), BF),
            pltpu.VMEM((2, ROWS, WIDTH), F32),
            pltpu.VMEM((ROWS, WIDTH), F32),
            pltpu.VMEM((4, 16, QUARTER), BF),
            pltpu.VMEM((4, 16, QUARTER), BF),
            pltpu.VMEM((256, 128), F32),
            pltpu.VMEM((256, 128), F32),
            *landing_shapes(),
            *sum_scratch(128, 512),
            *wire_sems(48),
            pltpu.SemaphoreType.DMA((2,)),
        ],
        compiler_params=pltpu.CompilerParams(
            collective_id=6, has_side_effects=True, vmem_limit_bytes=VMEM_BYTES
        ),
        name="weight_grad",
    )(
        dkv.reshape(2, 4, 2, 128, 512), dq, h1t, weights, g_out, small, x, d_mid, rows,
        cosine, sine,
    )


def tables():
    frequency = np.exp(
        np.arange(HEAD // 2, dtype=np.float32) * np.float32(-2.0 * math.log(10000.0) / HEAD)
    )
    angles = np.arange(LENGTH, dtype=np.float32)[:, None] * frequency[None, :]
    cosine, sine = np.cos(angles), np.sin(angles)
    return (
        np.concatenate([cosine] * 4, 1).astype(np.float32),
        np.concatenate([-sine, sine] * 2, 1).astype(np.float32),
    )


def stage_weights(w_query, key_weight, value_weight, w_out, w_router, gain_attn, gain_ffn):
    small = jnp.concatenate([w_router, gain_attn[:, None], gain_ffn[:, None]], 1)
    halves = []
    for i in range(2):
        halves += [
            w_query[:, 768 * i : 768 * i + 768],
            key_weight[:, 256 * i : 256 * i + 256],
            value_weight[:, 256 * i : 256 * i + 256],
            w_out[:, 768 * i : 768 * i + 768],
            small,
            jnp.zeros((12, HALF - COL_M - 34), BF),
        ]
    wide = jnp.concatenate(halves, 1)
    wide = jnp.pad(wide, ((0, 4), (0, 0)))
    return jnp.stack([wide[:, QUARTER * i : QUARTER * i + QUARTER] for i in range(4)])


def body(
    block_in, routes, cotangent, gain_attn, w_query, key_weight, value_weight, w_out,
    gain_ffn, w_router, w_gate, w_up, w_down,
):
    gate_full = lax.all_gather(w_gate, "seq", axis=1, tiled=True)
    up_full = lax.all_gather(w_up, "seq", axis=1, tiled=True)
    down_full = lax.all_gather(w_down, "seq", axis=1, tiled=True)
    cosine, sine = (jnp.asarray(table) for table in tables())
    x, dy = block_in[0], cotangent[0]
    stage = stage_weights(
        w_query, key_weight, value_weight, w_out, w_router, gain_attn, gain_ffn
    )
    weights, wo, rows, router, q, kv, h1t = first_call(stage, x, cosine, sine)
    kv = kv.reshape(LENGTH, 512)
    o, ot, lse = attend_call(q, kv)
    all_dy = share_call(dy.reshape(2, 64, WIDTH))
    middle, gates, tall = middle_call(o, wo, x, routes[0], rows, router)
    out_rows, d_rows, g_gate, g_up, g_down = expert_call(tall, all_dy, gate_full, up_full, down_full)
    g_gate = lax.psum_scatter(g_gate, "seq", scatter_dimension=1, tiled=True)
    g_up = lax.psum_scatter(g_up, "seq", scatter_dimension=1, tiled=True)
    g_down = lax.psum_scatter(g_down, "seq", scatter_dimension=1, tiled=True)
    d_mid, d_o, small, g_out = token_grad_call(
        d_rows, middle, gates, dy, rows, router, wo, ot
    )
    block_out = block_out_call(out_rows, middle)
    dq, dkv = attend_back_call(q, kv, d_o, lse, cosine, sine)
    grad_in, g_q, g_k, g_v, g_o, g_m = last_call(
        dkv, dq, h1t, weights, g_out, small, x, d_mid, rows, cosine, sine
    )
    return (
        block_out[None],
        grad_in[None],
        g_m[:, EXPERTS],
        g_q,
        g_k,
        g_v,
        g_o,
        g_m[:, EXPERTS + 1],
        g_m[:, 0:EXPERTS],
        g_gate.astype(F32),
        g_up.astype(F32),
        g_down.astype(F32),
    )


def solution(mesh):
    tokens, owned, experts = P("seq", "ctx", None), P(("seq", "ctx"), None), P("ctx", "seq", None)
    vector = P(("seq", "ctx"))
    return jax.shard_map(
        body,
        mesh=mesh,
        in_specs=(
            tokens, tokens, tokens, vector, owned, owned, owned, owned, vector, owned,
            experts, experts, experts,
        ),
        out_specs=(
            tokens, tokens, vector, owned, owned, owned, owned, vector, owned,
            experts, experts, experts,
        ),
        check_vma=False,
    )
```

time: 1740 us -> 602 us (0.35)
  waiting for transfers between devices: 1150 us -> 3.19 us
  Pallas kernels: 0 us -> 561 us
  local copies, waits for them, and re-layouts: 285 us -> 9.36 us
  matrix products: 197 us -> 0 us
  other arithmetic: 55.3 us -> 6.59 us
  starting transfers between devices: 21.7 us -> 0.23 us
    unnamed x10 -> x6, waiting for transfers between devices: 694 us -> 3.13 us
    pallas_call x0 -> x9, Pallas kernels: none -> 561 us  [the longest x1 143 us: last_call(): pl.pallas_call(last_kernel, out_shape=[shape((ROWS, WIDTH), F32), shape((...]
    all_gather x4 -> x3, waiting for transfers between devices: 240 us -> 0.06 us  [the longest x1 0.02 us: body(): gate_full = lax.all_gather(w_gate, 'seq', axis=1, tiled=True)]
    all_to_all x4 -> x0, waiting for transfers between devices: 214 us -> none  [the longest x1 78.2 us: body(): lax.all_to_all(outgoing, 'ctx', split_axis=0, concat_axis=0, tiled=True)]
    dot_general x44 -> x0, matrix products: 160 us -> none  [the longest x13 46.3 us: elementwise_product(): return jnp.dot(left_side, right_side, preferred_element_type=jnp.float32)]
    unnamed x100 -> x32, local copies, waits for them, and re-layouts: 126 us -> 6.21 us
    sub x8 -> x0, matrix products: 37.6 us -> none  [soft_scores(): raised = jnp.exp(scores - top_score)]
    another operation x7 -> x2, local copies, waits for them, and re-layouts: 33 us -> 0.02 us  [the longest x1 0.02 us: stage_weights(): jnp.stack([wide[:, QUARTER * i:QUARTER * i + QUARTER] for i in range(4)])]
  transfers between devices with their start and end apart: 12 -> 6, of which waited for: 8 -> 0; matrix products, arithmetic and copies ran while one was open for 21% -> 2% of each run, Pallas kernels for 0% -> 86%
where the time goes in v1:
time: 602 us; the launch traced here: 595 us
  Pallas kernels  561 us (93%)
  between operations  14.8 us (2%)
  local copies, waits for them, and re-layouts  9.36 us (2%)
  other arithmetic  6.59 us (1%)
    pallas_call x1, Pallas kernels, last_call(): pl.pallas_call(last_kernel, out_shape=[shape((ROWS, WIDTH), F32), shape((...  143 us
    pallas_call x1, Pallas kernels, first_call(): pl.pallas_call(first_kernel, out_shape=[shape((2, 4, 4, 3, 16, HALF)), sh...  109 us
    pallas_call x1, Pallas kernels, share_call(): pl.pallas_call(share_kernel, out_shape=shape((4, 2, 2, 2, 64, WIDTH)), in...  70 us
    pallas_call x1, Pallas kernels, middle_call(): pl.pallas_call(middle_kernel, out_shape=[shape((ROWS, WIDTH), F32), shape...  62.6 us
    pallas_call x1, Pallas kernels, token_grad_call(): pl.pallas_call(token_grad_kernel, out_shape=[shape((ROWS, WIDTH), F32), s...  56.6 us
    pallas_call x1, Pallas kernels, block_out_call(): pl.pallas_call(block_out_kernel, out_shape=shape((ROWS, WIDTH)), in_specs...  55.4 us
    pallas_call x1, Pallas kernels, expert_call(): pl.pallas_call(expert_kernel, out_shape=[shape((LENGTH, WIDTH)), shape((L...  51.1 us
  transfers between devices with their start and end apart: 6, of which 0 were waited for; matrix products, arithmetic and copies ran while one was open for 2% of the time, Pallas kernels for 86%

profile of v1, /device:TPU:1, one launch (start us, length us, event | category | flops | bytes accessed | tf_op | source)
XLA Modules:
  0.0 595.4 jit_solution(17732090671592835150)
XLA Ops:
  7.2 0.0 all-gather.4.cloned.1.call-start
  7.2 0.7 all-gather.4.cloned.1.call-update
  7.9 0.0 all-gather.6.cloned.1.call-start
  8.0 0.7 all-gather.6.cloned.1.call-update
  8.7 0.0 all-gather.8.cloned.1.call-start
  8.7 0.7 all-gather.8.cloned.1.call-update
  9.4 0.0 reduce-scatter.8.cloned.1.call-start
  9.4 0.7 copy.32
  10.2 0.8 copy.33
  10.9 1.4 copy.36
  12.4 0.0 copy-start.9
  12.4 70.0 %share_cotangent.1 = bf16[4,2,2,2,64,1536]{5,4,3,2,1,0:T(8,128)(2,1)} custom-call(bf16[2,64,1536]{2,1,0:T(8,128)(2,1)} %bitcast.34), custom_call_target="tpu_custom_call" | custom-call | tf_op jit(solution)/shard_map/share_cotangent/pallas_call | solution.py:501
  82.4 0.0 copy-done.10
  82.4 0.0 copy-done.11
  82.5 0.0 copy-done.5
  82.5 0.0 copy-done.6
  82.5 0.0 copy-done.9
  82.5 0.1 concatenate.5
  82.7 0.7 pad_maximum_fusion.stage
  83.3 109.0 %weights_qkv.1 = (bf16[2,4,4,3,16,2304]{5,4,3,2,1,0:T(8,128)(2,1)}, bf16[4,4,3,16,1536]{4,3,2,1,0:T(8,128)(2,1)}, f32[8,1536]{1,0:T(8,128)}, bf16[1536,128]{1,0:...) custom-call(bf16[4,16,1152]{2,1,0:T(8,128)(2,1)} %pad_maximum_fusion.stage,, ...), custom_call_target="tpu_custom_call" | custom-call | tf_op jit(solution)/shard_map/weights_qkv/pallas_call | solution.py:264
  192.3 5.8 attend.1
  198.1 62.6 %middle.1 = (f32[128,1536]{1,0:T(8,128)}, f32[128,128]{1,0:T(8,128)}, bf16[4,2,2,2,64,1664]{5,4,3,2,1,0:T(8,128)(2,1)}) custom-call(bf16[2,128,768]{2,1,0:T(8,128)(2,1)} %bitcast.38, bf16[4,4,3,16,1536]{4,3,2,1,0:T(8,128)(2,1)} %get-tuple-element.45.wo, bf16[128,1536]{1,0:T(8,128)(2,1)} %bitcast.31, s32[128,8]{1,0:T(8,128)} %bitcast.39, ...), custom_call_target="tpu_custom_call" | custom-call | tf_op jit(solution)/shard_map/middle/pallas_call | solution.py:555
  260.7 0.0 all-gather.4.cloned.1.call-done.w_gate
  260.7 0.0 all-gather.6.cloned.1.call-done.w_up
  260.7 0.0 all-gather.8.cloned.1.call-done.w_down
  260.8 51.1 %experts.1 = (bf16[2048,1536]{1,0:T(8,128)(2,1)}, bf16[2048,1664]{1,0:T(8,128)(2,1)}, bf16[2,1536,512]{2,1,0:T(8,128)(2,1)}, bf16[2,1536,512]{2,1,0:T(8,128)(2,1)}, bf16[2,512,1536]{2,1,0:T(8,128)(2,1)}) custom-call(bf16[2048,1664]{1,0:T(8,128)(2,1)} %bitcast.28, bf16[2048,1536]{1,0:T(8,128)(2,1)} %bitcast.24, ...), custom_call_target="tpu_custom_call" | custom-call | tf_op jit(solution)/shard_map/experts/pallas_call | solution.py:694
  311.9 0.0 reduce-scatter.8.cloned.1.call-update
  311.9 0.0 reduce-scatter.6.cloned.1.call-start
  311.9 0.5 reduce-scatter.6.cloned.1.call-update
  312.5 0.0 reduce-scatter.4.cloned.1.call-start
  312.5 0.5 reduce-scatter.4.cloned.1.call-update
  313.1 55.4 %block_out.1 = bf16[128,1536]{1,0:T(8,128)(2,1)} custom-call(bf16[4,2,2,2,64,1536]{5,4,3,2,1,0:T(8,128)(2,1)} %bitcast.29, f32[128,1536]{1,0:T(8,128)} %get-tuple-element.50.middle), custom_call_target="tpu_custom_call" | custom-call | tf_op jit(solution)/shard_map/block_out/pallas_call | solution.py:816
  368.5 56.6 %token_grad.1 = (f32[128,1536]{1,0:T(8,128)}, bf16[256,768]{1,0:T(8,128)(2,1)}, f32[128,1536]{1,0:T(8,128)}, bf16[2,4,4,3,16,768]{5,4,3,2,1,0:T(8,128)(2,1)}) custom-call(bf16[4,2,2,2,64,1664]{5,4,3,2,1,0:T(8,128)(2,1)} %bitcast.27, f32[128,1536]{1,0:T(8,128)} %get-tuple-element.50.middle, f32[128,128]{1,0:T(8,128)} %get-tuple-element.52.gates, ...), custom_call_target="tpu_custom_call" | custom-call | tf_op jit(solution)/shard_map/token_grad/pallas_call | solution.py:888
  425.0 7.8 %attend_back.1 = (bf16[256,768]{1,0:T(8,128)(2,1)}, bf16[2,8,128,512]{3,2,1,0:T(8,128)(2,1)}) custom-call(bf16[256,768]{1,0:T(8,128)(2,1)} %get-tuple-element.42.q, bf16[2048,512]{1,0:T(8,128)(2,1)} %bitcast.26, bf16[256,768]{1,0:T(8,128)(2,1)} %get-tuple-element.54.d_o, f32[4,8,768]{2,1,0:T(8,128)} %get-tuple-element.55.lse, ...), custom_call_target="tpu_custom_call" | custom-call | tf_op jit(solution)/shard_map/attend_back/pallas_call | solution.py:430
  432.9 143.0 %weight_grad.1 = (f32[128,1536]{1,0:T(8,128)}, f32[12,1536]{1,0:T(8,128)}, f32[12,512]{1,0:T(8,128)}, f32[12,512]{1,0:T(8,128)}, f32[12,1536]{1,0:T(8,128)}, /*index=5*/f32[12,128]{1,0:T(8,128)}) custom-call(bf16[2,4,2,128,512]{4,3,2,1,0:T(8,128)(2,1)} %bitcast.33, bf16[256,768]{1,0:T(8,128)(2,1)} %get-tuple-element.57.dq, ...), custom_call_target="tpu_custom_call" | custom-call | tf_op jit(solution)/shard_map/weight_grad/pallas_call | solution.py:1035
  575.9 0.0 copy-start
  575.9 1.5 slice_reduce_fusion
  577.4 2.0 convert_element_type.13
  579.4 2.0 convert_element_type.12
  581.4 2.0 convert_element_type.11
  583.4 0.7 copy.44
  584.1 0.0 copy-done.1
  584.1 0.9 copy.45
  585.0 0.6 copy.46
  585.6 0.6 copy.47
  586.2 0.6 copy.48
  586.9 0.6 copy.49
  587.5 0.6 copy.50
  (23 shorter events, 0.1 us)
Async XLA Ops:
  7.2 253.5 %all-gather.4.cloned.1.call-start = ((), (), s32[]{:S(2)}) async-start(), calls=%async_computation.3 | async-start | bytes 3538944 | tf_op jit(solution)/shard_map/all_gather | solution.py:1103
  7.9 252.8 %all-gather.6.cloned.1.call-start = ((), (), s32[]{:S(2)}) async-start(), calls=%async_computation.4 | async-start | bytes 3538944 | tf_op jit(solution)/shard_map/all_gather | solution.py:1104
  8.7 252.1 %all-gather.8.cloned.1.call-start = ((), (), s32[]{:S(2)}) async-start(), calls=%async_computation.5 | async-start | bytes 3538944 | tf_op jit(solution)/shard_map/all_gather | solution.py:1105
  9.4 568.0 %reduce-scatter.8.cloned.1.call-start = ((), (), s32[]{:S(2)}) async-start(), calls=%async_computation.8 | async-start | bytes 3538944 | tf_op jit(solution)/shard_map/reduce_scatter | solution.py:1119
  12.4 70.1 %copy-start.10 = (bf16[12,512]{1,0:T(8,128)(2,1)S(1)}, bf16[12,512]{1,0:T(8,128)(2,1)}, u32[]{:S(2)}) copy-start(bf16[12,512]{1,0:T(8,128)(2,1)} %param.21) | copy-start | bytes 36868
  12.4 70.1 %copy-start.11 = (bf16[12,512]{1,0:T(8,128)(2,1)S(1)}, bf16[12,512]{1,0:T(8,128)(2,1)}, u32[]{:S(2)}) copy-start(bf16[12,512]{1,0:T(8,128)(2,1)} %param.20) | copy-start | bytes 36868
  12.4 70.1 %copy-start.5 = (bf16[12,1536]{1,0:T(8,128)(2,1)S(1)}, bf16[12,1536]{1,0:T(8,128)(2,1)}, u32[]{:S(2)}) copy-start(bf16[12,1536]{1,0:T(8,128)(2,1)} %param.22) | copy-start | bytes 110596
  12.4 70.1 %copy-start.6 = (bf16[12,1536]{1,0:T(8,128)(2,1)S(1)}, bf16[12,1536]{1,0:T(8,128)(2,1)}, u32[]{:S(2)}) copy-start(bf16[12,1536]{1,0:T(8,128)(2,1)} %param.19) | copy-start | bytes 110596
  12.4 70.1 %copy-start.9 = (bf16[12,32]{1,0:T(8,128)(2,1)S(1)}, bf16[12,32]{1,0:T(8,128)(2,1)}, u32[]{:S(2)}) copy-start(bf16[12,32]{1,0:T(8,128)(2,1)} %param.24) | copy-start | bytes 2308
  311.9 267.5 %reduce-scatter.6.cloned.1.call-start = ((), (), s32[]{:S(2)}) async-start(), calls=%async_computation.7 | async-start | bytes 3538944 | tf_op jit(solution)/shard_map/reduce_scatter | solution.py:1118
  312.5 268.9 %reduce-scatter.4.cloned.1.call-start = ((), (), s32[]{:S(2)}) async-start(), calls=%async_computation.6 | async-start | bytes 3538944 | tf_op jit(solution)/shard_map/reduce_scatter | solution.py:1117
  575.9 7.5 %copy-start = (bf16[128,1536]{1,0:T(8,128)(2,1)S(1)}, bf16[128,1536]{1,0:T(8,128)(2,1)}, u32[]{:S(2)}) copy-start(bf16[128,1536]{1,0:T(8,128)(2,1)} %block_out.1) | copy-start | bytes 1179652
  575.9 8.2 %copy-start.1 = (f32[128,1536]{1,0:T(8,128)S(1)}, f32[128,1536]{1,0:T(8,128)}, u32[]{:S(2)}) copy-start(f32[128,1536]{1,0:T(8,128)} %get-tuple-element.63) | copy-start | bytes 2359300
  575.9 9.1 %copy-start.3 = (f32[12,1536]{1,0:T(8,128)S(1)}, f32[12,1536]{1,0:T(8,128)}, u32[]{:S(2)}) copy-start(f32[12,1536]{1,0:T(8,128)} %get-tuple-element.105) | copy-start | bytes 221188
  575.9 9.7 %copy-start.8 = (f32[12,512]{1,0:T(8,128)S(1)}, f32[12,512]{1,0:T(8,128)}, u32[]{:S(2)}) copy-start(f32[12,512]{1,0:T(8,128)} %get-tuple-element.106) | copy-start | bytes 73732
  575.9 10.3 %copy-start.7 = (f32[12,512]{1,0:T(8,128)S(1)}, f32[12,512]{1,0:T(8,128)}, u32[]{:S(2)}) copy-start(f32[12,512]{1,0:T(8,128)} %get-tuple-element.107) | copy-start | bytes 73732
  575.9 10.9 %copy-start.2 = (f32[12,1536]{1,0:T(8,128)S(1)}, f32[12,1536]{1,0:T(8,128)}, u32[]{:S(2)}) copy-start(f32[12,1536]{1,0:T(8,128)} %get-tuple-element.108) | copy-start | bytes 221188
  577.4 10.1 %copy-start.4 = (f32[12,128]{1,0:T(8,128)S(1)}, f32[12,128]{1,0:T(8,128)}, u32[]{:S(2)}) copy-start(f32[12,128]{1,0:T(8,128)} %get-tuple-element.64) | copy-start | bytes 18436
Sparse Core Ops, SparseCore 0:
  9.7 62.2 all-gather.3
  73.6 79.8 all-gather.5
  155.1 56.8 all-gather.7
  312.0 71.5 reduce-scatter.7
  385.9 59.3 reduce-scatter.5
  447.5 59.7 reduce-scatter.3

commit v2 on v1

v2 whole, which is shorter than its diff:
```python
import functools
import math

import jax
import jax.numpy as jnp
import numpy as np
from jax import lax
from jax.experimental import pallas as pl
from jax.experimental.pallas import tpu as pltpu
from jax.sharding import PartitionSpec as P

WIDTH = 1536
HEADS = 24
KV_HEADS = 8
HEAD = 64
TOPK = 8
ROWS = 128
LENGTH = 2048
EXPERTS = 32
FF = 512
CAP = 48
EPSILON = 1e-06

BF = jnp.bfloat16
F32 = jnp.float32
MESH = pl.DeviceIdType.MESH
VMEM_BYTES = 60 << 20

IN_Q, OUT_Q = 768, 384
IN_H, OUT_H = 2 * IN_Q, 2 * OUT_Q
STAGE = IN_Q + OUT_Q
COL_K, COL_V, COL_M, COL_END = 768, 1024, 1280, 1408
TALL = WIDTH + 128


def vm():
    return pl.BlockSpec(memory_space=pltpu.VMEM)


def hbm():
    return pl.BlockSpec(memory_space=pl.ANY)


def shape(dims, dtype=BF):
    return jax.ShapeDtypeStruct(dims, dtype)


def place():
    seq, ctx = lax.axis_index("seq"), lax.axis_index("ctx")
    return (ctx // 2 % 2 * 2 + seq // 4, ctx // 4, seq % 4, ctx % 2)


def device(x, y, z, core):
    return (x % 2 * 4 + z, (y * 2 + x // 2) * 2 + core)


def ring(at, dim, step):
    x, y, z, core = at
    if dim == 0:
        return ((x + step) % 4, y, z, core)
    if dim == 1:
        return (x, (y + step) % 4, z, core)
    return (x, y, (z + step) % 4, core)


def sibling(at):
    return (at[0], at[1], at[2], 1 - at[3])


def greet(peers):
    barrier = pltpu.get_barrier_semaphore()
    for peer in peers:
        pl.semaphore_signal(barrier, inc=1, device_id=device(*peer), device_id_type=MESH)
    pl.semaphore_wait(barrier, len(peers))


class Wires:
    def __init__(self, send, recv):
        self.send, self.recv, self.used, self.open = send, recv, 0, []

    def go(self, src, dst, peer):
        n = self.used
        self.used += 1
        copy = pltpu.make_async_remote_copy(
            src_ref=src,
            dst_ref=dst,
            send_sem=self.send.at[n],
            recv_sem=self.recv.at[n],
            device_id=device(*peer),
            device_id_type=MESH,
        )
        copy.start()
        self.open.append(copy)
        return copy

    def close(self):
        for copy in self.open:
            copy.wait_send()


def wire_sems(n):
    return [pltpu.SemaphoreType.DMA((n,)), pltpu.SemaphoreType.DMA((n,))]


def got(copies):
    for copy in copies:
        copy.wait_recv()


def dot(a, b):
    return jnp.dot(a, b, preferred_element_type=F32)


def dot_t(a, b):
    return lax.dot_general(a, b, (((1,), (1,)), ((), ())), preferred_element_type=F32)


def t_dot(a, b):
    return lax.dot_general(a, b, (((0,), (0,)), ((), ())), preferred_element_type=F32)


def iota(dims, axis):
    return lax.broadcasted_iota(jnp.int32, dims, axis)


def turn(block, cosine, sine):
    low = iota((block.shape[0], 128), 1) % HEAD < HEAD // 2
    parts = []
    for i in range(block.shape[1] // 128):
        unit = block[:, 128 * i : 128 * i + 128]
        other = jnp.where(low, pltpu.roll(unit, 96, 1), pltpu.roll(unit, 32, 1))
        parts.append(unit * cosine + other * sine)
    return jnp.concatenate(parts, 1)


def regroup():
    r, c = iota((48, 64), 0), iota((48, 64), 1)
    owner = c // 16 % 2 * 2 + c // 32
    hit = (r == owner * 12 + c % 16) & (c % 16 < 12)
    return hit.astype(F32).astype(BF)


def regroup_back():
    r, c = iota((64, 48), 0), iota((64, 48), 1)
    hit = (c == r // 16 * 12 + r % 16) & (r % 16 < 12)
    return hit.astype(F32).astype(BF)


ORDERS = ((0, 1, 2), (1, 2, 0), (2, 0, 1))


def block_of(quarter, part, fixed, at):
    x, y, z, _ = at
    whole = slice(None)
    columns = (
        pl.ds(pl.multiple_of(x // 2 * quarter, 128), quarter)
        if 0 in fixed
        else pl.ds(0, 2 * quarter)
    )
    return (
        x % 2 if 0 in fixed else whole,
        z if 2 in fixed else whole,
        y if 1 in fixed else whole,
        part,
        whole,
        columns,
    )


def spread(ref, quarter, wires, at):
    waits = [[], [], []]
    for phase in range(3):
        for part in range(3):
            got(waits[part])
            waits[part] = []
            fixed = ORDERS[part][phase:]
            spot = ref.at[block_of(quarter, part, fixed, at)]
            for step in (1, 2, 3):
                waits[part].append(wires.go(spot, spot, ring(at, fixed[0], step)))
        yield
    for part in range(3):
        got(waits[part])


def finish(*tasks):
    for task in tasks:
        for _ in task:
            pass


def partner(at):
    return (at[0] + 1 - 2 * (at[0] % 2), at[1], at[2], at[3])


def expert_pairs(shard, pair, wires, at):
    spot = pair.at[:, at[0] % 2]
    return wires.go(shard, spot, partner(at))


def expert_spread(own, full, wires, at):
    z = at[2]
    left, right = ring(at, 2, 3), ring(at, 2, 1)
    spot = full.at[:, :, z]
    a = wires.go(own, spot, right)
    b = wires.go(own, spot, left)
    yield
    got([a])
    spot = full.at[0, :, (z + 3) % 4]
    a = wires.go(spot, spot, right)
    got([b])
    spot = full.at[1, :, (z + 1) % 4]
    b = wires.go(spot, spot, left)
    yield
    got([a, b])


def expert_sum_scratch(rows, columns):
    return [
        pltpu.VMEM((3, 2, 2, rows, columns), BF),
        pltpu.VMEM((2, 2, rows, columns), BF),
        pltpu.VMEM((2, 2, 2, rows, columns), BF),
        pltpu.VMEM((2, rows, columns), BF),
        pltpu.SemaphoreType.DMA((3,)),
    ]


def expert_sum(grads, result, scratch, wires, at):
    own, halves, pairs, last, lsem = scratch
    z, x_lo = at[2], at[0] % 2
    left, right = ring(at, 2, 3), ring(at, 2, 1)
    loads = [
        pltpu.make_async_copy(grads.at[:, :, (z + step) % 4], own.at[i], lsem.at[i])
        for i, step in enumerate((0, 1, 3))
    ]
    for copy in loads:
        copy.start()
    a = wires.go(grads.at[0, :, (z + 2) % 4], halves.at[0], right)
    b = wires.go(grads.at[1, :, (z + 2) % 4], halves.at[1], left)
    yield
    for copy in loads:
        copy.wait()
    got([a])
    for i in range(2):
        own[1, 0, i] = (own[1, 0, i].astype(F32) + halves[0, i].astype(F32)).astype(BF)
    a = wires.go(own.at[1], pairs.at[0], right)
    got([b])
    for i in range(2):
        own[2, 1, i] = (own[2, 1, i].astype(F32) + halves[1, i].astype(F32)).astype(BF)
    b = wires.go(own.at[2], pairs.at[1], left)
    yield
    got([a, b])
    for e in range(2):
        for i in range(2):
            own[0, e, i] = (
                own[0, e, i].astype(F32)
                + pairs[0, e, i].astype(F32)
                + pairs[1, e, i].astype(F32)
            ).astype(BF)
    a = wires.go(own.at[0, :, 1 - x_lo], last, partner(at))
    yield
    got([a])
    for e in range(2):
        result[e] = own[0, e, x_lo].astype(F32) + last[e].astype(F32)


def ctx_peers(at):
    return [ring(at, 1, 1), ring(at, 1, 2), ring(at, 1, 3), ring(at, 0, 2)]


def all_peers(at):
    return [ring(at, d, s) for d in range(3) for s in (1, 2, 3)]


def first_kernel(
    stage, x, cosine, sine, w_gate, w_up, w_down,
    weights, rows, router, q, kv, h1t, unit_o, gate_full, up_pair, down_pair,
    both, slots, cos_v, sin_v, ssem, rsem, lsem,
):
    at = place()
    xx, y, z, core = at
    xh, chip = xx // 2, y * 2 + xx // 2
    diagonal = sibling(ring(at, 0, 2))
    greet(all_peers(at) + [sibling(at), diagonal])
    wires = Wires(ssem, rsem)
    local = [
        (cosine.at[pl.ds(pl.multiple_of(chip * 256, 256), 256)], cos_v),
        (sine.at[pl.ds(pl.multiple_of(chip * 256, 256), 256)], sin_v),
        (w_gate, gate_full.at[:, xx % 2, z]),
        (w_up, up_pair.at[:, xx % 2]),
        (w_down, down_pair.at[:, xx % 2]),
    ]
    local = [pltpu.make_async_copy(src, dst, lsem.at[i]) for i, (src, dst) in enumerate(local)]
    for copy in local:
        copy.start()
    mine = core * 2 + xh
    first = [
        wires.go(stage.at[peer[3] * 2 + peer[0] // 2], slots.at[mine], peer)
        for peer in (sibling(at), ring(at, 0, 2), diagonal)
    ]
    tokens = wires.go(x, both.at[core], sibling(at))
    slots[mine] = stage[mine]
    both[core] = x[...]
    got(first)
    unit = dot(regroup(), slots[...].reshape(64, STAGE)).astype(BF)
    lanes = pl.ds(pl.multiple_of(xh * IN_Q, 128), IN_Q)
    for part in range(3):
        weights[xx % 2, z, y, part, :, lanes] = unit[16 * part : 16 * part + 16, 0:IN_Q]
        unit_o[part] = unit[16 * part : 16 * part + 16, IN_Q:STAGE]
    task = spread(weights, IN_Q, wires, at)
    next(task)
    spot = gate_full.at[:, xx % 2, z]
    pair = wires.go(w_gate, spot, partner(at))
    finish(task)
    for copy in local:
        copy.wait()
    got([pair])
    gate = expert_spread(gate_full.at[:, :, z], gate_full, wires, at)
    next(gate)
    pairs = [
        expert_pairs(w_up, up_pair, wires, at),
        expert_pairs(w_down, down_pair, wires, at),
    ]

    small = weights[:, :, :, :, :, COL_M:COL_END].reshape(WIDTH, 128)
    router[...] = small
    turned = jnp.transpose(small.astype(F32))
    rows[...] = turned[32:40]
    got([tokens])
    values = both[...].reshape(256, WIDTH).astype(F32)
    inverse = lax.rsqrt(jnp.mean(values * values, -1, keepdims=True) + EPSILON)
    hidden = (values * inverse * turned[32:33]).astype(BF)
    made = dot(hidden, weights[:, :, :, :, :, 0:COL_M].reshape(WIDTH, COL_M))
    cos, sin = cos_v[...], sin_v[...]
    key = turn(made[:, COL_K:COL_V], cos, sin).astype(BF)
    value = made[:, COL_V:COL_M].astype(BF)
    for part in range(2):
        kv[y, xh, part, :, 0:256] = key[128 * part : 128 * part + 128]
        kv[y, xh, part, :, 256:512] = value[128 * part : 128 * part + 128]
    own = [kv.at[y, xh, 0], kv.at[y, xh, 1]]
    a = [wires.go(own[0], own[0], ring(at, 1, s)) for s in (1, 2, 3)]
    b = [wires.go(own[1], own[1], ring(at, 0, 2))]
    q[...] = turn(made[:, 0:COL_K], cos, sin).astype(BF)
    got(a)
    column = kv.at[:, xh, 0]
    a = [wires.go(column, column, ring(at, 0, 2))]
    got(b)
    pair = kv.at[y, :, 1]
    b = [wires.go(pair, pair, ring(at, 1, s)) for s in (1, 2, 3)]
    h1t[...] = jnp.transpose(hidden.astype(F32)).astype(BF)
    next(gate)
    got(a)
    got(b)
    finish(gate)
    got(pairs)
    wires.close()


def first_call(stage, x, cosine, sine, w_gate, w_up, w_down):
    return pl.pallas_call(
        first_kernel,
        out_shape=[
            shape((2, 4, 4, 3, 16, IN_H)),
            shape((8, WIDTH), F32),
            shape((WIDTH, 128)),
            shape((256, 768)),
            shape((4, 2, 2, 128, 512)),
            shape((WIDTH, 256)),
            shape((3, 16, OUT_Q)),
            shape((2, 2, 4, 192, FF)),
            shape((2, 2, 192, FF)),
            shape((2, 2, 64, WIDTH)),
        ],
        in_specs=[vm(), vm()] + [hbm()] * 5,
        out_specs=[vm()] * 7 + [hbm()] * 3,
        scratch_shapes=[
            pltpu.VMEM((2, 128, WIDTH), BF),
            pltpu.VMEM((4, 16, STAGE), BF),
            pltpu.VMEM((256, 128), F32),
            pltpu.VMEM((256, 128), F32),
            *wire_sems(56),
            pltpu.SemaphoreType.DMA((5,)),
        ],
        compiler_params=pltpu.CompilerParams(
            collective_id=1, has_side_effects=True, vmem_limit_bytes=VMEM_BYTES
        ),
        name="weights_qkv",
    )(stage, x, cosine, sine, w_gate, w_up, w_down)


def share_rows(ref, wires, at):
    x, y, _, core = at
    xh = x // 2
    near, far = sibling(at), ring(at, 0, 2)

    def pass_on(spot, peer):
        return wires.go(spot, spot, peer)

    inner = [pass_on(ref.at[y, xh, core], near)]
    a = [pass_on(ref.at[y, xh, core, 0], ring(at, 1, s)) for s in (1, 2, 3)]
    b = [pass_on(ref.at[y, xh, core, 1], far)]
    yield
    got(b)
    b = [pass_on(ref.at[y, :, core, 1], ring(at, 1, s)) for s in (1, 2, 3)]
    got(a)
    a = [pass_on(ref.at[:, xh, core, 0], far)]
    inner.append(pass_on(ref.at[y, 1 - xh, core, 1], near))
    for s in (1, 2, 3):
        inner.append(pass_on(ref.at[(y + s) % 4, xh, core, 0], near))
    yield
    got(a)
    inner.append(pass_on(ref.at[:, 1 - xh, core, 0], near))
    got(b)
    for s in (1, 2, 3):
        inner.append(pass_on(ref.at[(y + s) % 4, :, core, 1], near))
    yield
    got(inner)


def ctx_and_sibling(at):
    return ctx_peers(at) + [sibling(at)]


def sum_scratch(rows, columns):
    return [
        pltpu.VMEM((4, rows, columns), BF),
        pltpu.VMEM((3, 2, rows, columns), BF),
        pltpu.VMEM((4, rows, columns), BF),
        pltpu.VMEM((2, rows, columns), BF),
        pltpu.VMEM((3, rows, columns), BF),
        pltpu.VMEM((1, rows, columns), BF),
    ]


def sum_chips(source, scratch, wires, at):
    e0, e1, t0, t1, f0, f1 = scratch
    x, y, _, _ = at
    xh = x // 2
    far = ring(at, 0, 2)
    a = [wires.go(source.at[0, :, 1 - xh], e0, far)]
    b = [
        wires.go(source.at[1, (y + s) % 4], e1.at[s - 1], ring(at, 1, s)) for s in (1, 2, 3)
    ]
    yield None
    got(a)
    for i in range(4):
        t0[i] = (source[0, i, xh].astype(F32) + e0[i].astype(F32)).astype(BF)
    a = [wires.go(t0.at[(y + s) % 4], f0.at[s - 1], ring(at, 1, s)) for s in (1, 2, 3)]
    got(b)
    for i in range(2):
        total = source[1, y, i].astype(F32)
        for s in range(3):
            total += e1[s, i].astype(F32)
        t1[i] = total.astype(BF)
    b = [wires.go(t1.at[1 - xh], f1.at[0], far)]
    yield None
    got(a)
    first = t0[y].astype(F32)
    for s in range(3):
        first += f0[s].astype(F32)
    got(b)
    yield first, t1[xh].astype(F32) + f1[0].astype(F32)


def sum_rows_scratch(columns):
    return [
        pltpu.VMEM((2, 4, 2, 64, columns), BF),
        pltpu.VMEM((2, 4, 2, 64, columns), BF),
        *sum_scratch(64, columns),
    ]


def sum_rows(rows, scratch, wires, at):
    landed, own, rest = scratch[0], scratch[1], scratch[2:]
    core = at[3]
    copies = [
        wires.go(rows.at[:, :, 1 - core, part], landed.at[part], sibling(at)) for part in range(2)
    ]
    yield None
    for part in range(2):
        got([copies[part]])
        for i in range(4):
            for h in range(2):
                own[part, i, h] = (
                    rows[i, h, core, part].astype(F32) + landed[part, i, h].astype(F32)
                ).astype(BF)
    for result in sum_chips(own, rest, wires, at):
        yield result


def final(steps):
    result = None
    for result in steps:
        pass
    return result


def gather_sums(ref, quarter, landings, wires, at):
    orders = tuple(order[::-1] for order in ORDERS)
    waits = [[], [], []]

    def send(part, phase):
        fixed = orders[part][: phase + 1]
        dim = fixed[-1]
        for step in (1, 2, 3):
            peer = ring(at, dim, step)
            spot = ref.at[block_of(quarter, part, fixed, peer)]
            waits[part].append(wires.go(spot, landings[part][phase].at[step - 1], peer))

    def add(part, phase):
        got(waits[part])
        waits[part] = []
        fixed = orders[part][: phase + 1]
        index = block_of(quarter, part, fixed, at)
        total = ref[index].astype(F32)
        for step in range(3):
            total += landings[part][phase][step].astype(F32)
        ref[index] = total.astype(BF)

    for part in range(3):
        send(part, 0)
    yield
    for phase in range(3):
        for part in range(3):
            add(part, phase)
            if phase < 2:
                send(part, phase + 1)
        yield


def landing_shapes(quarter):
    found = []
    for order in ORDERS:
        for phase in range(3):
            fixed = order[::-1][: phase + 1]
            dims = [size for size, dim in ((2, 0), (4, 2), (4, 1)) if dim not in fixed]
            found.append(pltpu.VMEM((3, *dims, 16, quarter if 0 in fixed else 2 * quarter), BF))
    return found


def attend_kernel(
    q, kv, unit_o, dy, up_pair,
    o, ot, lse, wo, all_dy, up_full,
    scores, vt, qt, qz, out_t, columns, ssem, rsem, lsem,
):
    at = place()
    x, y, z, core = at
    chip = y * 2 + x // 2
    near = sibling(at)
    greet(all_peers(at) + [near])
    wires = Wires(ssem, rsem)
    local = [
        pltpu.make_async_copy(dy, all_dy.at[y, x // 2, core], lsem.at[0]),
        pltpu.make_async_copy(up_pair, up_full.at[:, :, z], lsem.at[1]),
    ]
    for copy in local:
        copy.start()
    lanes = pl.ds(pl.multiple_of(x // 2 * OUT_Q, 128), OUT_Q)
    for part in range(3):
        columns[x % 2, z, y, part, :, lanes] = unit_o[part]
    out_task = spread(columns, OUT_Q, wires, at)
    up_task = expert_spread(up_pair, up_full, wires, at)
    dy_task = share_rows(all_dy, wires, at)
    next(out_task)
    next(up_task)
    local[0].wait()
    next(dy_task)
    mine = pl.ds(pl.multiple_of(core * 768, 128), 768)

    def swap_out():
        finish(out_task)
        swap.append(
            wires.go(columns.at[1 - core], wo.at[:, :, :, :, mine], near)
        )
        for i in range(4):
            wo[i, :, :, :, mine] = columns[core, i]

    swap = []
    beside = [
        lambda: next(out_task),
        lambda: next(dy_task),
        lambda: next(out_task),
        lambda: next(up_task),
        swap_out,
        lambda: next(dy_task),
        lambda: finish(up_task),
        lambda: None,
    ]
    qt[...] = jnp.transpose(q[...].astype(F32) * 0.125).astype(BF)
    for kb in range(8):
        vt[kb] = jnp.transpose(kv[256 * kb : 256 * kb + 256, 256:512].astype(F32)).astype(BF)
    allowed = iota((256, 768), 0) <= iota((256, 768), 1) % 256
    for j in range(4):
        u, half = j // 2, j % 2
        qz[...] = jnp.zeros_like(qz)
        for g in range(3):
            h = 3 * j + g
            qz[64 * half : 64 * half + 64, 256 * g : 256 * g + 256] = qt[64 * h : 64 * h + 64]

        def score(kb):
            rows = pl.ds(pl.multiple_of(kb * 256, 256), 256)
            return rows, dot(kv[rows, 128 * u : 128 * u + 128], qz[...])

        def top(kb, most):
            rows, s = score(kb)
            scores[rows] = s
            return jnp.maximum(most, jnp.max(s.reshape(32, 8, 768), 0))

        most = lax.fori_loop(0, chip, top, jnp.full((8, 768), -1e30, F32))
        rows, s = score(chip)
        s = jnp.where(allowed, s, -1e30)
        scores[rows] = s
        most = jnp.maximum(most, jnp.max(s.reshape(32, 8, 768), 0))
        most = jnp.max(most, 0, keepdims=True)

        def raise_(kb, total):
            rows = pl.ds(pl.multiple_of(kb * 256, 256), 256)
            e = jnp.exp(scores[rows] - most)
            scores[rows] = e
            return total + jnp.sum(e.reshape(32, 8, 768), 0)

        beside[2 * j]()
        total = lax.fori_loop(0, chip + 1, raise_, jnp.zeros((8, 768), F32))
        total = jnp.sum(total, 0, keepdims=True)
        lse[j] = jnp.broadcast_to(most + jnp.log(total), (8, 768))
        inverse = 1.0 / total

        def mix(kb, acc):
            rows = pl.ds(pl.multiple_of(kb * 256, 256), 256)
            p = (scores[rows] * inverse).astype(BF)
            return acc + dot(vt[kb, 64 * j : 64 * j + 64], p)

        acc = lax.fori_loop(0, chip + 1, mix, jnp.zeros((64, 768), F32))
        for g in range(3):
            h = 3 * j + g
            out_t[64 * h : 64 * h + 64] = acc[:, 256 * g : 256 * g + 256]
        beside[2 * j + 1]()
    ot[...] = out_t[...].astype(BF)
    o[...] = jnp.transpose(out_t[...]).astype(BF)
    finish(dy_task)
    got(swap)
    local[1].wait()
    wires.close()


def attend_call(q, kv, unit_o, dy, up_pair):
    return pl.pallas_call(
        attend_kernel,
        out_shape=[
            shape((256, 768)),
            shape((768, 256)),
            shape((4, 8, 768), F32),
            shape((4, 4, 3, 16, WIDTH)),
            shape((4, 2, 2, 2, 64, WIDTH)),
            shape((2, 2, 4, 192, FF)),
        ],
        in_specs=[vm()] * 3 + [hbm()] * 2,
        out_specs=[vm()] * 4 + [hbm()] * 2,
        scratch_shapes=[
            pltpu.VMEM((LENGTH, 768), F32),
            pltpu.VMEM((8, 256, 256), BF),
            pltpu.VMEM((768, 256), BF),
            pltpu.VMEM((128, 768), BF),
            pltpu.VMEM((768, 256), F32),
            pltpu.VMEM((2, 4, 4, 3, 16, OUT_H), BF),
            *wire_sems(56),
            pltpu.SemaphoreType.DMA((2,)),
        ],
        compiler_params=pltpu.CompilerParams(
            collective_id=2, has_side_effects=True, vmem_limit_bytes=VMEM_BYTES
        ),
        name="attend",
    )(q, kv, unit_o, dy, up_pair)


def attend_back_kernel(
    q, kv, d_o, lse, out_rows, middle, g_out, g_gate, cosine, sine,
    dq, dkv, block_out, unit_o, gate_sum,
    probs, grads, kt, qt, dot_, qz, oz, acc, dqt, cos_v, sin_v, columns, *rest,
):
    row_scratch, landings = rest[:8], [rest[8 + 3 * i : 11 + 3 * i] for i in range(3)]
    expert_scratch = rest[17:22]
    ssem, rsem, lsem = rest[22:]
    at = place()
    xx, y, z, _ = at
    chip = y * 2 + xx // 2
    greet(all_peers(at) + [sibling(at)])
    wires = Wires(ssem, rsem)
    columns_in = pltpu.make_async_copy(g_out, columns, lsem.at[2])
    columns_in.start()
    tables = [
        pltpu.make_async_copy(src.at[pl.ds(pl.multiple_of(chip * 256, 256), 256)], dst, lsem.at[i])
        for i, (src, dst) in enumerate(((cosine, cos_v), (sine, sin_v)))
    ]
    for copy in tables:
        copy.start()
    row_task = sum_rows(out_rows, row_scratch, wires, at)
    gate_task = expert_sum(g_gate, gate_sum, expert_scratch, wires, at)
    out_task = gather_sums(columns, OUT_Q, landings, wires, at)
    next(row_task)
    next(gate_task)

    def start_out():
        columns_in.wait()
        next(out_task)

    beside = [
        lambda: next(row_task),
        lambda: next(gate_task),
        start_out,
        lambda: next(gate_task),
        lambda: next(row_task),
        lambda: next(out_task),
        lambda: finish(gate_task),
        lambda: next(out_task),
    ]
    qt[...] = jnp.transpose(q[...].astype(F32) * 0.125).astype(BF)
    dot_[...] = jnp.transpose(d_o[...].astype(F32)).astype(BF)
    for kb in range(8):
        kt[kb] = jnp.transpose(kv[256 * kb : 256 * kb + 256, 0:256].astype(F32)).astype(BF)
    acc[...] = jnp.zeros_like(acc)
    allowed = iota((256, 768), 0) <= iota((256, 768), 1) % 256
    for j in range(4):
        u, half = j // 2, j % 2
        qz[...] = jnp.zeros_like(qz)
        oz[...] = jnp.zeros_like(oz)
        for g in range(3):
            h = 3 * j + g
            qz[64 * half : 64 * half + 64, 256 * g : 256 * g + 256] = qt[64 * h : 64 * h + 64]
            oz[64 * half : 64 * half + 64, 256 * g : 256 * g + 256] = dot_[64 * h : 64 * h + 64]
        level = lse[j, 0:1]

        def share(kb, centre, masked):
            rows = pl.ds(pl.multiple_of(kb * 256, 256), 256)
            p = jnp.exp(dot(kv[rows, 128 * u : 128 * u + 128], qz[...]) - level)
            if masked:
                p = jnp.where(allowed, p, 0.0)
            probs[rows] = p
            dp = dot(kv[rows, 256 + 128 * u : 384 + 128 * u], oz[...])
            grads[rows] = dp
            acc[rows, 256 + 128 * u : 384 + 128 * u] += dot_t(p.astype(BF), oz[...])
            return centre + jnp.sum((p * dp).reshape(32, 8, 768), 0)

        centre = lax.fori_loop(
            0, chip, functools.partial(share, masked=False), jnp.zeros((8, 768), F32)
        )
        centre = share(chip, centre, True)
        centre = jnp.sum(centre, 0, keepdims=True)
        beside[2 * j]()

        def back(kb, total):
            rows = pl.ds(pl.multiple_of(kb * 256, 256), 256)
            ds = (probs[rows] * (grads[rows] - centre)).astype(BF)
            acc[rows, 128 * u : 128 * u + 128] += dot_t(ds, qz[...])
            return total + dot(kt[kb, 64 * j : 64 * j + 64], ds)

        total = lax.fori_loop(0, chip + 1, back, jnp.zeros((64, 768), F32))
        for g in range(3):
            h = 3 * j + g
            dqt[64 * h : 64 * h + 64] = total[:, 256 * g : 256 * g + 256] * 0.125
        beside[2 * j + 1]()
    for kb in range(8):
        for part in range(2):
            at_row = 256 * kb + 128 * part
            dkv[part, kb] = acc[at_row : at_row + 128].astype(BF)
    for copy in tables:
        copy.wait()
    dq[...] = turn(jnp.transpose(dqt[...]), cos_v[...], -sin_v[...]).astype(BF)
    parts = final(row_task)
    for part in range(2):
        cut = slice(64 * part, 64 * part + 64)
        block_out[cut] = (middle[cut] + parts[part]).astype(BF)
    finish(out_task)
    lanes = pl.ds(pl.multiple_of(xx // 2 * OUT_Q, 128), OUT_Q)
    for part in range(3):
        unit_o[part] = columns[xx % 2, z, y, part, :, lanes]
    wires.close()


def attend_back_call(q, kv, d_o, lse, out_rows, middle, g_out, g_gate, cosine, sine):
    return pl.pallas_call(
        attend_back_kernel,
        out_shape=[
            shape((256, 768)),
            shape((2, 8, 128, 512)),
            shape((ROWS, WIDTH)),
            shape((3, 16, OUT_Q)),
            shape((2, 192, FF), F32),
        ],
        in_specs=[vm()] * 6 + [hbm()] * 4,
        out_specs=[vm()] * 5,
        scratch_shapes=[
            pltpu.VMEM((LENGTH, 768), F32),
            pltpu.VMEM((LENGTH, 768), F32),
            pltpu.VMEM((8, 256, 256), BF),
            pltpu.VMEM((768, 256), BF),
            pltpu.VMEM((768, 256), BF),
            pltpu.VMEM((128, 768), BF),
            pltpu.VMEM((128, 768), BF),
            pltpu.VMEM((LENGTH, 512), F32),
            pltpu.VMEM((768, 256), F32),
            pltpu.VMEM((256, 128), F32),
            pltpu.VMEM((256, 128), F32),
            pltpu.VMEM((2, 4, 4, 3, 16, OUT_H), BF),
            *sum_rows_scratch(WIDTH),
            *landing_shapes(OUT_Q),
            *expert_sum_scratch(192, FF),
            *wire_sems(56),
            pltpu.SemaphoreType.DMA((3,)),
        ],
        compiler_params=pltpu.CompilerParams(
            collective_id=5, has_side_effects=True, vmem_limit_bytes=VMEM_BYTES
        ),
        name="attend_back",
    )(
        q, kv, d_o, lse, out_rows.reshape(4, 2, 2, 2, 64, WIDTH), middle, g_out,
        g_gate.reshape(2, 2, 4, 192, FF), cosine, sine,
    )


def normed(values):
    inverse = lax.rsqrt(jnp.mean(values * values, -1, keepdims=True) + EPSILON)
    return values * inverse, inverse


def middle_kernel(
    o, wo, x, routes, rows, router, down_pair,
    middle, gates, tall, down_full,
    product, arrived, ssem, rsem, lsem,
):
    at = place()
    xx, y, z, core = at
    near = sibling(at)
    greet(ctx_and_sibling(at) + [ring(at, 2, 1), ring(at, 2, 3)])
    wires = Wires(ssem, rsem)
    local = pltpu.make_async_copy(down_pair, down_full.at[:, :, z], lsem)
    local.start()
    down_task = expert_spread(down_pair, down_full, wires, at)
    next(down_task)
    full = wo[...].reshape(768, WIDTH)
    product[0] = dot(o[1 - core], full)
    swap = wires.go(product.at[0], arrived, near)
    product[1] = dot(o[core], full)
    lane = iota((ROWS, 128), 1)
    named = routes[:, 0:1] == lane
    for i in range(1, TOPK):
        named = named | (routes[:, i : i + 1] == lane)
    got([swap])
    mid = x[...].astype(F32) + product[1] + arrived[...]
    middle[...] = mid
    hidden = (normed(mid)[0] * rows[1:2]).astype(BF)
    logits = jnp.where(named, dot(hidden, router[...]), -jnp.inf)
    raised = jnp.exp(logits - jnp.max(logits, -1, keepdims=True))
    gate = raised / jnp.sum(raised, -1, keepdims=True)
    gates[...] = gate
    high = gate.astype(BF).astype(F32)
    both = high + pltpu.roll(gate - high, EXPERTS, 1)
    for part in range(2):
        cut = slice(64 * part, 64 * part + 64)
        tall[y, xx // 2, core, part, :, 0:WIDTH] = hidden[cut]
        tall[y, xx // 2, core, part, :, WIDTH:TALL] = both[cut].astype(BF)
    share = share_rows(tall, wires, at)
    next(share)
    next(share)
    next(down_task)
    finish(share, down_task)
    local.wait()
    wires.close()


def middle_call(o, wo, x, routes, rows, router, down_pair):
    return pl.pallas_call(
        middle_kernel,
        out_shape=[
            shape((ROWS, WIDTH), F32),
            shape((ROWS, 128), F32),
            shape((4, 2, 2, 2, 64, TALL)),
            shape((2, 2, 4, 64, WIDTH)),
        ],
        in_specs=[vm()] * 6 + [hbm()],
        out_specs=[vm()] * 3 + [hbm()],
        scratch_shapes=[
            pltpu.VMEM((2, ROWS, WIDTH), F32),
            pltpu.VMEM((ROWS, WIDTH), F32),
            *wire_sems(32),
            pltpu.SemaphoreType.DMA,
        ],
        compiler_params=pltpu.CompilerParams(
            collective_id=3, has_side_effects=True, vmem_limit_bytes=VMEM_BYTES
        ),
        name="middle",
    )(o.reshape(2, ROWS, 768), wo, x, routes, rows, router, down_pair)


def expert_kernel(
    tall, dy, w_gate, w_up, w_down,
    out_rows, d_rows, g_gate, g_up, g_down,
    big, wide, a_rows, y_rows, r_rows, back, wg, wu, wd, gg, gu, gd, m_s, dg_s, du_s, slot_t, sem,
):
    ctx = lax.axis_index("ctx")
    loads = [
        pltpu.make_async_copy(src, dst, sem.at[i])
        for i, (src, dst) in enumerate(
            ((tall, big), (dy, wide), (w_gate, wg), (w_up, wu), (w_down, wd))
        )
    ]
    for copy in loads:
        copy.start()
    lane = iota((128, 128), 1)
    earlier = (iota((128, 128), 1) < iota((128, 128), 0)).astype(F32).astype(BF)
    slots = iota((CAP, 128), 0).astype(F32)
    loads[0].wait()
    loads[1].wait()

    def collect(b, _):
        rows = pl.ds(pl.multiple_of(b * 128, 128), 128)
        packed = pl.ds(pl.multiple_of(b * CAP, CAP), CAP)
        both = big[rows, WIDTH:TALL].astype(F32)
        gate = both + pltpu.roll(both, 128 - EXPERTS, 1)
        hot = (gate > 0.0) & (lane < EXPERTS)
        rank = dot(earlier, hot.astype(F32).astype(BF))
        slot = jnp.where(hot, rank, -1.0)
        slot_t[...] = jnp.transpose(slot)
        picks = [
            (slot_t[pl.ds(2 * ctx + i, 1), :] == slots).astype(F32).astype(BF) for i in range(2)
        ]
        pick = jnp.concatenate(picks, 0)
        found = dot(pick, big[rows, :]).astype(BF)
        grads = dot(pick, wide[rows, :]).astype(BF)
        for i in range(2):
            a_rows[i, packed] = found[CAP * i : CAP * i + CAP]
            y_rows[i, packed] = grads[CAP * i : CAP * i + CAP]
        column = [
            jnp.sum(jnp.where(lane == 2 * ctx + i, slot, 0.0), 1, keepdims=True) for i in range(2)
        ]
        spot = lane.astype(F32)
        put = jnp.where(lane < CAP, column[0], column[1] + CAP) == spot
        back[b] = put.astype(F32).astype(BF)
        return 0

    lax.fori_loop(0, 16, collect, 0)
    for copy in loads[2:]:
        copy.wait()
    stores = []
    for e in range(2):
        number = 2 * ctx + e

        def forward(c, _):
            rows = pl.ds(pl.multiple_of(c * 384, 384), 384)
            a = a_rows[e, rows, 0:WIDTH]
            ag, au = dot(a, wg[e]), dot(a, wu[e])
            sg = jax.nn.sigmoid(ag)
            act = ag * sg
            m = (act * au).astype(BF)
            r = dot(m, wd[e]).astype(BF).astype(F32)
            lanes = iota((384, 128), 1)
            hits = (lanes == number) | (lanes == number + EXPERTS)
            gate = jnp.sum(
                jnp.where(hits, a_rows[e, rows, WIDTH:TALL].astype(F32), 0.0), 1, keepdims=True
            )
            y = y_rows[e, rows].astype(F32)
            d_gate = jnp.sum(y * r, 1, keepdims=True)
            r_rows[e, rows] = (gate * r).astype(BF)
            gr = (gate * y).astype(BF)
            y_rows[e, rows] = gr
            dm = dot_t(gr, wd[e])
            m_s[rows] = m
            dg_s[rows] = (dm * au * (sg * (1.0 + ag * (1.0 - sg)))).astype(BF)
            du_s[rows] = (dm * act).astype(BF)
            high = d_gate.astype(BF).astype(F32)
            d_both = jnp.where(
                lanes == number, high, jnp.where(lanes == number + EXPERTS, d_gate - high, 0.0)
            )
            a_rows[e, rows, WIDTH:TALL] = d_both.astype(BF)
            return 0

        lax.fori_loop(0, 2, forward, 0)
        gd[e] = t_dot(m_s[...], y_rows[e]).astype(BF)
        gg[e] = t_dot(a_rows[e, :, 0:WIDTH], dg_s[...]).astype(BF)
        gu[e] = t_dot(a_rows[e, :, 0:WIDTH], du_s[...]).astype(BF)
        for i, (src, dst) in enumerate(((gd, g_down), (gg, g_gate), (gu, g_up))):
            copy = pltpu.make_async_copy(src.at[e], dst.at[e], sem.at[5 + 3 * e + i])
            copy.start()
            stores.append(copy)

        def to_tokens(c, _):
            rows = pl.ds(pl.multiple_of(c * 384, 384), 384)
            back_rows = dot_t(dg_s[rows], wg[e]) + dot_t(du_s[rows], wu[e])
            a_rows[e, rows, 0:WIDTH] = back_rows.astype(BF)
            return 0

        lax.fori_loop(0, 2, to_tokens, 0)

    def hand_back(b, _):
        rows = pl.ds(pl.multiple_of(b * 128, 128), 128)
        packed = pl.ds(pl.multiple_of(b * CAP, CAP), CAP)
        put = back[b][:, 0 : 2 * CAP]
        big[rows, :] = dot(put, jnp.concatenate([a_rows[0, packed], a_rows[1, packed]], 0)).astype(BF)
        wide[rows, :] = dot(put, jnp.concatenate([r_rows[0, packed], r_rows[1, packed]], 0)).astype(BF)
        return 0

    lax.fori_loop(0, 16, hand_back, 0)
    for i, (src, dst) in enumerate(((big, d_rows), (wide, out_rows))):
        copy = pltpu.make_async_copy(src, dst, sem.at[i])
        copy.start()
        stores.append(copy)
    for copy in stores:
        copy.wait()


def expert_call(tall, dy, w_gate, w_up, w_down):
    slots = 16 * CAP
    return pl.pallas_call(
        expert_kernel,
        out_shape=[
            shape((LENGTH, WIDTH)),
            shape((LENGTH, TALL)),
            shape((2, WIDTH, FF)),
            shape((2, WIDTH, FF)),
            shape((2, FF, WIDTH)),
        ],
        in_specs=[hbm()] * 5,
        out_specs=[hbm()] * 5,
        scratch_shapes=[
            pltpu.VMEM((LENGTH, TALL), BF),
            pltpu.VMEM((LENGTH, WIDTH), BF),
            pltpu.VMEM((2, slots, TALL), BF),
            pltpu.VMEM((2, slots, WIDTH), BF),
            pltpu.VMEM((2, slots, WIDTH), BF),
            pltpu.VMEM((16, 128, 128), BF),
            pltpu.VMEM((2, WIDTH, FF), BF),
            pltpu.VMEM((2, WIDTH, FF), BF),
            pltpu.VMEM((2, FF, WIDTH), BF),
            pltpu.VMEM((2, WIDTH, FF), BF),
            pltpu.VMEM((2, WIDTH, FF), BF),
            pltpu.VMEM((2, FF, WIDTH), BF),
            pltpu.VMEM((slots, FF), BF),
            pltpu.VMEM((slots, FF), BF),
            pltpu.VMEM((slots, FF), BF),
            pltpu.VMEM((128, 128), F32),
            pltpu.SemaphoreType.DMA((11,)),
        ],
        compiler_params=pltpu.CompilerParams(vmem_limit_bytes=VMEM_BYTES),
        name="experts",
    )(
        tall.reshape(LENGTH, TALL), dy.reshape(LENGTH, WIDTH), w_gate.reshape(2, WIDTH, FF),
        w_up.reshape(2, WIDTH, FF), w_down.reshape(2, FF, WIDTH),
    )


def split_dot(left, right, form):
    high = left.astype(BF)
    low = (left - high.astype(F32)).astype(BF)
    return form(high, right) + form(low, right)


def norm_back(grad, gain, n, inverse):
    scaled = grad * gain
    return inverse * (scaled - n * jnp.mean(scaled * n, -1, keepdims=True))


def token_grad_kernel(
    d_rows, middle, gates, dy, rows, router, wo, ot, g_down,
    d_mid, d_o, small, g_out, down_sum,
    low, product, *rest,
):
    scratch, expert_scratch, (ssem, rsem) = rest[:8], rest[8:13], rest[13:]
    at = place()
    core = at[3]
    near = sibling(at)
    greet(ctx_and_sibling(at) + [ring(at, 2, 1), ring(at, 2, 3), partner(at)])
    wires = Wires(ssem, rsem)
    steps = sum_rows(d_rows, scratch, wires, at)
    next(steps)
    down_task = expert_sum(g_down, down_sum, expert_scratch, wires, at)
    next(down_task)
    next(steps)
    next(down_task)
    n, inverse = normed(middle[...])
    hidden = (n * rows[1:2]).astype(BF)
    parts = final(steps)
    total = jnp.concatenate(parts, 0)
    d_hidden = total[:, 0:WIDTH]
    both = total[:, WIDTH:TALL]
    gate = gates[...]
    lane = iota((ROWS, 128), 1)
    d_gate = jnp.where(lane < EXPERTS, both + pltpu.roll(both, 128 - EXPERTS, 1), 0.0)
    centre = jnp.sum(gate * d_gate, -1, keepdims=True)
    d_logits = gate * (d_gate - centre)
    d_hidden += split_dot(d_logits, router[...], dot_t)
    d_middle = norm_back(d_hidden, rows[1:2], n, inverse) + dy[...].astype(F32)
    d_low = d_middle.astype(BF)
    low[core] = d_low
    swap = wires.go(low.at[core], low.at[core], near)
    d_mid[...] = d_middle
    grads = split_dot(jnp.transpose(d_logits), hidden, dot)
    line = jnp.sum(d_hidden * n, 0, keepdims=True)
    small[...] = grads + jnp.where(iota((128, WIDTH), 0) == EXPERTS + 1, line, 0.0)
    next(down_task)
    got([swap])
    chip_rows = low[...].reshape(256, WIDTH)
    d_o[...] = dot_t(chip_rows, wo[...].reshape(768, WIDTH)).astype(BF)
    product[...] = dot(ot[...], chip_rows).astype(BF).reshape(4, 4, 3, 16, WIDTH)
    lanes = pl.ds(pl.multiple_of((1 - core) * 768, 128), 768)
    mine = pl.ds(pl.multiple_of(core * 768, 128), 768)
    swap = wires.go(product.at[:, :, :, :, lanes], g_out.at[core], near)
    for i in range(4):
        g_out[core, i] = product[i, :, :, :, mine]
    finish(down_task)
    got([swap])
    wires.close()


def token_grad_call(d_rows, middle, gates, dy, rows, router, wo, ot, g_down):
    return pl.pallas_call(
        token_grad_kernel,
        out_shape=[
            shape((ROWS, WIDTH), F32),
            shape((256, 768)),
            shape((128, WIDTH), F32),
            shape((2, 4, 4, 3, 16, 768)),
            shape((2, 64, WIDTH), F32),
        ],
        in_specs=[vm()] * 8 + [hbm()],
        out_specs=[vm()] * 5,
        scratch_shapes=[
            pltpu.VMEM((2, ROWS, WIDTH), BF),
            pltpu.VMEM((4, 4, 3, 16, WIDTH), BF),
            *sum_rows_scratch(TALL),
            *expert_sum_scratch(64, WIDTH),
            *wire_sems(24),
        ],
        compiler_params=pltpu.CompilerParams(
            collective_id=4, has_side_effects=True, vmem_limit_bytes=VMEM_BYTES
        ),
        name="token_grad",
    )(
        d_rows.reshape(4, 2, 2, 2, 64, TALL), middle, gates, dy, rows, router, wo, ot,
        g_down.reshape(2, 2, 4, 64, WIDTH),
    )


def last_kernel(
    dkv, dq, h1t, weights, unit_o, small, x, d_mid, rows, g_up, cosine, sine,
    grad_in, g_q, g_k, g_v, g_o, g_m, up_sum,
    whole, product, arrived, slots, taken, cos_v, sin_v, *rest,
):
    landings = [rest[3 * i : 3 * i + 3] for i in range(3)]
    chips, expert_scratch = rest[9:15], rest[15:20]
    ssem, rsem, lsem = rest[20:]
    at = place()
    xx, y, z, core = at
    xh, chip = xx // 2, y * 2 + xx // 2
    near = sibling(at)
    diagonal = sibling(ring(at, 0, 2))
    greet(all_peers(at) + [near, diagonal])
    wires = Wires(ssem, rsem)
    tables = [
        pltpu.make_async_copy(src.at[pl.ds(pl.multiple_of(chip * 256, 256), 256)], dst, lsem.at[i])
        for i, (src, dst) in enumerate(((cosine, cos_v), (sine, sin_v)))
    ]
    for copy in tables:
        copy.start()
    steps = sum_chips(dkv, chips, wires, at)
    next(steps)
    up_task = expert_sum(g_up, up_sum, expert_scratch, wires, at)
    next(up_task)
    n, inverse = normed(x[...].astype(F32))
    next(steps)
    next(up_task)
    parts = final(steps)
    for copy in tables:
        copy.wait()
    total = jnp.concatenate(parts, 0)
    dk = turn(total[:, 0:256], cos_v[...], -sin_v[...]).astype(BF)
    grads = jnp.concatenate([dq[...], dk, total[:, 256:512].astype(BF)], 1)
    into = weights[:, :, :, :, :, 0:COL_M].reshape(WIDTH, COL_M)
    back = dot_t(grads, into)
    product[0] = back[0:128]
    product[1] = back[128:256]
    swap = wires.go(product.at[1 - core], arrived, near)
    whole[:, :, :, :, :, 0:COL_M] = dot(h1t[...], grads).astype(BF).reshape(2, 4, 4, 3, 16, COL_M)
    whole[:, :, :, :, :, COL_END:IN_H] = jnp.zeros((2, 4, 4, 3, 16, IN_H - COL_END), BF)
    got([swap])
    d_hidden = product[core] + arrived[...]
    line = jnp.sum(d_hidden * n, 0, keepdims=True)
    tiny = small[...] + jnp.where(iota((128, WIDTH), 0) == EXPERTS, line, 0.0)
    whole[:, :, :, :, :, COL_M:COL_END] = (
        jnp.transpose(tiny).astype(BF).reshape(2, 4, 4, 3, 16, 128)
    )
    sums = gather_sums(whole, IN_Q, landings, wires, at)
    next(sums)
    grad_in[...] = d_mid[...] + norm_back(d_hidden, rows[0:1], n, inverse)
    next(up_task)
    finish(sums, up_task)
    lanes = pl.ds(pl.multiple_of(xh * IN_Q, 128), IN_Q)
    unit = jnp.concatenate([whole[xx % 2, z, y, part, :, lanes] for part in range(3)], 0)
    unit = jnp.concatenate([unit, unit_o[...].reshape(48, OUT_Q)], 1)
    slots[...] = dot(regroup_back(), unit).astype(BF).reshape(4, 16, STAGE)
    mine = core * 2 + xh
    copies = [
        wires.go(slots.at[peer[0] // 2 * 2 + peer[3]], taken.at[mine], peer)
        for peer in (near, ring(at, 0, 2), diagonal)
    ]
    taken[mine] = slots[xh * 2 + core]
    got(copies)
    tiny = jnp.zeros((12, 128), F32)
    for i in range(2):
        left, right = taken[2 * i].astype(F32)[0:12], taken[2 * i + 1].astype(F32)[0:12]
        g_q[:, 768 * i : 768 * i + 768] = left[:, 0:IN_Q]
        g_k[:, 256 * i : 256 * i + 256] = right[:, 0:256]
        g_v[:, 256 * i : 256 * i + 256] = right[:, 256:512]
        g_o[:, 768 * i : 768 * i + OUT_Q] = left[:, IN_Q:STAGE]
        g_o[:, 768 * i + OUT_Q : 768 * i + 768] = right[:, IN_Q:STAGE]
        tiny += right[:, 512:640]
    g_m[...] = tiny
    wires.close()


def last_call(dkv, dq, h1t, weights, unit_o, small, x, d_mid, rows, g_up, cosine, sine):
    return pl.pallas_call(
        last_kernel,
        out_shape=[
            shape((ROWS, WIDTH), F32),
            shape((12, WIDTH), F32),
            shape((12, 512), F32),
            shape((12, 512), F32),
            shape((12, WIDTH), F32),
            shape((12, 128), F32),
            shape((2, 192, FF), F32),
        ],
        in_specs=[vm()] * 9 + [hbm()] * 3,
        out_specs=[vm()] * 7,
        scratch_shapes=[
            pltpu.VMEM((2, 4, 4, 3, 16, IN_H), BF),
            pltpu.VMEM((2, ROWS, WIDTH), F32),
            pltpu.VMEM((ROWS, WIDTH), F32),
            pltpu.VMEM((4, 16, STAGE), BF),
            pltpu.VMEM((4, 16, STAGE), BF),
            pltpu.VMEM((256, 128), F32),
            pltpu.VMEM((256, 128), F32),
            *landing_shapes(IN_Q),
            *sum_scratch(128, 512),
            *expert_sum_scratch(192, FF),
            *wire_sems(56),
            pltpu.SemaphoreType.DMA((2,)),
        ],
        compiler_params=pltpu.CompilerParams(
            collective_id=6, has_side_effects=True, vmem_limit_bytes=VMEM_BYTES
        ),
        name="weight_grad",
    )(
        dkv.reshape(2, 4, 2, 128, 512), dq, h1t, weights, unit_o, small, x, d_mid, rows,
        g_up.reshape(2, 2, 4, 192, FF), cosine, sine,
    )


def tables():
    frequency = np.exp(
        np.arange(HEAD // 2, dtype=np.float32) * np.float32(-2.0 * math.log(10000.0) / HEAD)
    )
    angles = np.arange(LENGTH, dtype=np.float32)[:, None] * frequency[None, :]
    cosine, sine = np.cos(angles), np.sin(angles)
    return (
        np.concatenate([cosine] * 4, 1).astype(np.float32),
        np.concatenate([-sine, sine] * 2, 1).astype(np.float32),
    )


def stage_weights(w_query, key_weight, value_weight, w_out, w_router, gain_attn, gain_ffn):
    small = jnp.concatenate([w_router, gain_attn[:, None], gain_ffn[:, None]], 1)
    small = jnp.pad(small, ((0, 0), (0, IN_H - COL_M - EXPERTS - 2)))
    quarters = []
    for i in range(2):
        own_out = w_out[:, 768 * i : 768 * i + 768]
        quarters.append([w_query[:, 768 * i : 768 * i + 768], own_out[:, :OUT_Q]])
        quarters.append(
            [
                key_weight[:, 256 * i : 256 * i + 256],
                value_weight[:, 256 * i : 256 * i + 256],
                small,
                own_out[:, OUT_Q:],
            ]
        )
    stage = jnp.stack([jnp.concatenate(quarter, 1) for quarter in quarters])
    return jnp.pad(stage, ((0, 0), (0, 4), (0, 0)))


def body(
    block_in, routes, cotangent, gain_attn, w_query, key_weight, value_weight, w_out,
    gain_ffn, w_router, w_gate, w_up, w_down,
):
    cosine, sine = (jnp.asarray(table) for table in tables())
    x, dy = block_in[0], cotangent[0]
    stage = stage_weights(
        w_query, key_weight, value_weight, w_out, w_router, gain_attn, gain_ffn
    )
    weights, rows, router, q, kv, h1t, unit_o, gate_full, up_pair, down_pair = first_call(
        stage, x, cosine, sine, w_gate, w_up, w_down
    )
    kv = kv.reshape(LENGTH, 512)
    o, ot, lse, wo, all_dy, up_full = attend_call(q, kv, unit_o, dy.reshape(2, 64, WIDTH), up_pair)
    middle, gates, tall, down_full = middle_call(o, wo, x, routes[0], rows, router, down_pair)
    out_rows, d_rows, g_gate, g_up, g_down = expert_call(tall, all_dy, gate_full, up_full, down_full)
    d_mid, d_o, small, g_out, g_down = token_grad_call(
        d_rows, middle, gates, dy, rows, router, wo, ot, g_down
    )
    dq, dkv, block_out, unit_o, g_gate = attend_back_call(
        q, kv, d_o, lse, out_rows, middle, g_out, g_gate, cosine, sine
    )
    grad_in, g_q, g_k, g_v, g_o, g_m, g_up = last_call(
        dkv, dq, h1t, weights, unit_o, small, x, d_mid, rows, g_up, cosine, sine
    )
    return (
        block_out[None],
        grad_in[None],
        g_m[:, EXPERTS],
        g_q,
        g_k,
        g_v,
        g_o,
        g_m[:, EXPERTS + 1],
        g_m[:, 0:EXPERTS],
        g_gate,
        g_up,
        g_down,
    )


def solution(mesh):
    tokens, owned, experts = P("seq", "ctx", None), P(("seq", "ctx"), None), P("ctx", "seq", None)
    vector = P(("seq", "ctx"))
    return jax.shard_map(
        body,
        mesh=mesh,
        in_specs=(
            tokens, tokens, tokens, vector, owned, owned, owned, owned, vector, owned,
            experts, experts, experts,
        ),
        out_specs=(
            tokens, tokens, vector, owned, owned, owned, owned, vector, owned,
            experts, experts, experts,
        ),
        check_vma=False,
    )
```

time: 602 us -> 475 us (0.79)
  Pallas kernels: 561 us -> 445 us
  between operations: 14.8 us -> 1.19 us
  local copies, waits for them, and re-layouts: 9.36 us -> 20 us
    pallas_call x3 -> x1, Pallas kernels: 234 us -> 83.3 us  [first_call(): pl.pallas_call(first_kernel, out_shape=[shape((2, 4, 4, 3, 16, IN_H)), sh...]
    pallas_call x1, Pallas kernels: 143 us -> 76.3 us  [last_call(): pl.pallas_call(last_kernel, out_shape=[shape((ROWS, WIDTH), F32), shape((...]
    pallas_call x1, Pallas kernels: 5.77 us -> 66.3 us  [attend_call(): pl.pallas_call(attend_kernel, out_shape=[shape((256, 768)), shape((768, 2...]
    pallas_call x1, Pallas kernels: 7.82 us -> 61.1 us  [attend_back_call(): pl.pallas_call(attend_back_kernel, out_shape=[shape((256, 768)), shape((2...]
    pallas_call x1, Pallas kernels: 62.6 us -> 50 us  [middle_call(): pl.pallas_call(middle_kernel, out_shape=[shape((ROWS, WIDTH), F32), shape...]
    unnamed x32 -> x19, local copies, waits for them, and re-layouts: 6.21 us -> 14 us
  transfers between devices with their start and end apart: 6 -> 0, of which waited for: 0 -> 0; matrix products, arithmetic and copies ran while one was open for 2% -> 0% of each run, Pallas kernels for 86% -> 0%
where the time goes in v2:
time: 475 us; the launch traced here: 468 us
  Pallas kernels  445 us (94%)
  local copies, waits for them, and re-layouts  20 us (4%)
    pallas_call x1, Pallas kernels, first_call(): pl.pallas_call(first_kernel, out_shape=[shape((2, 4, 4, 3, 16, IN_H)), sh...  83.3 us
    pallas_call x1, Pallas kernels, last_call(): pl.pallas_call(last_kernel, out_shape=[shape((ROWS, WIDTH), F32), shape((...  76.3 us
    pallas_call x1, Pallas kernels, attend_call(): pl.pallas_call(attend_kernel, out_shape=[shape((256, 768)), shape((768, 2...  66.3 us
    pallas_call x1, Pallas kernels, attend_back_call(): pl.pallas_call(attend_back_kernel, out_shape=[shape((256, 768)), shape((2...  61.1 us
    pallas_call x1, Pallas kernels, token_grad_call(): pl.pallas_call(token_grad_kernel, out_shape=[shape((ROWS, WIDTH), F32), s...  57.1 us
    pallas_call x1, Pallas kernels, expert_call(): pl.pallas_call(expert_kernel, out_shape=[shape((LENGTH, WIDTH)), shape((L...  50.9 us
    pallas_call x1, Pallas kernels, middle_call(): pl.pallas_call(middle_kernel, out_shape=[shape((ROWS, WIDTH), F32), shape...  50 us
    unnamed x19, local copies, waits for them, and re-layouts  14 us

profile of v2, /device:TPU:1, one launch (start us, length us, event | category | flops | bytes accessed | tf_op | source)
XLA Modules:
  0.0 467.6 jit_solution(12151165773776797853)
XLA Ops:
  0.6 0.7 copy.30
  1.4 0.8 copy.31
  2.1 0.8 fusion.15
  2.9 0.7 fusion.18
  3.6 0.7 fusion.19
  4.4 0.8 fusion.17
  5.1 0.8 fusion.16
  5.9 0.7 fusion.6.stage
  6.6 1.4 copy.32
  8.0 83.3 %weights_qkv.1 = (bf16[2,4,4,3,16,1536]{5,4,3,2,1,0:T(8,128)(2,1)}, f32[8,1536]{1,0:T(8,128)}, bf16[1536,128]{1,0:T(8,128)(2,1)}, bf16[256,768]{1,0:T(8,128)(2,1...) custom-call(bf16[4,16,1152]{2,1,0:T(8,128)(2,1)} %fusion.6.stage, ...), custom_call_target="tpu_custom_call" | custom-call | tf_op jit(solution)/shard_map/weights_qkv/pallas_call | solution.py:359
  91.3 66.3 %attend.1 = (bf16[256,768]{1,0:T(8,128)(2,1)}, bf16[768,256]{1,0:T(8,128)(2,1)}, f32[4,8,768]{2,1,0:T(8,128)}, bf16[4,4,3,16,1536]{4,3,2,1,0:T(8,128)(2,1)}, bf1...) custom-call(bf16[256,768]{1,0:T(8,128)(2,1)} %get-tuple-element.54.q, ...), custom_call_target="tpu_custom_call" | custom-call | tf_op jit(solution)/shard_map/attend/pallas_call | solution.py:646
  157.6 50.0 %middle.1 = (f32[128,1536]{1,0:T(8,128)}, f32[128,128]{1,0:T(8,128)}, bf16[4,2,2,2,64,1664]{5,4,3,2,1,0:T(8,128)(2,1)}, bf16[2,2,4,64,1536]{4,3,2,1,0:T(8,128)(2,1)}) custom-call(bf16[2,128,768]{2,1,0:T(8,128)(2,1)} %bitcast.49, bf16[4,4,3,16,1536]{4,3,2,1,0:T(8,128)(2,1)} %get-tuple-element.59.wo, bf16[128,1536]{1,0:T(8,128)(2,1)} %bitcast.37, ...), custom_call_target="tpu_custom_call" | custom-call | tf_op jit(solution)/shard_map/middle/pallas_call | solution.py:871
  207.6 50.9 %experts.1 = (bf16[2048,1536]{1,0:T(8,128)(2,1)}, bf16[2048,1664]{1,0:T(8,128)(2,1)}, bf16[2,1536,512]{2,1,0:T(8,128)(2,1)}, bf16[2,1536,512]{2,1,0:T(8,128)(2,1)}, bf16[2,512,1536]{2,1,0:T(8,128)(2,1)}) custom-call(bf16[2048,1664]{1,0:T(8,128)(2,1)} %bitcast.33, bf16[2048,1536]{1,0:T(8,128)(2,1)} %bitcast.35, bf16[2,1536,512]{2,1,0:T(8,128)(2,1)} %bitcast.41, ...), custom_call_target="tpu_custom_call" | custom-call | tf_op jit(solution)/shard_map/experts/pallas_call | solution.py:1012
  258.5 57.1 %token_grad.1 = (f32[128,1536]{1,0:T(8,128)}, bf16[256,768]{1,0:T(8,128)(2,1)}, f32[128,1536]{1,0:T(8,128)}, bf16[2,4,4,3,16,768]{5,4,3,2,1,0:T(8,128)(2,1)}, f32[2,64,1536]{2,1,0:T(8,128)}) custom-call(bf16[4,2,2,2,64,1664]{5,4,3,2,1,0:T(8,128)(2,1)} %bitcast.32, f32[128,1536]{1,0:T(8,128)} %get-tuple-element.69.middle, ...), custom_call_target="tpu_custom_call" | custom-call | tf_op jit(solution)/shard_map/token_grad/pallas_call | solution.py:1114
  315.6 61.1 %attend_back.1 = (bf16[256,768]{1,0:T(8,128)(2,1)}, bf16[2,8,128,512]{3,2,1,0:T(8,128)(2,1)}, bf16[128,1536]{1,0:T(8,128)(2,1)}, bf16[3,16,384]{2,1,0:T(8,128)(2,1)}, f32[2,192,512]{2,1,0:T(8,128)}) custom-call(bf16[256,768]{1,0:T(8,128)(2,1)} %get-tuple-element.54.q, bf16[2048,512]{1,0:T(8,128)(2,1)} %bitcast.31, bf16[256,768]{1,0:T(8,128)(2,1)} %get-tuple-element.73.d_o, ...), custom_call_target="tpu_custom_call" | custom-call | tf_op jit(solution)/shard_map/attend_back/pallas_call | solution.py:780
  376.7 0.0 copy-start.3
  376.7 76.3 %weight_grad.1 = (f32[128,1536]{1,0:T(8,128)}, f32[12,1536]{1,0:T(8,128)}, f32[12,512]{1,0:T(8,128)}, f32[12,512]{1,0:T(8,128)}, f32[12,1536]{1,0:T(8,128)}, /*index=5*/f32[12,128]{1,0:T(8,128)}, f32[2,192,512]{2,1,0:T(8,128)}) custom-call(bf16[2,4,2,128,512]{4,3,2,1,0:T(8,128)(2,1)} %bitcast.45, bf16[256,768]{1,0:T(8,128)(2,1)} %get-tuple-element.80.dq, ...), custom_call_target="tpu_custom_call" | custom-call | tf_op jit(solution)/shard_map/weight_grad/pallas_call | solution.py:1220
  453.0 0.0 copy-start.1
  453.0 0.0 copy-start.2
  453.0 0.0 copy-start
  453.0 1.6 slice_reduce_fusion
  454.6 0.0 copy-done.3
  454.6 0.7 copy.43
  455.3 2.1 copy.44
  457.4 1.5 copy.45
  458.9 1.4 copy.46
  460.3 1.4 copy.47
  461.7 1.5 copy.48
  463.2 1.3 copy.49
  464.5 0.0 copy-done.1
  464.5 0.9 copy.50
  465.4 0.0 copy-done.2
  465.4 0.9 copy.51
  466.3 0.0 copy-done
  466.3 0.9 copy.52
  (2 shorter events, 0.0 us)
Async XLA Ops:
  376.7 77.9 %copy-start.3 = (bf16[128,1536]{1,0:T(8,128)(2,1)S(1)}, bf16[128,1536]{1,0:T(8,128)(2,1)}, u32[]{:S(2)}) copy-start(bf16[128,1536]{1,0:T(8,128)(2,1)} %get-tuple-element.78) | copy-start | bytes 1179652
  453.0 11.5 %copy-start.1 = (f32[2,192,512]{2,1,0:T(8,128)S(1)}, f32[2,192,512]{2,1,0:T(8,128)}, u32[]{:S(2)}) copy-start(f32[2,192,512]{2,1,0:T(8,128)} %get-tuple-element.132) | copy-start | bytes 2359300
  453.0 12.4 %copy-start.2 = (f32[2,192,512]{2,1,0:T(8,128)S(1)}, f32[2,192,512]{2,1,0:T(8,128)}, u32[]{:S(2)}) copy-start(f32[2,192,512]{2,1,0:T(8,128)} %get-tuple-element.133) | copy-start | bytes 2359300
  453.0 13.3 %copy-start = (f32[2,64,1536]{2,1,0:T(8,128)S(1)}, f32[2,64,1536]{2,1,0:T(8,128)}, u32[]{:S(2)}) copy-start(f32[2,64,1536]{2,1,0:T(8,128)} %get-tuple-element.134) | copy-start | bytes 2359300

commit v3 on v2

--- a/solution.py
+++ b/solution.py
@@ -192,17 +192,19 @@
     return (at[0] + 1 - 2 * (at[0] % 2), at[1], at[2], at[3])
 
 
-def expert_pairs(shard, pair, wires, at):
-    spot = pair.at[:, at[0] % 2]
-    return wires.go(shard, spot, partner(at))
-
-
-def expert_spread(own, full, wires, at):
-    z = at[2]
+def expert_spread(shard, full, wires, at, sem):
+    x, _, z, _ = at
     left, right = ring(at, 2, 3), ring(at, 2, 1)
+    spot = full.at[:, x % 2, z]
+    local = pltpu.make_async_copy(shard, spot, sem)
+    local.start()
+    pair = wires.go(shard, spot, partner(at))
+    yield
+    local.wait()
+    got([pair])
     spot = full.at[:, :, z]
-    a = wires.go(own, spot, right)
-    b = wires.go(own, spot, left)
+    a = wires.go(spot, spot, right)
+    b = wires.go(spot, spot, left)
     yield
     got([a])
     spot = full.at[0, :, (z + 3) % 4]
@@ -271,149 +273,52 @@
     return [ring(at, d, s) for d in range(3) for s in (1, 2, 3)]
 
 
-def first_kernel(
-    stage, x, cosine, sine, w_gate, w_up, w_down,
-    weights, rows, router, q, kv, h1t, unit_o, gate_full, up_pair, down_pair,
-    both, slots, cos_v, sin_v, ssem, rsem, lsem,
-):
-    at = place()
-    xx, y, z, core = at
-    xh, chip = xx // 2, y * 2 + xx // 2
-    diagonal = sibling(ring(at, 0, 2))
-    greet(all_peers(at) + [sibling(at), diagonal])
-    wires = Wires(ssem, rsem)
-    local = [
-        (cosine.at[pl.ds(pl.multiple_of(chip * 256, 256), 256)], cos_v),
-        (sine.at[pl.ds(pl.multiple_of(chip * 256, 256), 256)], sin_v),
-        (w_gate, gate_full.at[:, xx % 2, z]),
-        (w_up, up_pair.at[:, xx % 2]),
-        (w_down, down_pair.at[:, xx % 2]),
-    ]
-    local = [pltpu.make_async_copy(src, dst, lsem.at[i]) for i, (src, dst) in enumerate(local)]
-    for copy in local:
-        copy.start()
-    mine = core * 2 + xh
-    first = [
-        wires.go(stage.at[peer[3] * 2 + peer[0] // 2], slots.at[mine], peer)
-        for peer in (sibling(at), ring(at, 0, 2), diagonal)
-    ]
-    tokens = wires.go(x, both.at[core], sibling(at))
-    slots[mine] = stage[mine]
-    both[core] = x[...]
-    got(first)
-    unit = dot(regroup(), slots[...].reshape(64, STAGE)).astype(BF)
-    lanes = pl.ds(pl.multiple_of(xh * IN_Q, 128), IN_Q)
-    for part in range(3):
-        weights[xx % 2, z, y, part, :, lanes] = unit[16 * part : 16 * part + 16, 0:IN_Q]
-        unit_o[part] = unit[16 * part : 16 * part + 16, IN_Q:STAGE]
-    task = spread(weights, IN_Q, wires, at)
-    next(task)
-    spot = gate_full.at[:, xx % 2, z]
-    pair = wires.go(w_gate, spot, partner(at))
-    finish(task)
-    for copy in local:
-        copy.wait()
-    got([pair])
-    gate = expert_spread(gate_full.at[:, :, z], gate_full, wires, at)
-    next(gate)
-    pairs = [
-        expert_pairs(w_up, up_pair, wires, at),
-        expert_pairs(w_down, down_pair, wires, at),
-    ]
-
-    small = weights[:, :, :, :, :, COL_M:COL_END].reshape(WIDTH, 128)
-    router[...] = small
-    turned = jnp.transpose(small.astype(F32))
-    rows[...] = turned[32:40]
-    got([tokens])
-    values = both[...].reshape(256, WIDTH).astype(F32)
-    inverse = lax.rsqrt(jnp.mean(values * values, -1, keepdims=True) + EPSILON)
-    hidden = (values * inverse * turned[32:33]).astype(BF)
-    made = dot(hidden, weights[:, :, :, :, :, 0:COL_M].reshape(WIDTH, COL_M))
-    cos, sin = cos_v[...], sin_v[...]
-    key = turn(made[:, COL_K:COL_V], cos, sin).astype(BF)
-    value = made[:, COL_V:COL_M].astype(BF)
-    for part in range(2):
-        kv[y, xh, part, :, 0:256] = key[128 * part : 128 * part + 128]
-        kv[y, xh, part, :, 256:512] = value[128 * part : 128 * part + 128]
-    own = [kv.at[y, xh, 0], kv.at[y, xh, 1]]
-    a = [wires.go(own[0], own[0], ring(at, 1, s)) for s in (1, 2, 3)]
-    b = [wires.go(own[1], own[1], ring(at, 0, 2))]
-    q[...] = turn(made[:, 0:COL_K], cos, sin).astype(BF)
-    got(a)
-    column = kv.at[:, xh, 0]
-    a = [wires.go(column, column, ring(at, 0, 2))]
-    got(b)
-    pair = kv.at[y, :, 1]
-    b = [wires.go(pair, pair, ring(at, 1, s)) for s in (1, 2, 3)]
-    h1t[...] = jnp.transpose(hidden.astype(F32)).astype(BF)
-    next(gate)
-    got(a)
-    got(b)
-    finish(gate)
-    got(pairs)
-    wires.close()
-
-
-def first_call(stage, x, cosine, sine, w_gate, w_up, w_down):
-    return pl.pallas_call(
-        first_kernel,
-        out_shape=[
-            shape((2, 4, 4, 3, 16, IN_H)),
-            shape((8, WIDTH), F32),
-            shape((WIDTH, 128)),
-            shape((256, 768)),
-            shape((4, 2, 2, 128, 512)),
-            shape((WIDTH, 256)),
-            shape((3, 16, OUT_Q)),
-            shape((2, 2, 4, 192, FF)),
-            shape((2, 2, 192, FF)),
-            shape((2, 2, 64, WIDTH)),
-        ],
-        in_specs=[vm(), vm()] + [hbm()] * 5,
-        out_specs=[vm()] * 7 + [hbm()] * 3,
-        scratch_shapes=[
-            pltpu.VMEM((2, 128, WIDTH), BF),
-            pltpu.VMEM((4, 16, STAGE), BF),
-            pltpu.VMEM((256, 128), F32),
-            pltpu.VMEM((256, 128), F32),
-            *wire_sems(56),
-            pltpu.SemaphoreType.DMA((5,)),
-        ],
-        compiler_params=pltpu.CompilerParams(
-            collective_id=1, has_side_effects=True, vmem_limit_bytes=VMEM_BYTES
-        ),
-        name="weights_qkv",
-    )(stage, x, cosine, sine, w_gate, w_up, w_down)
+def share(spot, wires, at, inner=True):
+    x, y, _, _ = at
+    xh = x // 2
+    near, far, up, down = sibling(at), ring(at, 0, 2), ring(at, 1, 1), ring(at, 1, 3)
+    above, below, across = (y + 1) % 4, (y + 3) % 4, (y + 2) % 4
+    kept = []
+
+    def send(where, peer):
+        return wires.go(spot(*where), spot(*where), peer)
+
+    def pass_on(*where):
+        if inner:
+            kept.append(send(where, near))
+
+    a, b = send((y, xh), up), send((y, xh), down)
+    c = send((y, xh), far)
+    pass_on(y, xh)
+    yield
+    got([a])
+    a1 = send((below, xh, 0), up)
+    got([b])
+    b1 = send((above, xh, 1), down)
+    pass_on(below, xh)
+    pass_on(above, xh)
+    got([c])
+    a2, b2 = send((y, 1 - xh), up), send((y, 1 - xh), down)
+    pass_on(y, 1 - xh)
+    yield
+    got([a1, b1])
+    pass_on(across, xh)
+    got([a2])
+    a3 = send((below, 1 - xh, 0), up)
+    got([b2])
+    b3 = send((above, 1 - xh, 1), down)
+    pass_on(below, 1 - xh)
+    pass_on(above, 1 - xh)
+    yield
+    got([a3, b3])
+    pass_on(across, 1 - xh)
+    yield
+    got(kept)
 
 
 def share_rows(ref, wires, at):
-    x, y, _, core = at
-    xh = x // 2
-    near, far = sibling(at), ring(at, 0, 2)
-
-    def pass_on(spot, peer):
-        return wires.go(spot, spot, peer)
-
-    inner = [pass_on(ref.at[y, xh, core], near)]
-    a = [pass_on(ref.at[y, xh, core, 0], ring(at, 1, s)) for s in (1, 2, 3)]
-    b = [pass_on(ref.at[y, xh, core, 1], far)]
-    yield
-    got(b)
-    b = [pass_on(ref.at[y, :, core, 1], ring(at, 1, s)) for s in (1, 2, 3)]
-    got(a)
-    a = [pass_on(ref.at[:, xh, core, 0], far)]
-    inner.append(pass_on(ref.at[y, 1 - xh, core, 1], near))
-    for s in (1, 2, 3):
-        inner.append(pass_on(ref.at[(y + s) % 4, xh, core, 0], near))
-    yield
-    got(a)
-    inner.append(pass_on(ref.at[:, 1 - xh, core, 0], near))
-    got(b)
-    for s in (1, 2, 3):
-        inner.append(pass_on(ref.at[(y + s) % 4, :, core, 1], near))
-    yield
-    got(inner)
+    core = at[3]
+    return share(lambda y, xh, *half: ref.at[(y, xh, core, *half)], wires, at)
 
 
 def ctx_and_sibling(at):
@@ -537,57 +442,17 @@
     return found
 
 
-def attend_kernel(
-    q, kv, unit_o, dy, up_pair,
-    o, ot, lse, wo, all_dy, up_full,
-    scores, vt, qt, qz, out_t, columns, ssem, rsem, lsem,
-):
-    at = place()
-    x, y, z, core = at
-    chip = y * 2 + x // 2
-    near = sibling(at)
-    greet(all_peers(at) + [near])
-    wires = Wires(ssem, rsem)
-    local = [
-        pltpu.make_async_copy(dy, all_dy.at[y, x // 2, core], lsem.at[0]),
-        pltpu.make_async_copy(up_pair, up_full.at[:, :, z], lsem.at[1]),
-    ]
-    for copy in local:
-        copy.start()
-    lanes = pl.ds(pl.multiple_of(x // 2 * OUT_Q, 128), OUT_Q)
-    for part in range(3):
-        columns[x % 2, z, y, part, :, lanes] = unit_o[part]
-    out_task = spread(columns, OUT_Q, wires, at)
-    up_task = expert_spread(up_pair, up_full, wires, at)
-    dy_task = share_rows(all_dy, wires, at)
-    next(out_task)
-    next(up_task)
-    local[0].wait()
-    next(dy_task)
-    mine = pl.ds(pl.multiple_of(core * 768, 128), 768)
-
-    def swap_out():
-        finish(out_task)
-        swap.append(
-            wires.go(columns.at[1 - core], wo.at[:, :, :, :, mine], near)
-        )
-        for i in range(4):
-            wo[i, :, :, :, mine] = columns[core, i]
-
-    swap = []
-    beside = [
-        lambda: next(out_task),
-        lambda: next(dy_task),
-        lambda: next(out_task),
-        lambda: next(up_task),
-        swap_out,
-        lambda: next(dy_task),
-        lambda: finish(up_task),
-        lambda: None,
-    ]
+def normed(values):
+    inverse = lax.rsqrt(jnp.mean(values * values, -1, keepdims=True) + EPSILON)
+    return values * inverse, inverse
+
+
+def attend(q, kv, o, ot, lse, scratch, chip, beside):
+    scores, vt, qt, qz, out_t = scratch
     qt[...] = jnp.transpose(q[...].astype(F32) * 0.125).astype(BF)
     for kb in range(8):
-        vt[kb] = jnp.transpose(kv[256 * kb : 256 * kb + 256, 256:512].astype(F32)).astype(BF)
+        block = kv[kb // 2, kb % 2, :, :, 256:512].reshape(256, 256)
+        vt[kb] = jnp.transpose(block.astype(F32)).astype(BF)
     allowed = iota((256, 768), 0) <= iota((256, 768), 1) % 256
     for j in range(4):
         u, half = j // 2, j % 2
@@ -598,7 +463,8 @@
 
         def score(kb):
             rows = pl.ds(pl.multiple_of(kb * 256, 256), 256)
-            return rows, dot(kv[rows, 128 * u : 128 * u + 128], qz[...])
+            keys = kv[kb // 2, kb % 2, :, :, 128 * u : 128 * u + 128].reshape(256, 128)
+            return rows, dot(keys, qz[...])
 
         def top(kb, most):
             rows, s = score(kb)
@@ -635,207 +501,125 @@
             out_t[64 * h : 64 * h + 64] = acc[:, 256 * g : 256 * g + 256]
         beside[2 * j + 1]()
     ot[...] = out_t[...].astype(BF)
-    o[...] = jnp.transpose(out_t[...]).astype(BF)
-    finish(dy_task)
-    got(swap)
-    local[1].wait()
-    wires.close()
-
-
-def attend_call(q, kv, unit_o, dy, up_pair):
-    return pl.pallas_call(
-        attend_kernel,
-        out_shape=[
-            shape((256, 768)),
-            shape((768, 256)),
-            shape((4, 8, 768), F32),
-            shape((4, 4, 3, 16, WIDTH)),
-            shape((4, 2, 2, 2, 64, WIDTH)),
-            shape((2, 2, 4, 192, FF)),
-        ],
-        in_specs=[vm()] * 3 + [hbm()] * 2,
-        out_specs=[vm()] * 4 + [hbm()] * 2,
-        scratch_shapes=[
-            pltpu.VMEM((LENGTH, 768), F32),
-            pltpu.VMEM((8, 256, 256), BF),
-            pltpu.VMEM((768, 256), BF),
-            pltpu.VMEM((128, 768), BF),
-            pltpu.VMEM((768, 256), F32),
-            pltpu.VMEM((2, 4, 4, 3, 16, OUT_H), BF),
-            *wire_sems(56),
-            pltpu.SemaphoreType.DMA((2,)),
-        ],
-        compiler_params=pltpu.CompilerParams(
-            collective_id=2, has_side_effects=True, vmem_limit_bytes=VMEM_BYTES
-        ),
-        name="attend",
-    )(q, kv, unit_o, dy, up_pair)
-
-
-def attend_back_kernel(
-    q, kv, d_o, lse, out_rows, middle, g_out, g_gate, cosine, sine,
-    dq, dkv, block_out, unit_o, gate_sum,
-    probs, grads, kt, qt, dot_, qz, oz, acc, dqt, cos_v, sin_v, columns, *rest,
-):
-    row_scratch, landings = rest[:8], [rest[8 + 3 * i : 11 + 3 * i] for i in range(3)]
-    expert_scratch = rest[17:22]
-    ssem, rsem, lsem = rest[22:]
-    at = place()
-    xx, y, z, _ = at
-    chip = y * 2 + xx // 2
-    greet(all_peers(at) + [sibling(at)])
-    wires = Wires(ssem, rsem)
-    columns_in = pltpu.make_async_copy(g_out, columns, lsem.at[2])
-    columns_in.start()
-    tables = [
-        pltpu.make_async_copy(src.at[pl.ds(pl.multiple_of(chip * 256, 256), 256)], dst, lsem.at[i])
-        for i, (src, dst) in enumerate(((cosine, cos_v), (sine, sin_v)))
-    ]
-    for copy in tables:
-        copy.start()
-    row_task = sum_rows(out_rows, row_scratch, wires, at)
-    gate_task = expert_sum(g_gate, gate_sum, expert_scratch, wires, at)
-    out_task = gather_sums(columns, OUT_Q, landings, wires, at)
-    next(row_task)
-    next(gate_task)
-
-    def start_out():
-        columns_in.wait()
-        next(out_task)
-
-    beside = [
-        lambda: next(row_task),
-        lambda: next(gate_task),
-        start_out,
-        lambda: next(gate_task),
-        lambda: next(row_task),
-        lambda: next(out_task),
-        lambda: finish(gate_task),
-        lambda: next(out_task),
-    ]
-    qt[...] = jnp.transpose(q[...].astype(F32) * 0.125).astype(BF)
-    dot_[...] = jnp.transpose(d_o[...].astype(F32)).astype(BF)
-    for kb in range(8):
-        kt[kb] = jnp.transpose(kv[256 * kb : 256 * kb + 256, 0:256].astype(F32)).astype(BF)
-    acc[...] = jnp.zeros_like(acc)
-    allowed = iota((256, 768), 0) <= iota((256, 768), 1) % 256
-    for j in range(4):
-        u, half = j // 2, j % 2
-        qz[...] = jnp.zeros_like(qz)
-        oz[...] = jnp.zeros_like(oz)
-        for g in range(3):
-            h = 3 * j + g
-            qz[64 * half : 64 * half + 64, 256 * g : 256 * g + 256] = qt[64 * h : 64 * h + 64]
-            oz[64 * half : 64 * half + 64, 256 * g : 256 * g + 256] = dot_[64 * h : 64 * h + 64]
-        level = lse[j, 0:1]
-
-        def share(kb, centre, masked):
-            rows = pl.ds(pl.multiple_of(kb * 256, 256), 256)
-            p = jnp.exp(dot(kv[rows, 128 * u : 128 * u + 128], qz[...]) - level)
-            if masked:
-                p = jnp.where(allowed, p, 0.0)
-            probs[rows] = p
-            dp = dot(kv[rows, 256 + 128 * u : 384 + 128 * u], oz[...])
-            grads[rows] = dp
-            acc[rows, 256 + 128 * u : 384 + 128 * u] += dot_t(p.astype(BF), oz[...])
-            return centre + jnp.sum((p * dp).reshape(32, 8, 768), 0)
-
-        centre = lax.fori_loop(
-            0, chip, functools.partial(share, masked=False), jnp.zeros((8, 768), F32)
-        )
-        centre = share(chip, centre, True)
-        centre = jnp.sum(centre, 0, keepdims=True)
-        beside[2 * j]()
-
-        def back(kb, total):
-            rows = pl.ds(pl.multiple_of(kb * 256, 256), 256)
-            ds = (probs[rows] * (grads[rows] - centre)).astype(BF)
-            acc[rows, 128 * u : 128 * u + 128] += dot_t(ds, qz[...])
-            return total + dot(kt[kb, 64 * j : 64 * j + 64], ds)
-
-        total = lax.fori_loop(0, chip + 1, back, jnp.zeros((64, 768), F32))
-        for g in range(3):
-            h = 3 * j + g
-            dqt[64 * h : 64 * h + 64] = total[:, 256 * g : 256 * g + 256] * 0.125
-        beside[2 * j + 1]()
-    for kb in range(8):
-        for part in range(2):
-            at_row = 256 * kb + 128 * part
-            dkv[part, kb] = acc[at_row : at_row + 128].astype(BF)
-    for copy in tables:
-        copy.wait()
-    dq[...] = turn(jnp.transpose(dqt[...]), cos_v[...], -sin_v[...]).astype(BF)
-    parts = final(row_task)
-    for part in range(2):
-        cut = slice(64 * part, 64 * part + 64)
-        block_out[cut] = (middle[cut] + parts[part]).astype(BF)
-    finish(out_task)
-    lanes = pl.ds(pl.multiple_of(xx // 2 * OUT_Q, 128), OUT_Q)
-    for part in range(3):
-        unit_o[part] = columns[xx % 2, z, y, part, :, lanes]
-    wires.close()
-
-
-def attend_back_call(q, kv, d_o, lse, out_rows, middle, g_out, g_gate, cosine, sine):
-    return pl.pallas_call(
-        attend_back_kernel,
-        out_shape=[
-            shape((256, 768)),
-            shape((2, 8, 128, 512)),
-            shape((ROWS, WIDTH)),
-            shape((3, 16, OUT_Q)),
-            shape((2, 192, FF), F32),
-        ],
-        in_specs=[vm()] * 6 + [hbm()] * 4,
-        out_specs=[vm()] * 5,
-        scratch_shapes=[
-            pltpu.VMEM((LENGTH, 768), F32),
-            pltpu.VMEM((LENGTH, 768), F32),
-            pltpu.VMEM((8, 256, 256), BF),
-            pltpu.VMEM((768, 256), BF),
-            pltpu.VMEM((768, 256), BF),
-            pltpu.VMEM((128, 768), BF),
-            pltpu.VMEM((128, 768), BF),
-            pltpu.VMEM((LENGTH, 512), F32),
-            pltpu.VMEM((768, 256), F32),
-            pltpu.VMEM((256, 128), F32),
-            pltpu.VMEM((256, 128), F32),
-            pltpu.VMEM((2, 4, 4, 3, 16, OUT_H), BF),
-            *sum_rows_scratch(WIDTH),
-            *landing_shapes(OUT_Q),
-            *expert_sum_scratch(192, FF),
-            *wire_sems(56),
-            pltpu.SemaphoreType.DMA((3,)),
-        ],
-        compiler_params=pltpu.CompilerParams(
-            collective_id=5, has_side_effects=True, vmem_limit_bytes=VMEM_BYTES
-        ),
-        name="attend_back",
-    )(
-        q, kv, d_o, lse, out_rows.reshape(4, 2, 2, 2, 64, WIDTH), middle, g_out,
-        g_gate.reshape(2, 2, 4, 192, FF), cosine, sine,
-    )
-
-
-def normed(values):
-    inverse = lax.rsqrt(jnp.mean(values * values, -1, keepdims=True) + EPSILON)
-    return values * inverse, inverse
-
-
-def middle_kernel(
-    o, wo, x, routes, rows, router, down_pair,
-    middle, gates, tall, down_full,
-    product, arrived, ssem, rsem, lsem,
+    out = jnp.transpose(out_t[...]).astype(BF)
+    o[0], o[1] = out[0:128], out[128:256]
+
+
+def forward_kernel(
+    stage, x, routes, cosine, sine, dy, w_gate, w_up, w_down,
+    rows, router, q, h1t, ot, lse, middle, gates,
+    weights_out, wo_out, kv_out, tall, all_dy, gate_full, up_full, down_full,
+    weights, columns, wo, kv, both, slots, cos_v, sin_v, o, tall_own, product, arrived,
+    scores, vt, qt, qz, out_t, ssem, rsem, lsem,
 ):
     at = place()
     xx, y, z, core = at
+    xh, chip = xx // 2, y * 2 + xx // 2
     near = sibling(at)
-    greet(ctx_and_sibling(at) + [ring(at, 2, 1), ring(at, 2, 3)])
+    diagonal = sibling(ring(at, 0, 2))
+    greet(all_peers(at) + [near, diagonal])
     wires = Wires(ssem, rsem)
-    local = pltpu.make_async_copy(down_pair, down_full.at[:, :, z], lsem)
-    local.start()
-    down_task = expert_spread(down_pair, down_full, wires, at)
+
+    def local(n, src, dst):
+        copy = pltpu.make_async_copy(src, dst, lsem.at[n])
+        copy.start()
+        return copy
+
+    angle = pl.ds(pl.multiple_of(chip * 256, 256), 256)
+    angles = [local(0, cosine.at[angle], cos_v), local(1, sine.at[angle], sin_v)]
+    dy_in = local(2, dy, all_dy.at[y, xh, core])
+    mine = core * 2 + xh
+    first = [
+        wires.go(stage.at[peer[3] * 2 + peer[0] // 2], slots.at[mine], peer)
+        for peer in (near, ring(at, 0, 2), diagonal)
+    ]
+    tokens = wires.go(x, both.at[core], near)
+    slots[mine] = stage[mine]
+    both[core] = x[...]
+    got(first)
+    unit = dot(regroup(), slots[...].reshape(64, STAGE)).astype(BF)
+    in_lanes = pl.ds(pl.multiple_of(xh * IN_Q, 128), IN_Q)
+    out_lanes = pl.ds(pl.multiple_of(xh * OUT_Q, 128), OUT_Q)
+    for part in range(3):
+        weights[xx % 2, z, y, part, :, in_lanes] = unit[16 * part : 16 * part + 16, 0:IN_Q]
+        columns[xx % 2, z, y, part, :, out_lanes] = unit[16 * part : 16 * part + 16, IN_Q:STAGE]
+    in_task = spread(weights, IN_Q, wires, at)
+    out_task = spread(columns, OUT_Q, wires, at)
+    dy_task = share_rows(all_dy, wires, at)
+    gate_task = expert_spread(w_gate, gate_full, wires, at, lsem.at[3])
+    up_task = expert_spread(w_up, up_full, wires, at, lsem.at[4])
+    down_task = expert_spread(w_down, down_full, wires, at, lsem.at[5])
+    next(in_task)
+    next(in_task)
+    next(gate_task)
+    next(in_task)
+    finish(in_task)
+    weights_kept = local(6, weights, weights_out)
+    next(gate_task)
+    next(up_task)
+    dy_in.wait()
+    next(dy_task)
+
+    small = weights[:, :, :, :, :, COL_M:COL_END].reshape(WIDTH, 128)
+    router[...] = small
+    turned = jnp.transpose(small.astype(F32))
+    rows[...] = turned[32:40]
+    got([tokens])
+    values = both[...].reshape(256, WIDTH).astype(F32)
+    hidden = (normed(values)[0] * turned[32:33]).astype(BF)
+    made = dot(hidden, weights[:, :, :, :, :, 0:COL_M].reshape(WIDTH, COL_M))
+    for copy in angles:
+        copy.wait()
+    cos, sin = cos_v[...], sin_v[...]
+    key = turn(made[:, COL_K:COL_V], cos, sin).astype(BF)
+    value = made[:, COL_V:COL_M].astype(BF)
+    for part in range(2):
+        kv[y, xh, part, :, 0:256] = key[128 * part : 128 * part + 128]
+        kv[y, xh, part, :, 256:512] = value[128 * part : 128 * part + 128]
+    own = [kv.at[y, xh, 0], kv.at[y, xh, 1]]
+    a = [wires.go(own[0], own[0], ring(at, 1, s)) for s in (1, 2, 3)]
+    b = [wires.go(own[1], own[1], ring(at, 0, 2))]
+    q[...] = turn(made[:, 0:COL_K], cos, sin).astype(BF)
+    got(b)
+    pair = kv.at[y, :, 1]
+    b = [wires.go(pair, pair, ring(at, 1, s)) for s in (1, 2, 3)]
+    got(a)
+    column = kv.at[:, xh, 0]
+    a = [wires.go(column, column, ring(at, 0, 2))]
+    next(out_task)
+    h1t[...] = jnp.transpose(hidden.astype(F32)).astype(BF)
+    next(up_task)
     next(down_task)
+    next(out_task)
+    got(a)
+    got(b)
+    kv_kept = local(7, kv, kv_out)
+    next(gate_task)
+    next(dy_task)
+
+    half = pl.ds(pl.multiple_of(core * 768, 128), 768)
+    swap = []
+
+    def swap_out():
+        finish(out_task)
+        swap.append(wires.go(columns.at[1 - core], wo.at[:, :, :, :, half], near))
+        for i in range(4):
+            wo[i, :, :, :, half] = columns[core, i]
+
+    beside = [
+        lambda: next(out_task),
+        lambda: next(down_task),
+        lambda: next(dy_task),
+        lambda: next(up_task),
+        swap_out,
+        lambda: next(dy_task),
+        lambda: None,
+        lambda: None,
+    ]
+    attend(q, kv, o, ot, lse, (scores, vt, qt, qz, out_t), chip, beside)
+    got(swap)
+    wo_kept = local(8, wo, wo_out)
+
     full = wo[...].reshape(768, WIDTH)
     product[0] = dot(o[1 - core], full)
     swap = wires.go(product.at[0], arrived, near)
@@ -853,42 +637,74 @@
     gate = raised / jnp.sum(raised, -1, keepdims=True)
     gates[...] = gate
     high = gate.astype(BF).astype(F32)
-    both = high + pltpu.roll(gate - high, EXPERTS, 1)
+    two = high + pltpu.roll(gate - high, EXPERTS, 1)
     for part in range(2):
         cut = slice(64 * part, 64 * part + 64)
-        tall[y, xx // 2, core, part, :, 0:WIDTH] = hidden[cut]
-        tall[y, xx // 2, core, part, :, WIDTH:TALL] = both[cut].astype(BF)
-    share = share_rows(tall, wires, at)
-    next(share)
-    next(share)
+        tall_own[part, :, 0:WIDTH] = hidden[cut]
+        tall_own[part, :, WIDTH:TALL] = two[cut].astype(BF)
+    tall_in = local(9, tall_own, tall.at[y, xh, core])
+    tall_task = share_rows(tall, wires, at)
+    tall_in.wait()
+    next(tall_task)
     next(down_task)
-    finish(share, down_task)
-    local.wait()
+    next(tall_task)
+    next(tall_task)
+    finish(dy_task, gate_task, up_task)
+    finish(tall_task, down_task)
+    for copy in (weights_kept, kv_kept, wo_kept):
+        copy.wait()
     wires.close()
 
 
-def middle_call(o, wo, x, routes, rows, router, down_pair):
+def forward_call(stage, x, routes, cosine, sine, dy, w_gate, w_up, w_down):
     return pl.pallas_call(
-        middle_kernel,
+        forward_kernel,
         out_shape=[
+            shape((8, WIDTH), F32),
+            shape((WIDTH, 128)),
+            shape((256, 768)),
+            shape((WIDTH, 256)),
+            shape((768, 256)),
+            shape((4, 8, 768), F32),
             shape((ROWS, WIDTH), F32),
             shape((ROWS, 128), F32),
+            shape((2, 4, 4, 3, 16, IN_H)),
+            shape((4, 4, 3, 16, WIDTH)),
+            shape((4, 2, 2, 128, 512)),
             shape((4, 2, 2, 2, 64, TALL)),
+            shape((4, 2, 2, 2, 64, WIDTH)),
+            shape((2, 2, 4, 192, FF)),
+            shape((2, 2, 4, 192, FF)),
             shape((2, 2, 4, 64, WIDTH)),
         ],
-        in_specs=[vm()] * 6 + [hbm()],
-        out_specs=[vm()] * 3 + [hbm()],
+        in_specs=[vm()] * 3 + [hbm()] * 2 + [vm()] * 4,
+        out_specs=[vm()] * 8 + [hbm()] * 8,
         scratch_shapes=[
+            pltpu.VMEM((2, 4, 4, 3, 16, IN_H), BF),
+            pltpu.VMEM((2, 4, 4, 3, 16, OUT_H), BF),
+            pltpu.VMEM((4, 4, 3, 16, WIDTH), BF),
+            pltpu.VMEM((4, 2, 2, 128, 512), BF),
+            pltpu.VMEM((2, 128, WIDTH), BF),
+            pltpu.VMEM((4, 16, STAGE), BF),
+            pltpu.VMEM((256, 128), F32),
+            pltpu.VMEM((256, 128), F32),
+            pltpu.VMEM((2, 128, 768), BF),
+            pltpu.VMEM((2, 64, TALL), BF),
             pltpu.VMEM((2, ROWS, WIDTH), F32),
             pltpu.VMEM((ROWS, WIDTH), F32),
-            *wire_sems(32),
-            pltpu.SemaphoreType.DMA,
+            pltpu.VMEM((LENGTH, 768), F32),
+            pltpu.VMEM((8, 256, 256), BF),
+            pltpu.VMEM((768, 256), BF),
+            pltpu.VMEM((128, 768), BF),
+            pltpu.VMEM((768, 256), F32),
+            *wire_sems(144),
+            pltpu.SemaphoreType.DMA((10,)),
         ],
         compiler_params=pltpu.CompilerParams(
-            collective_id=3, has_side_effects=True, vmem_limit_bytes=VMEM_BYTES
+            collective_id=1, has_side_effects=True, vmem_limit_bytes=VMEM_BYTES
         ),
-        name="middle",
-    )(o.reshape(2, ROWS, 768), wo, x, routes, rows, router, down_pair)
+        name="forward",
+    )(stage, x, routes, cosine, sine, dy, w_gate, w_up, w_down)
 
 
 def expert_kernel(
@@ -1139,6 +955,151 @@
     )
 
 
+def attend_back_kernel(
+    q, kv, d_o, lse, out_rows, middle, g_out, g_gate, cosine, sine,
+    dq, dkv, block_out, unit_o, gate_sum,
+    probs, grads, kt, qt, dot_, qz, oz, acc, dqt, cos_v, sin_v, columns, *rest,
+):
+    row_scratch, landings = rest[:8], [rest[8 + 3 * i : 11 + 3 * i] for i in range(3)]
+    expert_scratch = rest[17:22]
+    ssem, rsem, lsem = rest[22:]
+    at = place()
+    xx, y, z, _ = at
+    chip = y * 2 + xx // 2
+    greet(all_peers(at) + [sibling(at)])
+    wires = Wires(ssem, rsem)
+    columns_in = pltpu.make_async_copy(g_out, columns, lsem.at[2])
+    columns_in.start()
+    tables = [
+        pltpu.make_async_copy(src.at[pl.ds(pl.multiple_of(chip * 256, 256), 256)], dst, lsem.at[i])
+        for i, (src, dst) in enumerate(((cosine, cos_v), (sine, sin_v)))
+    ]
+    for copy in tables:
+        copy.start()
+    row_task = sum_rows(out_rows, row_scratch, wires, at)
+    gate_task = expert_sum(g_gate, gate_sum, expert_scratch, wires, at)
+    out_task = gather_sums(columns, OUT_Q, landings, wires, at)
+    next(row_task)
+    next(gate_task)
+
+    def start_out():
+        columns_in.wait()
+        next(out_task)
+
+    beside = [
+        lambda: next(row_task),
+        lambda: next(gate_task),
+        start_out,
+        lambda: next(gate_task),
+        lambda: next(row_task),
+        lambda: next(out_task),
+        lambda: finish(gate_task),
+        lambda: next(out_task),
+    ]
+    qt[...] = jnp.transpose(q[...].astype(F32) * 0.125).astype(BF)
+    dot_[...] = jnp.transpose(d_o[...].astype(F32)).astype(BF)
+    for kb in range(8):
+        kt[kb] = jnp.transpose(kv[256 * kb : 256 * kb + 256, 0:256].astype(F32)).astype(BF)
+    acc[...] = jnp.zeros_like(acc)
+    allowed = iota((256, 768), 0) <= iota((256, 768), 1) % 256
+    for j in range(4):
+        u, half = j // 2, j % 2
+        qz[...] = jnp.zeros_like(qz)
+        oz[...] = jnp.zeros_like(oz)
+        for g in range(3):
+            h = 3 * j + g
+            qz[64 * half : 64 * half + 64, 256 * g : 256 * g + 256] = qt[64 * h : 64 * h + 64]
+            oz[64 * half : 64 * half + 64, 256 * g : 256 * g + 256] = dot_[64 * h : 64 * h + 64]
+        level = lse[j, 0:1]
+
+        def share(kb, centre, masked):
+            rows = pl.ds(pl.multiple_of(kb * 256, 256), 256)
+            p = jnp.exp(dot(kv[rows, 128 * u : 128 * u + 128], qz[...]) - level)
+            if masked:
+                p = jnp.where(allowed, p, 0.0)
+            probs[rows] = p
+            dp = dot(kv[rows, 256 + 128 * u : 384 + 128 * u], oz[...])
+            grads[rows] = dp
+            acc[rows, 256 + 128 * u : 384 + 128 * u] += dot_t(p.astype(BF), oz[...])
+            return centre + jnp.sum((p * dp).reshape(32, 8, 768), 0)
+
+        centre = lax.fori_loop(
+            0, chip, functools.partial(share, masked=False), jnp.zeros((8, 768), F32)
+        )
+        centre = share(chip, centre, True)
+        centre = jnp.sum(centre, 0, keepdims=True)
+        beside[2 * j]()
+
+        def back(kb, total):
+            rows = pl.ds(pl.multiple_of(kb * 256, 256), 256)
+            ds = (probs[rows] * (grads[rows] - centre)).astype(BF)
+            acc[rows, 128 * u : 128 * u + 128] += dot_t(ds, qz[...])
+            return total + dot(kt[kb, 64 * j : 64 * j + 64], ds)
+
+        total = lax.fori_loop(0, chip + 1, back, jnp.zeros((64, 768), F32))
+        for g in range(3):
+            h = 3 * j + g
+            dqt[64 * h : 64 * h + 64] = total[:, 256 * g : 256 * g + 256] * 0.125
+        beside[2 * j + 1]()
+    for kb in range(8):
+        for part in range(2):
+            at_row = 256 * kb + 128 * part
+            dkv[part, kb] = acc[at_row : at_row + 128].astype(BF)
+    for copy in tables:
+        copy.wait()
+    dq[...] = turn(jnp.transpose(dqt[...]), cos_v[...], -sin_v[...]).astype(BF)
+    parts = final(row_task)
+    for part in range(2):
+        cut = slice(64 * part, 64 * part + 64)
+        block_out[cut] = (middle[cut] + parts[part]).astype(BF)
+    finish(out_task)
+    lanes = pl.ds(pl.multiple_of(xx // 2 * OUT_Q, 128), OUT_Q)
+    for part in range(3):
+        unit_o[part] = columns[xx % 2, z, y, part, :, lanes]
+    wires.close()
+
+
+def attend_back_call(q, kv, d_o, lse, out_rows, middle, g_out, g_gate, cosine, sine):
+    return pl.pallas_call(
+        attend_back_kernel,
+        out_shape=[
+            shape((256, 768)),
+            shape((2, 8, 128, 512)),
+            shape((ROWS, WIDTH)),
+            shape((3, 16, OUT_Q)),
+            shape((2, 192, FF), F32),
+        ],
+        in_specs=[vm()] * 6 + [hbm()] * 4,
+        out_specs=[vm()] * 5,
+        scratch_shapes=[
+            pltpu.VMEM((LENGTH, 768), F32),
+            pltpu.VMEM((LENGTH, 768), F32),
+            pltpu.VMEM((8, 256, 256), BF),
+            pltpu.VMEM((768, 256), BF),
+            pltpu.VMEM((768, 256), BF),
+            pltpu.VMEM((128, 768), BF),
+            pltpu.VMEM((128, 768), BF),
+            pltpu.VMEM((LENGTH, 512), F32),
+            pltpu.VMEM((768, 256), F32),
+            pltpu.VMEM((256, 128), F32),
+            pltpu.VMEM((256, 128), F32),
+            pltpu.VMEM((2, 4, 4, 3, 16, OUT_H), BF),
+            *sum_rows_scratch(WIDTH),
+            *landing_shapes(OUT_Q),
+            *expert_sum_scratch(192, FF),
+            *wire_sems(56),
+            pltpu.SemaphoreType.DMA((3,)),
+        ],
+        compiler_params=pltpu.CompilerParams(
+            collective_id=5, has_side_effects=True, vmem_limit_bytes=VMEM_BYTES
+        ),
+        name="attend_back",
+    )(
+        q, kv, d_o, lse, out_rows.reshape(4, 2, 2, 2, 64, WIDTH), middle, g_out,
+        g_gate.reshape(2, 2, 4, 192, FF), cosine, sine,
+    )
+
+
 def last_kernel(
     dkv, dq, h1t, weights, unit_o, small, x, d_mid, rows, g_up, cosine, sine,
     grad_in, g_q, g_k, g_v, g_o, g_m, up_sum,
@@ -1294,12 +1255,13 @@
     stage = stage_weights(
         w_query, key_weight, value_weight, w_out, w_router, gain_attn, gain_ffn
     )
-    weights, rows, router, q, kv, h1t, unit_o, gate_full, up_pair, down_pair = first_call(
-        stage, x, cosine, sine, w_gate, w_up, w_down
+    (
+        rows, router, q, h1t, ot, lse, middle, gates,
+        weights, wo, kv, tall, all_dy, gate_full, up_full, down_full,
+    ) = forward_call(
+        stage, x, routes[0], cosine, sine, dy.reshape(2, 64, WIDTH), w_gate, w_up, w_down
     )
     kv = kv.reshape(LENGTH, 512)
-    o, ot, lse, wo, all_dy, up_full = attend_call(q, kv, unit_o, dy.reshape(2, 64, WIDTH), up_pair)
-    middle, gates, tall, down_full = middle_call(o, wo, x, routes[0], rows, router, down_pair)
     out_rows, d_rows, g_gate, g_up, g_down = expert_call(tall, all_dy, gate_full, up_full, down_full)
     d_mid, d_o, small, g_out, g_down = token_grad_call(
         d_rows, middle, gates, dy, rows, router, wo, ot, g_down

time: 475 us -> 436 us (0.918)
  Pallas kernels: 445 us -> 406 us
    pallas_call x3 -> x1, Pallas kernels: 200 us -> 160 us  [forward_call(): pl.pallas_call(forward_kernel, out_shape=[shape((8, WIDTH), F32), shape((...]
where the time goes in v3:
time: 436 us; the launch traced here: 429 us
  Pallas kernels  406 us (93%)
  local copies, waits for them, and re-layouts  20 us (5%)
    pallas_call x1, Pallas kernels, forward_call(): pl.pallas_call(forward_kernel, out_shape=[shape((8, WIDTH), F32), shape((...  160 us
    pallas_call x1, Pallas kernels, last_call(): pl.pallas_call(last_kernel, out_shape=[shape((ROWS, WIDTH), F32), shape((...  76.6 us
    pallas_call x1, Pallas kernels, attend_back_call(): pl.pallas_call(attend_back_kernel, out_shape=[shape((256, 768)), shape((2...  61.1 us
    pallas_call x1, Pallas kernels, token_grad_call(): pl.pallas_call(token_grad_kernel, out_shape=[shape((ROWS, WIDTH), F32), s...  57.5 us
    pallas_call x1, Pallas kernels, expert_call(): pl.pallas_call(expert_kernel, out_shape=[shape((LENGTH, WIDTH)), shape((L...  51 us
    unnamed x19, local copies, waits for them, and re-layouts  14 us

profile of v3, /device:TPU:1, one launch (start us, length us, event | category | flops | bytes accessed | tf_op | source)
XLA Modules:
  0.0 429.1 jit_solution(15327766179204179138)
XLA Ops:
  0.6 0.7 copy.30
  1.4 0.8 copy.31
  2.1 0.8 fusion.15
  2.9 0.7 fusion.18
  3.6 0.7 fusion.19
  4.4 0.8 fusion.17
  5.1 0.8 fusion.16
  5.9 0.7 fusion.6.stage
  6.6 1.4 copy.32
  8.0 160.1 %forward.1 = (f32[8,1536]{1,0:T(8,128)}, bf16[1536,128]{1,0:T(8,128)(2,1)}, bf16[256,768]{1,0:T(8,128)(2,1)}, bf16[1536,256]{1,0:T(8,128)(2,1)}, bf16[768,256]{1...) custom-call(bf16[4,16,1152]{2,1,0:T(8,128)(2,1)} %fusion.6.stage, ...), custom_call_target="tpu_custom_call" | custom-call | tf_op jit(solution)/shard_map/forward/pallas_call | solution.py:660
  168.1 51.0 %experts.1 = (bf16[2048,1536]{1,0:T(8,128)(2,1)}, bf16[2048,1664]{1,0:T(8,128)(2,1)}, bf16[2,1536,512]{2,1,0:T(8,128)(2,1)}, bf16[2,1536,512]{2,1,0:T(8,128)(2,1)}, bf16[2,512,1536]{2,1,0:T(8,128)(2,1)}) custom-call(bf16[2048,1664]{1,0:T(8,128)(2,1)} %bitcast.30, bf16[2048,1536]{1,0:T(8,128)(2,1)} %bitcast.32, bf16[2,1536,512]{2,1,0:T(8,128)(2,1)} %bitcast.36, ...), custom_call_target="tpu_custom_call" | custom-call | tf_op jit(solution)/shard_map/experts/pallas_call | solution.py:828
  219.2 57.5 %token_grad.1 = (f32[128,1536]{1,0:T(8,128)}, bf16[256,768]{1,0:T(8,128)(2,1)}, f32[128,1536]{1,0:T(8,128)}, bf16[2,4,4,3,16,768]{5,4,3,2,1,0:T(8,128)(2,1)}, f32[2,64,1536]{2,1,0:T(8,128)}) custom-call(bf16[4,2,2,2,64,1664]{5,4,3,2,1,0:T(8,128)(2,1)} %bitcast.29, f32[128,1536]{1,0:T(8,128)} %get-tuple-element.58.middle, ...), custom_call_target="tpu_custom_call" | custom-call | tf_op jit(solution)/shard_map/token_grad/pallas_call | solution.py:930
  276.7 61.1 %attend_back.1 = (bf16[256,768]{1,0:T(8,128)(2,1)}, bf16[2,8,128,512]{3,2,1,0:T(8,128)(2,1)}, bf16[128,1536]{1,0:T(8,128)(2,1)}, bf16[3,16,384]{2,1,0:T(8,128)(2,1)}, f32[2,192,512]{2,1,0:T(8,128)}) custom-call(bf16[256,768]{1,0:T(8,128)(2,1)} %get-tuple-element.50.q, bf16[2048,512]{1,0:T(8,128)(2,1)} %bitcast.39, bf16[256,768]{1,0:T(8,128)(2,1)} %get-tuple-element.65.d_o, ...), custom_call_target="tpu_custom_call" | custom-call | tf_op jit(solution)/shard_map/attend_back/pallas_call | solution.py:1063
  337.8 0.0 copy-start.3
  337.9 76.6 %weight_grad.1 = (f32[128,1536]{1,0:T(8,128)}, f32[12,1536]{1,0:T(8,128)}, f32[12,512]{1,0:T(8,128)}, f32[12,512]{1,0:T(8,128)}, f32[12,1536]{1,0:T(8,128)}, /*index=5*/f32[12,128]{1,0:T(8,128)}, f32[2,192,512]{2,1,0:T(8,128)}) custom-call(bf16[2,4,2,128,512]{4,3,2,1,0:T(8,128)(2,1)} %bitcast.40, bf16[256,768]{1,0:T(8,128)(2,1)} %get-tuple-element.72.dq, ...), custom_call_target="tpu_custom_call" | custom-call | tf_op jit(solution)/shard_map/weight_grad/pallas_call | solution.py:1181
  414.5 0.0 copy-start.1
  414.5 0.0 copy-start.2
  414.5 0.0 copy-start
  414.5 1.6 slice_reduce_fusion
  416.1 0.0 copy-done.3
  416.1 0.7 copy.43
  416.8 2.1 copy.44
  418.9 1.5 copy.45
  420.4 1.4 copy.46
  421.8 1.4 copy.47
  423.2 1.5 copy.48
  424.7 1.3 copy.49
  426.0 0.0 copy-done.1
  426.0 0.9 copy.50
  426.9 0.0 copy-done.2
  426.9 0.9 copy.51
  427.8 0.0 copy-done
  427.8 0.9 copy.52
  (2 shorter events, 0.0 us)
Async XLA Ops:
  337.8 78.2 %copy-start.3 = (bf16[128,1536]{1,0:T(8,128)(2,1)S(1)}, bf16[128,1536]{1,0:T(8,128)(2,1)}, u32[]{:S(2)}) copy-start(bf16[128,1536]{1,0:T(8,128)(2,1)} %get-tuple-element.70) | copy-start | bytes 1179652
  414.5 11.5 %copy-start.1 = (f32[2,192,512]{2,1,0:T(8,128)S(1)}, f32[2,192,512]{2,1,0:T(8,128)}, u32[]{:S(2)}) copy-start(f32[2,192,512]{2,1,0:T(8,128)} %get-tuple-element.124) | copy-start | bytes 2359300
  414.5 12.4 %copy-start.2 = (f32[2,192,512]{2,1,0:T(8,128)S(1)}, f32[2,192,512]{2,1,0:T(8,128)}, u32[]{:S(2)}) copy-start(f32[2,192,512]{2,1,0:T(8,128)} %get-tuple-element.125) | copy-start | bytes 2359300
  414.5 13.3 %copy-start = (f32[2,64,1536]{2,1,0:T(8,128)S(1)}, f32[2,64,1536]{2,1,0:T(8,128)}, u32[]{:S(2)}) copy-start(f32[2,64,1536]{2,1,0:T(8,128)} %get-tuple-element.126) | copy-start | bytes 2359300

commit v4 on v3

--- a/solution.py
+++ b/solution.py
@@ -218,7 +218,8 @@
 
 def expert_sum_scratch(rows, columns):
     return [
-        pltpu.VMEM((3, 2, 2, rows, columns), BF),
+        pltpu.VMEM((2, 2, rows, columns), BF),
+        pltpu.VMEM((2, 2, rows, columns), BF),
         pltpu.VMEM((2, 2, rows, columns), BF),
         pltpu.VMEM((2, 2, 2, rows, columns), BF),
         pltpu.VMEM((2, rows, columns), BF),
@@ -227,42 +228,51 @@
 
 
 def expert_sum(grads, result, scratch, wires, at):
-    own, halves, pairs, last, lsem = scratch
+    passing, own, halves, pairs, last, lsem = scratch
     z, x_lo = at[2], at[0] % 2
-    left, right = ring(at, 2, 3), ring(at, 2, 1)
+    up, down = ring(at, 2, 1), ring(at, 2, 3)
+    above, below, across = (z + 1) % 4, (z + 3) % 4, (z + 2) % 4
     loads = [
-        pltpu.make_async_copy(grads.at[:, :, (z + step) % 4], own.at[i], lsem.at[i])
-        for i, step in enumerate((0, 1, 3))
+        pltpu.make_async_copy(src, dst, lsem.at[i])
+        for i, (src, dst) in enumerate(
+            (
+                (grads.at[0, :, above], passing.at[0]),
+                (grads.at[1, :, below], passing.at[1]),
+                (grads.at[:, :, z], own),
+            )
+        )
     ]
     for copy in loads:
         copy.start()
-    a = wires.go(grads.at[0, :, (z + 2) % 4], halves.at[0], right)
-    b = wires.go(grads.at[1, :, (z + 2) % 4], halves.at[1], left)
+    a = wires.go(grads.at[0, :, across], halves.at[0], up)
+    b = wires.go(grads.at[1, :, across], halves.at[1], down)
+    direct = [
+        wires.go(grads.at[1, :, above], pairs.at[0, 1], up),
+        wires.go(grads.at[0, :, below], pairs.at[1, 0], down),
+    ]
     yield
     for copy in loads:
         copy.wait()
     got([a])
     for i in range(2):
-        own[1, 0, i] = (own[1, 0, i].astype(F32) + halves[0, i].astype(F32)).astype(BF)
-    a = wires.go(own.at[1], pairs.at[0], right)
+        passing[0, i] = (passing[0, i].astype(F32) + halves[0, i].astype(F32)).astype(BF)
+    a = wires.go(passing.at[0], pairs.at[0, 0], up)
     got([b])
     for i in range(2):
-        own[2, 1, i] = (own[2, 1, i].astype(F32) + halves[1, i].astype(F32)).astype(BF)
-    b = wires.go(own.at[2], pairs.at[1], left)
+        passing[1, i] = (passing[1, i].astype(F32) + halves[1, i].astype(F32)).astype(BF)
+    b = wires.go(passing.at[1], pairs.at[1, 1], down)
     yield
-    got([a, b])
+    got([*direct, a, b])
     for e in range(2):
         for i in range(2):
-            own[0, e, i] = (
-                own[0, e, i].astype(F32)
-                + pairs[0, e, i].astype(F32)
-                + pairs[1, e, i].astype(F32)
+            own[e, i] = (
+                own[e, i].astype(F32) + pairs[0, e, i].astype(F32) + pairs[1, e, i].astype(F32)
             ).astype(BF)
-    a = wires.go(own.at[0, :, 1 - x_lo], last, partner(at))
+    a = wires.go(own.at[:, 1 - x_lo], last, partner(at))
     yield
     got([a])
     for e in range(2):
-        result[e] = own[0, e, x_lo].astype(F32) + last[e].astype(F32)
+        result[e] = own[e, x_lo].astype(F32) + last[e].astype(F32)
 
 
 def ctx_peers(at):
@@ -321,6 +331,35 @@
     return share(lambda y, xh, *half: ref.at[(y, xh, core, *half)], wires, at)
 
 
+def share_rows_two(ref, wires, at):
+    x, y, _, core = at
+    xh = x // 2
+    near, far = sibling(at), ring(at, 0, 2)
+
+    def pass_on(spot, peer):
+        return wires.go(spot, spot, peer)
+
+    inner = [pass_on(ref.at[y, xh, core], near)]
+    a = [pass_on(ref.at[y, xh, core, 0], ring(at, 1, s)) for s in (1, 2, 3)]
+    b = [pass_on(ref.at[y, xh, core, 1], far)]
+    yield
+    got(b)
+    b = [pass_on(ref.at[y, :, core, 1], ring(at, 1, s)) for s in (1, 2, 3)]
+    got(a)
+    a = [pass_on(ref.at[:, xh, core, 0], far)]
+    inner.append(pass_on(ref.at[y, 1 - xh, core, 1], near))
+    for s in (1, 2, 3):
+        inner.append(pass_on(ref.at[(y + s) % 4, xh, core, 0], near))
+    yield
+    got(a)
+    inner.append(pass_on(ref.at[:, 1 - xh, core, 0], near))
+    got(b)
+    for s in (1, 2, 3):
+        inner.append(pass_on(ref.at[(y + s) % 4, :, core, 1], near))
+    yield
+    got(inner)
+
+
 def ctx_and_sibling(at):
     return ctx_peers(at) + [sibling(at)]
 
@@ -341,18 +380,18 @@
     x, y, _, _ = at
     xh = x // 2
     far = ring(at, 0, 2)
-    a = [wires.go(source.at[0, :, 1 - xh], e0, far)]
+    a = [wires.go(source.at[:, 1 - xh, 0], e0, far)]
     b = [
-        wires.go(source.at[1, (y + s) % 4], e1.at[s - 1], ring(at, 1, s)) for s in (1, 2, 3)
+        wires.go(source.at[(y + s) % 4, :, 1], e1.at[s - 1], ring(at, 1, s)) for s in (1, 2, 3)
     ]
     yield None
     got(a)
     for i in range(4):
-        t0[i] = (source[0, i, xh].astype(F32) + e0[i].astype(F32)).astype(BF)
+        t0[i] = (source[i, xh, 0].astype(F32) + e0[i].astype(F32)).astype(BF)
     a = [wires.go(t0.at[(y + s) % 4], f0.at[s - 1], ring(at, 1, s)) for s in (1, 2, 3)]
     got(b)
     for i in range(2):
-        total = source[1, y, i].astype(F32)
+        total = source[y, i, 1].astype(F32)
         for s in range(3):
             total += e1[s, i].astype(F32)
         t1[i] = total.astype(BF)
@@ -368,27 +407,35 @@
 
 def sum_rows_scratch(columns):
     return [
-        pltpu.VMEM((2, 4, 2, 64, columns), BF),
-        pltpu.VMEM((2, 4, 2, 64, columns), BF),
+        pltpu.VMEM((4, 2, 2, 64, columns), BF),
+        pltpu.VMEM((4, 2, 2, 64, columns), BF),
         *sum_scratch(64, columns),
+        pltpu.SemaphoreType.DMA((2,)),
     ]
 
 
 def sum_rows(rows, scratch, wires, at):
-    landed, own, rest = scratch[0], scratch[1], scratch[2:]
+    landed, own, lsem = scratch[0], scratch[1], scratch[-1]
     core = at[3]
     copies = [
-        wires.go(rows.at[:, :, 1 - core, part], landed.at[part], sibling(at)) for part in range(2)
+        wires.go(rows.at[:, :, 1 - core, part], landed.at[:, :, part], sibling(at)) for part in range(2)
     ]
+    loads = [
+        pltpu.make_async_copy(rows.at[:, :, core, part], own.at[:, :, part], lsem.at[part])
+        for part in range(2)
+    ]
+    for copy in loads:
+        copy.start()
     yield None
     for part in range(2):
+        loads[part].wait()
         got([copies[part]])
         for i in range(4):
             for h in range(2):
-                own[part, i, h] = (
-                    rows[i, h, core, part].astype(F32) + landed[part, i, h].astype(F32)
+                own[i, h, part] = (
+                    own[i, h, part].astype(F32) + landed[i, h, part].astype(F32)
                 ).astype(BF)
-    for result in sum_chips(own, rest, wires, at):
+    for result in sum_chips(own, scratch[2:-1], wires, at):
         yield result
 
 
@@ -545,7 +592,7 @@
         columns[xx % 2, z, y, part, :, out_lanes] = unit[16 * part : 16 * part + 16, IN_Q:STAGE]
     in_task = spread(weights, IN_Q, wires, at)
     out_task = spread(columns, OUT_Q, wires, at)
-    dy_task = share_rows(all_dy, wires, at)
+    dy_task = share_rows_two(all_dy, wires, at)
     gate_task = expert_spread(w_gate, gate_full, wires, at, lsem.at[3])
     up_task = expert_spread(w_up, up_full, wires, at, lsem.at[4])
     down_task = expert_spread(w_down, down_full, wires, at, lsem.at[5])
@@ -595,7 +642,6 @@
     got(b)
     kv_kept = local(7, kv, kv_out)
     next(gate_task)
-    next(dy_task)
 
     half = pl.ds(pl.multiple_of(core * 768, 128), 768)
     swap = []
@@ -612,7 +658,7 @@
         lambda: next(dy_task),
         lambda: next(up_task),
         swap_out,
-        lambda: next(dy_task),
+        lambda: None,
         lambda: None,
         lambda: None,
     ]
@@ -647,6 +693,7 @@
     tall_in.wait()
     next(tall_task)
     next(down_task)
+    next(dy_task)
     next(tall_task)
     next(tall_task)
     finish(dy_task, gate_task, up_task)
@@ -879,7 +926,7 @@
     d_mid, d_o, small, g_out, down_sum,
     low, product, *rest,
 ):
-    scratch, expert_scratch, (ssem, rsem) = rest[:8], rest[8:13], rest[13:]
+    scratch, expert_scratch, (ssem, rsem) = rest[:9], rest[9:15], rest[15:]
     at = place()
     core = at[3]
     near = sibling(at)
@@ -910,7 +957,7 @@
     d_mid[...] = d_middle
     grads = split_dot(jnp.transpose(d_logits), hidden, dot)
     line = jnp.sum(d_hidden * n, 0, keepdims=True)
-    small[...] = grads + jnp.where(iota((128, WIDTH), 0) == EXPERTS + 1, line, 0.0)
+    small[...] = (grads + jnp.where(iota((128, WIDTH), 0) == EXPERTS + 1, line, 0.0))[0:40]
     next(down_task)
     got([swap])
     chip_rows = low[...].reshape(256, WIDTH)
@@ -932,11 +979,11 @@
         out_shape=[
             shape((ROWS, WIDTH), F32),
             shape((256, 768)),
-            shape((128, WIDTH), F32),
+            shape((40, WIDTH), F32),
             shape((2, 4, 4, 3, 16, 768)),
             shape((2, 64, WIDTH), F32),
         ],
-        in_specs=[vm()] * 8 + [hbm()],
+        in_specs=[hbm()] + [vm()] * 7 + [hbm()],
         out_specs=[vm()] * 5,
         scratch_shapes=[
             pltpu.VMEM((2, ROWS, WIDTH), BF),
@@ -955,55 +1002,19 @@
     )
 
 
-def attend_back_kernel(
-    q, kv, d_o, lse, out_rows, middle, g_out, g_gate, cosine, sine,
-    dq, dkv, block_out, unit_o, gate_sum,
-    probs, grads, kt, qt, dot_, qz, oz, acc, dqt, cos_v, sin_v, columns, *rest,
-):
-    row_scratch, landings = rest[:8], [rest[8 + 3 * i : 11 + 3 * i] for i in range(3)]
-    expert_scratch = rest[17:22]
-    ssem, rsem, lsem = rest[22:]
-    at = place()
-    xx, y, z, _ = at
-    chip = y * 2 + xx // 2
-    greet(all_peers(at) + [sibling(at)])
-    wires = Wires(ssem, rsem)
-    columns_in = pltpu.make_async_copy(g_out, columns, lsem.at[2])
-    columns_in.start()
-    tables = [
-        pltpu.make_async_copy(src.at[pl.ds(pl.multiple_of(chip * 256, 256), 256)], dst, lsem.at[i])
-        for i, (src, dst) in enumerate(((cosine, cos_v), (sine, sin_v)))
-    ]
-    for copy in tables:
-        copy.start()
-    row_task = sum_rows(out_rows, row_scratch, wires, at)
-    gate_task = expert_sum(g_gate, gate_sum, expert_scratch, wires, at)
-    out_task = gather_sums(columns, OUT_Q, landings, wires, at)
-    next(row_task)
-    next(gate_task)
-
-    def start_out():
-        columns_in.wait()
-        next(out_task)
-
-    beside = [
-        lambda: next(row_task),
-        lambda: next(gate_task),
-        start_out,
-        lambda: next(gate_task),
-        lambda: next(row_task),
-        lambda: next(out_task),
-        lambda: finish(gate_task),
-        lambda: next(out_task),
-    ]
+def attend_back(q, kv, d_o, lse, dq, scratch, chip, turned_back, beside):
+    probs, acc, kt, qt, dot_, qz, oz, dqt = scratch
     qt[...] = jnp.transpose(q[...].astype(F32) * 0.125).astype(BF)
     dot_[...] = jnp.transpose(d_o[...].astype(F32)).astype(BF)
     for kb in range(8):
-        kt[kb] = jnp.transpose(kv[256 * kb : 256 * kb + 256, 0:256].astype(F32)).astype(BF)
-    acc[...] = jnp.zeros_like(acc)
+        block = kv[kb // 2, kb % 2, :, :, 0:256].reshape(256, 256)
+        kt[kb] = jnp.transpose(block.astype(F32)).astype(BF)
     allowed = iota((256, 768), 0) <= iota((256, 768), 1) % 256
     for j in range(4):
         u, half = j // 2, j % 2
+        keys, values = slice(128 * u, 128 * u + 128), slice(256 + 128 * u, 384 + 128 * u)
+        if half == 0:
+            acc[...] = jnp.zeros_like(acc)
         qz[...] = jnp.zeros_like(qz)
         oz[...] = jnp.zeros_like(oz)
         for g in range(3):
@@ -1012,102 +1023,60 @@
             oz[64 * half : 64 * half + 64, 256 * g : 256 * g + 256] = dot_[64 * h : 64 * h + 64]
         level = lse[j, 0:1]
 
-        def share(kb, centre, masked):
+        def d_share(kb):
+            return dot(kv[kb // 2, kb % 2, :, :, values].reshape(256, 128), oz[...])
+
+        def share_of(kb, centre, masked):
             rows = pl.ds(pl.multiple_of(kb * 256, 256), 256)
-            p = jnp.exp(dot(kv[rows, 128 * u : 128 * u + 128], qz[...]) - level)
+            block = kv[kb // 2, kb % 2, :, :, keys].reshape(256, 128)
+            p = jnp.exp(dot(block, qz[...]) - level)
             if masked:
                 p = jnp.where(allowed, p, 0.0)
             probs[rows] = p
-            dp = dot(kv[rows, 256 + 128 * u : 384 + 128 * u], oz[...])
-            grads[rows] = dp
-            acc[rows, 256 + 128 * u : 384 + 128 * u] += dot_t(p.astype(BF), oz[...])
-            return centre + jnp.sum((p * dp).reshape(32, 8, 768), 0)
+            acc[rows, 128:256] += dot_t(p.astype(BF), oz[...])
+            return centre + jnp.sum((p * d_share(kb)).reshape(32, 8, 768), 0)
 
         centre = lax.fori_loop(
-            0, chip, functools.partial(share, masked=False), jnp.zeros((8, 768), F32)
+            0, chip, functools.partial(share_of, masked=False), jnp.zeros((8, 768), F32)
         )
-        centre = share(chip, centre, True)
+        beside(4 * j)
+        centre = share_of(chip, centre, True)
         centre = jnp.sum(centre, 0, keepdims=True)
-        beside[2 * j]()
+        beside(4 * j + 1)
 
         def back(kb, total):
             rows = pl.ds(pl.multiple_of(kb * 256, 256), 256)
-            ds = (probs[rows] * (grads[rows] - centre)).astype(BF)
-            acc[rows, 128 * u : 128 * u + 128] += dot_t(ds, qz[...])
+            ds = (probs[rows] * (d_share(kb) - centre)).astype(BF)
+            acc[rows, 0:128] += dot_t(ds, qz[...])
             return total + dot(kt[kb, 64 * j : 64 * j + 64], ds)
 
-        total = lax.fori_loop(0, chip + 1, back, jnp.zeros((64, 768), F32))
+        total = lax.fori_loop(0, chip, back, jnp.zeros((64, 768), F32))
+        beside(4 * j + 2)
+        total = back(chip, total)
         for g in range(3):
             h = 3 * j + g
             dqt[64 * h : 64 * h + 64] = total[:, 256 * g : 256 * g + 256] * 0.125
-        beside[2 * j + 1]()
-    for kb in range(8):
-        for part in range(2):
-            at_row = 256 * kb + 128 * part
-            dkv[part, kb] = acc[at_row : at_row + 128].astype(BF)
-    for copy in tables:
-        copy.wait()
-    dq[...] = turn(jnp.transpose(dqt[...]), cos_v[...], -sin_v[...]).astype(BF)
-    parts = final(row_task)
-    for part in range(2):
-        cut = slice(64 * part, 64 * part + 64)
-        block_out[cut] = (middle[cut] + parts[part]).astype(BF)
-    finish(out_task)
-    lanes = pl.ds(pl.multiple_of(xx // 2 * OUT_Q, 128), OUT_Q)
-    for part in range(3):
-        unit_o[part] = columns[xx % 2, z, y, part, :, lanes]
-    wires.close()
-
-
-def attend_back_call(q, kv, d_o, lse, out_rows, middle, g_out, g_gate, cosine, sine):
-    return pl.pallas_call(
-        attend_back_kernel,
-        out_shape=[
-            shape((256, 768)),
-            shape((2, 8, 128, 512)),
-            shape((ROWS, WIDTH)),
-            shape((3, 16, OUT_Q)),
-            shape((2, 192, FF), F32),
-        ],
-        in_specs=[vm()] * 6 + [hbm()] * 4,
-        out_specs=[vm()] * 5,
-        scratch_shapes=[
-            pltpu.VMEM((LENGTH, 768), F32),
-            pltpu.VMEM((LENGTH, 768), F32),
-            pltpu.VMEM((8, 256, 256), BF),
-            pltpu.VMEM((768, 256), BF),
-            pltpu.VMEM((768, 256), BF),
-            pltpu.VMEM((128, 768), BF),
-            pltpu.VMEM((128, 768), BF),
-            pltpu.VMEM((LENGTH, 512), F32),
-            pltpu.VMEM((768, 256), F32),
-            pltpu.VMEM((256, 128), F32),
-            pltpu.VMEM((256, 128), F32),
-            pltpu.VMEM((2, 4, 4, 3, 16, OUT_H), BF),
-            *sum_rows_scratch(WIDTH),
-            *landing_shapes(OUT_Q),
-            *expert_sum_scratch(192, FF),
-            *wire_sems(56),
-            pltpu.SemaphoreType.DMA((3,)),
-        ],
-        compiler_params=pltpu.CompilerParams(
-            collective_id=5, has_side_effects=True, vmem_limit_bytes=VMEM_BYTES
-        ),
-        name="attend_back",
-    )(
-        q, kv, d_o, lse, out_rows.reshape(4, 2, 2, 2, 64, WIDTH), middle, g_out,
-        g_gate.reshape(2, 2, 4, 192, FF), cosine, sine,
-    )
-
-
-def last_kernel(
-    dkv, dq, h1t, weights, unit_o, small, x, d_mid, rows, g_up, cosine, sine,
-    grad_in, g_q, g_k, g_v, g_o, g_m, up_sum,
-    whole, product, arrived, slots, taken, cos_v, sin_v, *rest,
+        if half == 1:
+            for kb in range(8):
+                for part in range(2):
+                    row = 256 * kb + 128 * part
+                    kv[kb // 2, kb % 2, part, :, keys] = acc[row : row + 128, 0:128].astype(BF)
+                    kv[kb // 2, kb % 2, part, :, values] = acc[row : row + 128, 128:256].astype(BF)
+        beside(4 * j + 3)
+    dq[...] = turned_back(jnp.transpose(dqt[...])).astype(BF)
+
+
+def backward_kernel(
+    q, d_o, lse, middle, h1t, small, x, rows,
+    kv_in, d_mid, out_rows, g_out, g_gate, g_up, weights, cosine, sine,
+    grad_in, block_out, g_q, g_k, g_v, g_o, g_m, gate_sum, up_sum,
+    columns, whole, kv, dq, product, arrived, slots, taken, cos_v, sin_v, *rest,
 ):
-    landings = [rest[3 * i : 3 * i + 3] for i in range(3)]
-    chips, expert_scratch = rest[9:15], rest[15:20]
-    ssem, rsem, lsem = rest[20:]
+    att_scratch, rest = rest[:8], rest[8:]
+    row_scratch, rest = rest[:9], rest[9:]
+    out_landings, rest = [rest[3 * i : 3 * i + 3] for i in range(3)], rest[9:]
+    in_landings, rest = [rest[3 * i : 3 * i + 3] for i in range(3)], rest[9:]
+    gate_scratch, up_scratch, chips, (ssem, rsem, lsem) = rest[:6], rest[6:12], rest[12:18], rest[18:]
     at = place()
     xx, y, z, core = at
     xh, chip = xx // 2, y * 2 + xx // 2
@@ -1115,47 +1084,94 @@
     diagonal = sibling(ring(at, 0, 2))
     greet(all_peers(at) + [near, diagonal])
     wires = Wires(ssem, rsem)
-    tables = [
-        pltpu.make_async_copy(src.at[pl.ds(pl.multiple_of(chip * 256, 256), 256)], dst, lsem.at[i])
-        for i, (src, dst) in enumerate(((cosine, cos_v), (sine, sin_v)))
-    ]
-    for copy in tables:
+
+    def local(n, src, dst):
+        copy = pltpu.make_async_copy(src, dst, lsem.at[n])
         copy.start()
-    steps = sum_chips(dkv, chips, wires, at)
+        return copy
+
+    columns_in = local(2, g_out, columns)
+    kv_loaded = local(4, kv_in, kv)
+    d_mid_in = local(5, d_mid, grad_in)
+    angle = pl.ds(pl.multiple_of(chip * 256, 256), 256)
+    angles = [local(0, cosine.at[angle], cos_v), local(1, sine.at[angle], sin_v)]
+    row_task = sum_rows(out_rows, row_scratch, wires, at)
+    gate_task = expert_sum(g_gate, gate_sum, gate_scratch, wires, at)
+    up_task = expert_sum(g_up, up_sum, up_scratch, wires, at)
+    out_task = gather_sums(columns, OUT_Q, out_landings, wires, at)
+    next(row_task)
+    next(gate_task)
+    columns_in.wait()
+    next(out_task)
+
+    def put_out():
+        parts = final(row_task)
+        for part in range(2):
+            cut = slice(64 * part, 64 * part + 64)
+            block_out[cut] = (middle[cut] + parts[part]).astype(BF)
+
+    steps_beside = {
+        3: lambda: next(row_task),
+        9: lambda: next(gate_task),
+        12: lambda: next(row_task),
+    }
+
+    def beside(n):
+        if n in steps_beside:
+            steps_beside[n]()
+
+    def turned_back(values):
+        for copy in angles:
+            copy.wait()
+        return turn(values, cos_v[...], -sin_v[...])
+
+    weights_in = local(3, weights, whole)
+    kv_loaded.wait()
+    attend_back(q, kv, d_o, lse, dq, att_scratch, chip, turned_back, beside)
+    steps = sum_chips(kv, chips, wires, at)
     next(steps)
-    up_task = expert_sum(g_up, up_sum, expert_scratch, wires, at)
+    n, inverse = normed(x[...].astype(F32))
+    next(gate_task)
     next(up_task)
-    n, inverse = normed(x[...].astype(F32))
+    next(out_task)
     next(steps)
+    next(out_task)
+    parts = final(steps)
+    next(out_task)
     next(up_task)
-    parts = final(steps)
-    for copy in tables:
-        copy.wait()
     total = jnp.concatenate(parts, 0)
     dk = turn(total[:, 0:256], cos_v[...], -sin_v[...]).astype(BF)
     grads = jnp.concatenate([dq[...], dk, total[:, 256:512].astype(BF)], 1)
-    into = weights[:, :, :, :, :, 0:COL_M].reshape(WIDTH, COL_M)
-    back = dot_t(grads, into)
+    weights_in.wait()
+    back = dot_t(grads, whole[:, :, :, :, :, 0:COL_M].reshape(WIDTH, COL_M))
     product[0] = back[0:128]
     product[1] = back[128:256]
     swap = wires.go(product.at[1 - core], arrived, near)
-    whole[:, :, :, :, :, 0:COL_M] = dot(h1t[...], grads).astype(BF).reshape(2, 4, 4, 3, 16, COL_M)
+    for i in range(8):
+        made = dot(h1t[192 * i : 192 * i + 192], grads).astype(BF)
+        whole[i // 4, i % 4, :, :, :, 0:COL_M] = made.reshape(4, 3, 16, COL_M)
     whole[:, :, :, :, :, COL_END:IN_H] = jnp.zeros((2, 4, 4, 3, 16, IN_H - COL_END), BF)
+    put_out()
     got([swap])
     d_hidden = product[core] + arrived[...]
     line = jnp.sum(d_hidden * n, 0, keepdims=True)
-    tiny = small[...] + jnp.where(iota((128, WIDTH), 0) == EXPERTS, line, 0.0)
+    tiny = small[...] + jnp.where(iota((40, WIDTH), 0) == EXPERTS, line, 0.0)
+    tiny = jnp.concatenate([tiny, jnp.zeros((88, WIDTH), F32)], 0)
     whole[:, :, :, :, :, COL_M:COL_END] = (
         jnp.transpose(tiny).astype(BF).reshape(2, 4, 4, 3, 16, 128)
     )
-    sums = gather_sums(whole, IN_Q, landings, wires, at)
+    sums = gather_sums(whole, IN_Q, in_landings, wires, at)
     next(sums)
-    grad_in[...] = d_mid[...] + norm_back(d_hidden, rows[0:1], n, inverse)
+    d_mid_in.wait()
+    grad_in[...] += norm_back(d_hidden, rows[0:1], n, inverse)
     next(up_task)
+    finish(gate_task, out_task)
     finish(sums, up_task)
-    lanes = pl.ds(pl.multiple_of(xh * IN_Q, 128), IN_Q)
-    unit = jnp.concatenate([whole[xx % 2, z, y, part, :, lanes] for part in range(3)], 0)
-    unit = jnp.concatenate([unit, unit_o[...].reshape(48, OUT_Q)], 1)
+    in_lanes = pl.ds(pl.multiple_of(xh * IN_Q, 128), IN_Q)
+    out_lanes = pl.ds(pl.multiple_of(xh * OUT_Q, 128), OUT_Q)
+    unit = jnp.concatenate([whole[xx % 2, z, y, part, :, in_lanes] for part in range(3)], 0)
+    out_unit = jnp.concatenate([columns[xx % 2, z, y, part, :, out_lanes] for part in range(3)], 0)
+    unit = jnp.concatenate([unit, out_unit], 1)
     slots[...] = dot(regroup_back(), unit).astype(BF).reshape(4, 16, STAGE)
     mine = core * 2 + xh
     copies = [
@@ -1177,41 +1193,61 @@
     wires.close()
 
 
-def last_call(dkv, dq, h1t, weights, unit_o, small, x, d_mid, rows, g_up, cosine, sine):
+def backward_call(
+    q, d_o, lse, middle, h1t, small, x, rows, kv, d_mid,
+    out_rows, g_out, g_gate, g_up, weights, cosine, sine,
+):
     return pl.pallas_call(
-        last_kernel,
+        backward_kernel,
         out_shape=[
             shape((ROWS, WIDTH), F32),
+            shape((ROWS, WIDTH)),
             shape((12, WIDTH), F32),
             shape((12, 512), F32),
             shape((12, 512), F32),
             shape((12, WIDTH), F32),
             shape((12, 128), F32),
             shape((2, 192, FF), F32),
+            shape((2, 192, FF), F32),
         ],
-        in_specs=[vm()] * 9 + [hbm()] * 3,
-        out_specs=[vm()] * 7,
+        in_specs=[vm()] * 8 + [hbm()] * 9,
+        out_specs=[vm()] * 9,
         scratch_shapes=[
+            pltpu.VMEM((2, 4, 4, 3, 16, OUT_H), BF),
             pltpu.VMEM((2, 4, 4, 3, 16, IN_H), BF),
+            pltpu.VMEM((4, 2, 2, 128, 512), BF),
+            pltpu.VMEM((256, 768), BF),
             pltpu.VMEM((2, ROWS, WIDTH), F32),
             pltpu.VMEM((ROWS, WIDTH), F32),
             pltpu.VMEM((4, 16, STAGE), BF),
             pltpu.VMEM((4, 16, STAGE), BF),
             pltpu.VMEM((256, 128), F32),
             pltpu.VMEM((256, 128), F32),
+            pltpu.VMEM((LENGTH, 768), F32),
+            pltpu.VMEM((LENGTH, 256), F32),
+            pltpu.VMEM((8, 256, 256), BF),
+            pltpu.VMEM((768, 256), BF),
+            pltpu.VMEM((768, 256), BF),
+            pltpu.VMEM((128, 768), BF),
+            pltpu.VMEM((128, 768), BF),
+            pltpu.VMEM((768, 256), F32),
+            *sum_rows_scratch(WIDTH),
+            *landing_shapes(OUT_Q),
             *landing_shapes(IN_Q),
+            *expert_sum_scratch(192, FF),
+            *expert_sum_scratch(192, FF),
             *sum_scratch(128, 512),
-            *expert_sum_scratch(192, FF),
-            *wire_sems(56),
-            pltpu.SemaphoreType.DMA((2,)),
+            *wire_sems(112),
+            pltpu.SemaphoreType.DMA((6,)),
         ],
         compiler_params=pltpu.CompilerParams(
-            collective_id=6, has_side_effects=True, vmem_limit_bytes=VMEM_BYTES
+            collective_id=5, has_side_effects=True, vmem_limit_bytes=VMEM_BYTES
         ),
-        name="weight_grad",
+        name="backward",
     )(
-        dkv.reshape(2, 4, 2, 128, 512), dq, h1t, weights, unit_o, small, x, d_mid, rows,
-        g_up.reshape(2, 2, 4, 192, FF), cosine, sine,
+        q, d_o, lse, middle, h1t, small, x, rows, kv, d_mid,
+        out_rows.reshape(4, 2, 2, 2, 64, WIDTH), g_out, g_gate.reshape(2, 2, 4, 192, FF),
+        g_up.reshape(2, 2, 4, 192, FF), weights, cosine, sine,
     )
 
 
@@ -1261,16 +1297,13 @@
     ) = forward_call(
         stage, x, routes[0], cosine, sine, dy.reshape(2, 64, WIDTH), w_gate, w_up, w_down
     )
-    kv = kv.reshape(LENGTH, 512)
     out_rows, d_rows, g_gate, g_up, g_down = expert_call(tall, all_dy, gate_full, up_full, down_full)
     d_mid, d_o, small, g_out, g_down = token_grad_call(
         d_rows, middle, gates, dy, rows, router, wo, ot, g_down
     )
-    dq, dkv, block_out, unit_o, g_gate = attend_back_call(
-        q, kv, d_o, lse, out_rows, middle, g_out, g_gate, cosine, sine
-    )
-    grad_in, g_q, g_k, g_v, g_o, g_m, g_up = last_call(
-        dkv, dq, h1t, weights, unit_o, small, x, d_mid, rows, g_up, cosine, sine
+    grad_in, block_out, g_q, g_k, g_v, g_o, g_m, g_gate, g_up = backward_call(
+        q, d_o, lse, middle, h1t, small, x, rows, kv, d_mid,
+        out_rows, g_out, g_gate, g_up, weights, cosine, sine,
     )
     return (
         block_out[None],

time: 436 us -> 410 us (0.940)
  Pallas kernels: 406 us -> 380 us
    pallas_call x2 -> x1, Pallas kernels: 138 us -> 117 us  [backward_call(): pl.pallas_call(backward_kernel, out_shape=[shape((ROWS, WIDTH), F32), sha...]
    unnamed x19 -> x17, local copies, waits for them, and re-layouts: 14 us -> 15 us
where the time goes in v4:
time: 410 us; the launch traced here: 403 us
  Pallas kernels  380 us (93%)
  local copies, waits for them, and re-layouts  21 us (5%)
    pallas_call x1, Pallas kernels, forward_call(): pl.pallas_call(forward_kernel, out_shape=[shape((8, WIDTH), F32), shape((...  156 us
    pallas_call x1, Pallas kernels, backward_call(): pl.pallas_call(backward_kernel, out_shape=[shape((ROWS, WIDTH), F32), sha...  117 us
    pallas_call x1, Pallas kernels, token_grad_call(): pl.pallas_call(token_grad_kernel, out_shape=[shape((ROWS, WIDTH), F32), s...  55.5 us
    pallas_call x1, Pallas kernels, expert_call(): pl.pallas_call(expert_kernel, out_shape=[shape((LENGTH, WIDTH)), shape((L...  51 us
    unnamed x17, local copies, waits for them, and re-layouts  15 us

profile of v4, /device:TPU:1, one launch (start us, length us, event | category | flops | bytes accessed | tf_op | source)
XLA Modules:
  0.0 403.4 jit_solution(6874840908207663767)
XLA Ops:
  0.6 0.7 copy.30
  1.4 0.8 copy.31
  2.1 0.8 fusion.15
  2.9 0.7 fusion.18
  3.6 0.7 fusion.19
  4.4 0.8 fusion.17
  5.1 0.8 fusion.16
  5.9 0.7 fusion.6.stage
  6.6 1.4 copy.32
  8.0 155.9 %forward.1 = (f32[8,1536]{1,0:T(8,128)}, bf16[1536,128]{1,0:T(8,128)(2,1)}, bf16[256,768]{1,0:T(8,128)(2,1)}, bf16[1536,256]{1,0:T(8,128)(2,1)}, bf16[768,256]{1...) custom-call(bf16[4,16,1152]{2,1,0:T(8,128)(2,1)} %fusion.6.stage, ...), custom_call_target="tpu_custom_call" | custom-call | tf_op jit(solution)/shard_map/forward/pallas_call | solution.py:707
  163.9 51.0 %experts.1 = (bf16[2048,1536]{1,0:T(8,128)(2,1)}, bf16[2048,1664]{1,0:T(8,128)(2,1)}, bf16[2,1536,512]{2,1,0:T(8,128)(2,1)}, bf16[2,1536,512]{2,1,0:T(8,128)(2,1)}, bf16[2,512,1536]{2,1,0:T(8,128)(2,1)}) custom-call(bf16[2048,1664]{1,0:T(8,128)(2,1)} %bitcast.28, bf16[2048,1536]{1,0:T(8,128)(2,1)} %bitcast.30, bf16[2,1536,512]{2,1,0:T(8,128)(2,1)} %bitcast.34, ...), custom_call_target="tpu_custom_call" | custom-call | tf_op jit(solution)/shard_map/experts/pallas_call | solution.py:875
  214.9 55.5 %token_grad.1 = (f32[128,1536]{1,0:T(8,128)}, bf16[256,768]{1,0:T(8,128)(2,1)}, f32[40,1536]{1,0:T(8,128)}, bf16[2,4,4,3,16,768]{5,4,3,2,1,0:T(8,128)(2,1)}, f32[2,64,1536]{2,1,0:T(8,128)}) custom-call(bf16[4,2,2,2,64,1664]{5,4,3,2,1,0:T(8,128)(2,1)} %bitcast.27, f32[128,1536]{1,0:T(8,128)} %get-tuple-element.54.middle, f32[128,128]{1,0:T(8,128)} %get-tuple-element.55.gates, ...), custom_call_target="tpu_custom_call" | custom-call | tf_op jit(solution)/shard_map/token_grad/pallas_call | solution.py:977
  270.5 117.3 %backward.1 = (f32[128,1536]{1,0:T(8,128)}, bf16[128,1536]{1,0:T(8,128)(2,1)}, f32[12,1536]{1,0:T(8,128)}, f32[12,512]{1,0:T(8,128)}, f32[12,512]{1,0:T(8,128)},...) custom-call(bf16[256,768]{1,0:T(8,128)(2,1)} %get-tuple-element.47.q, ...), custom_call_target="tpu_custom_call" | custom-call | tf_op jit(solution)/shard_map/backward/pallas_call | solution.py:1200
  387.7 0.0 copy-start.2
  387.7 0.0 copy-start.1
  387.8 0.0 copy-start
  387.8 1.6 slice_reduce_fusion
  389.3 1.8 copy.43
  391.1 2.1 copy.44
  393.2 1.5 copy.45
  394.7 1.4 copy.46
  396.1 1.4 copy.47
  397.5 1.5 copy.48
  399.0 1.3 copy.49
  400.3 0.0 copy-done.2
  400.3 0.9 copy.50
  401.2 0.0 copy-done.1
  401.2 0.9 copy.51
  402.1 0.0 copy-done
  402.1 0.9 copy.52
  (2 shorter events, 0.0 us)
Async XLA Ops:
  387.7 12.6 %copy-start.2 = (f32[2,192,512]{2,1,0:T(8,128)S(1)}, f32[2,192,512]{2,1,0:T(8,128)}, u32[]{:S(2)}) copy-start(f32[2,192,512]{2,1,0:T(8,128)} %get-tuple-element.118) | copy-start | bytes 2359300
  387.7 13.4 %copy-start.1 = (f32[2,192,512]{2,1,0:T(8,128)S(1)}, f32[2,192,512]{2,1,0:T(8,128)}, u32[]{:S(2)}) copy-start(f32[2,192,512]{2,1,0:T(8,128)} %get-tuple-element.119) | copy-start | bytes 2359300
  387.8 14.3 %copy-start = (f32[2,64,1536]{2,1,0:T(8,128)S(1)}, f32[2,64,1536]{2,1,0:T(8,128)}, u32[]{:S(2)}) copy-start(f32[2,64,1536]{2,1,0:T(8,128)} %get-tuple-element.120) | copy-start | bytes 2359300

commit v5 on v4

--- a/solution.py
+++ b/solution.py
@@ -149,7 +149,7 @@
 ORDERS = ((0, 1, 2), (1, 2, 0), (2, 0, 1))
 
 
-def block_of(quarter, part, fixed, at):
+def block_of(quarter, part, fixed, at, half=None):
     x, y, z, _ = at
     whole = slice(None)
     columns = (
@@ -157,10 +157,13 @@
         if 0 in fixed
         else pl.ds(0, 2 * quarter)
     )
+    spans = {dim: whole for dim in (1, 2)}
+    if half is not None:
+        spans[1 if 2 in fixed else 2] = pl.ds(2 * half, 2)
     return (
         x % 2 if 0 in fixed else whole,
-        z if 2 in fixed else whole,
-        y if 1 in fixed else whole,
+        z if 2 in fixed else spans[2],
+        y if 1 in fixed else spans[1],
         part,
         whole,
         columns,
@@ -168,6 +171,39 @@
 
 
 def spread(ref, quarter, wires, at):
+    waits = [[], [], []]
+
+    def send(part, fixed, where, peer, half=None):
+        spot = ref.at[block_of(quarter, part, fixed, where, half)]
+        waits[part].append(wires.go(spot, spot, peer))
+
+    for phase in range(2):
+        for part in range(3):
+            got(waits[part])
+            waits[part] = []
+            fixed = ORDERS[part][phase:]
+            for step in (1, 2, 3):
+                send(part, fixed, at, ring(at, fixed[0], step))
+        yield
+    for part in range(3):
+        got(waits[part])
+        waits[part] = []
+        fixed = ORDERS[part][2:]
+        for step in (1, 3):
+            send(part, fixed, at, ring(at, fixed[0], step))
+    yield
+    for part in range(3):
+        first, waits[part] = waits[part], []
+        fixed = ORDERS[part][2:]
+        for half, step in ((0, 1), (1, 3)):
+            got([first[half]])
+            send(part, fixed, ring(at, fixed[0], 4 - step), ring(at, fixed[0], step), half)
+    yield
+    for part in range(3):
+        got(waits[part])
+
+
+def spread_direct(ref, quarter, wires, at):
     waits = [[], [], []]
     for phase in range(3):
         for part in range(3):
@@ -450,26 +486,54 @@
     orders = tuple(order[::-1] for order in ORDERS)
     waits = [[], [], []]
 
+    def half_of(part, slot, half):
+        span = pl.ds(2 * half, 2)
+        where = landings[part][0].at[slot]
+        return where.at[span] if orders[part][0] == 0 else where.at[:, span]
+
+    def first(part):
+        fixed = orders[part][:1]
+        up, across, down = (ring(at, fixed[0], step) for step in (1, 2, 3))
+        for half, peer, slot in ((0, up, 0), (1, down, 1)):
+            spot = ref.at[block_of(quarter, part, fixed, across, half)]
+            waits[part].append(wires.go(spot, half_of(part, 2, half), peer))
+        for half, peer, slot in ((1, up, 0), (0, down, 1)):
+            spot = ref.at[block_of(quarter, part, fixed, peer, half)]
+            waits[part].append(wires.go(spot, half_of(part, slot, half), peer))
+
+    def forward(part):
+        fixed = orders[part][:1]
+        passing, waits[part] = waits[part][:2], waits[part][2:]
+        for half, step in ((0, 1), (1, 3)):
+            peer = ring(at, fixed[0], step)
+            got([passing[half]])
+            index = block_of(quarter, part, fixed, peer, half)
+            ref[index] = (
+                ref[index].astype(F32) + half_of(part, 2, half)[...].astype(F32)
+            ).astype(BF)
+            waits[part].append(wires.go(ref.at[index], half_of(part, half, half), peer))
+
     def send(part, phase):
         fixed = orders[part][: phase + 1]
-        dim = fixed[-1]
         for step in (1, 2, 3):
-            peer = ring(at, dim, step)
+            peer = ring(at, fixed[-1], step)
             spot = ref.at[block_of(quarter, part, fixed, peer)]
             waits[part].append(wires.go(spot, landings[part][phase].at[step - 1], peer))
 
     def add(part, phase):
         got(waits[part])
         waits[part] = []
-        fixed = orders[part][: phase + 1]
-        index = block_of(quarter, part, fixed, at)
+        index = block_of(quarter, part, orders[part][: phase + 1], at)
         total = ref[index].astype(F32)
-        for step in range(3):
+        for step in range(3 if phase else 2):
             total += landings[part][phase][step].astype(F32)
         ref[index] = total.astype(BF)
 
     for part in range(3):
-        send(part, 0)
+        first(part)
+    yield
+    for part in range(3):
+        forward(part)
     yield
     for phase in range(3):
         for part in range(3):
@@ -553,11 +617,11 @@
 
 
 def forward_kernel(
-    stage, x, routes, cosine, sine, dy, w_gate, w_up, w_down,
+    w_query, w_key, w_value, w_out, w_small, x, routes, cosine, sine, dy, w_gate, w_up, w_down,
     rows, router, q, h1t, ot, lse, middle, gates,
     weights_out, wo_out, kv_out, tall, all_dy, gate_full, up_full, down_full,
     weights, columns, wo, kv, both, slots, cos_v, sin_v, o, tall_own, product, arrived,
-    scores, vt, qt, qz, out_t, ssem, rsem, lsem,
+    scores, vt, qt, qz, out_t, stage, ssem, rsem, lsem,
 ):
     at = place()
     xx, y, z, core = at
@@ -575,6 +639,15 @@
     angle = pl.ds(pl.multiple_of(chip * 256, 256), 256)
     angles = [local(0, cosine.at[angle], cos_v), local(1, sine.at[angle], sin_v)]
     dy_in = local(2, dy, all_dy.at[y, xh, core])
+    stage[...] = jnp.zeros_like(stage)
+    for i in range(2):
+        left, right, cut = stage.at[2 * i], stage.at[2 * i + 1], 768 * i + OUT_Q
+        left[0:12, 0:IN_Q] = w_query[:, 768 * i : 768 * i + 768]
+        left[0:12, IN_Q:STAGE] = w_out[:, 768 * i : cut]
+        right[0:12, 0:256] = w_key[:, 256 * i : 256 * i + 256]
+        right[0:12, 256:512] = w_value[:, 256 * i : 256 * i + 256]
+        right[0:12, 512:640] = w_small[...]
+        right[0:12, IN_Q:STAGE] = w_out[:, cut : cut + OUT_Q]
     mine = core * 2 + xh
     first = [
         wires.go(stage.at[peer[3] * 2 + peer[0] // 2], slots.at[mine], peer)
@@ -590,8 +663,8 @@
     for part in range(3):
         weights[xx % 2, z, y, part, :, in_lanes] = unit[16 * part : 16 * part + 16, 0:IN_Q]
         columns[xx % 2, z, y, part, :, out_lanes] = unit[16 * part : 16 * part + 16, IN_Q:STAGE]
-    in_task = spread(weights, IN_Q, wires, at)
-    out_task = spread(columns, OUT_Q, wires, at)
+    in_task = spread_direct(weights, IN_Q, wires, at)
+    out_task = spread_direct(columns, OUT_Q, wires, at)
     dy_task = share_rows_two(all_dy, wires, at)
     gate_task = expert_spread(w_gate, gate_full, wires, at, lsem.at[3])
     up_task = expert_spread(w_up, up_full, wires, at, lsem.at[4])
@@ -703,7 +776,9 @@
     wires.close()
 
 
-def forward_call(stage, x, routes, cosine, sine, dy, w_gate, w_up, w_down):
+def forward_call(
+    w_query, w_key, w_value, w_out, w_small, x, routes, cosine, sine, dy, w_gate, w_up, w_down
+):
     return pl.pallas_call(
         forward_kernel,
         out_shape=[
@@ -724,7 +799,7 @@
             shape((2, 2, 4, 192, FF)),
             shape((2, 2, 4, 64, WIDTH)),
         ],
-        in_specs=[vm()] * 3 + [hbm()] * 2 + [vm()] * 4,
+        in_specs=[vm()] * 7 + [hbm()] * 2 + [vm()] * 4,
         out_specs=[vm()] * 8 + [hbm()] * 8,
         scratch_shapes=[
             pltpu.VMEM((2, 4, 4, 3, 16, IN_H), BF),
@@ -744,6 +819,7 @@
             pltpu.VMEM((768, 256), BF),
             pltpu.VMEM((128, 768), BF),
             pltpu.VMEM((768, 256), F32),
+            pltpu.VMEM((4, 16, STAGE), BF),
             *wire_sems(144),
             pltpu.SemaphoreType.DMA((10,)),
         ],
@@ -751,7 +827,7 @@
             collective_id=1, has_side_effects=True, vmem_limit_bytes=VMEM_BYTES
         ),
         name="forward",
-    )(stage, x, routes, cosine, sine, dy, w_gate, w_up, w_down)
+    )(w_query, w_key, w_value, w_out, w_small, x, routes, cosine, sine, dy, w_gate, w_up, w_down)
 
 
 def expert_kernel(
@@ -760,19 +836,22 @@
     big, wide, a_rows, y_rows, r_rows, back, wg, wu, wd, gg, gu, gd, m_s, dg_s, du_s, slot_t, sem,
 ):
     ctx = lax.axis_index("ctx")
+    def copy(n, src, dst):
+        made = pltpu.make_async_copy(src, dst, sem.at[n])
+        made.start()
+        return made
+
+    quarters = [pl.ds(512 * i, 512) for i in range(4)]
     loads = [
-        pltpu.make_async_copy(src, dst, sem.at[i])
-        for i, (src, dst) in enumerate(
-            ((tall, big), (dy, wide), (w_gate, wg), (w_up, wu), (w_down, wd))
-        )
+        (copy(2 * i, tall.at[rows], big.at[rows]), copy(2 * i + 1, dy.at[rows], wide.at[rows]))
+        for i, rows in enumerate(quarters)
     ]
-    for copy in loads:
-        copy.start()
+    w_loads = [
+        copy(8 + i, src, dst) for i, (src, dst) in enumerate(((w_gate, wg), (w_up, wu), (w_down, wd)))
+    ]
     lane = iota((128, 128), 1)
     earlier = (iota((128, 128), 1) < iota((128, 128), 0)).astype(F32).astype(BF)
     slots = iota((CAP, 128), 0).astype(F32)
-    loads[0].wait()
-    loads[1].wait()
 
     def collect(b, _):
         rows = pl.ds(pl.multiple_of(b * 128, 128), 128)
@@ -782,9 +861,10 @@
         hot = (gate > 0.0) & (lane < EXPERTS)
         rank = dot(earlier, hot.astype(F32).astype(BF))
         slot = jnp.where(hot, rank, -1.0)
-        slot_t[...] = jnp.transpose(slot)
+        ranks = slot_t.at[b % 4]
+        ranks[...] = jnp.transpose(slot)
         picks = [
-            (slot_t[pl.ds(2 * ctx + i, 1), :] == slots).astype(F32).astype(BF) for i in range(2)
+            (ranks[pl.ds(2 * ctx + i, 1), :] == slots).astype(F32).astype(BF) for i in range(2)
         ]
         pick = jnp.concatenate(picks, 0)
         found = dot(pick, big[rows, :]).astype(BF)
@@ -800,9 +880,12 @@
         back[b] = put.astype(F32).astype(BF)
         return 0
 
-    lax.fori_loop(0, 16, collect, 0)
-    for copy in loads[2:]:
-        copy.wait()
+    for i in range(4):
+        for load in loads[i]:
+            load.wait()
+        lax.fori_loop(4 * i, 4 * i + 4, collect, 0, unroll=4)
+    for load in w_loads:
+        load.wait()
     stores = []
     for e in range(2):
         number = 2 * ctx + e
@@ -841,9 +924,7 @@
         gg[e] = t_dot(a_rows[e, :, 0:WIDTH], dg_s[...]).astype(BF)
         gu[e] = t_dot(a_rows[e, :, 0:WIDTH], du_s[...]).astype(BF)
         for i, (src, dst) in enumerate(((gd, g_down), (gg, g_gate), (gu, g_up))):
-            copy = pltpu.make_async_copy(src.at[e], dst.at[e], sem.at[5 + 3 * e + i])
-            copy.start()
-            stores.append(copy)
+            stores.append(copy(11 + 3 * e + i, src.at[e], dst.at[e]))
 
         def to_tokens(c, _):
             rows = pl.ds(pl.multiple_of(c * 384, 384), 384)
@@ -861,13 +942,12 @@
         wide[rows, :] = dot(put, jnp.concatenate([r_rows[0, packed], r_rows[1, packed]], 0)).astype(BF)
         return 0
 
-    lax.fori_loop(0, 16, hand_back, 0)
-    for i, (src, dst) in enumerate(((big, d_rows), (wide, out_rows))):
-        copy = pltpu.make_async_copy(src, dst, sem.at[i])
-        copy.start()
-        stores.append(copy)
-    for copy in stores:
-        copy.wait()
+    for i, rows in enumerate(quarters):
+        lax.fori_loop(4 * i, 4 * i + 4, hand_back, 0, unroll=4)
+        stores.append(copy(2 * i, big.at[rows], d_rows.at[rows]))
+        stores.append(copy(2 * i + 1, wide.at[rows], out_rows.at[rows]))
+    for store in stores:
+        store.wait()
 
 
 def expert_call(tall, dy, w_gate, w_up, w_down):
@@ -899,8 +979,8 @@
             pltpu.VMEM((slots, FF), BF),
             pltpu.VMEM((slots, FF), BF),
             pltpu.VMEM((slots, FF), BF),
-            pltpu.VMEM((128, 128), F32),
-            pltpu.SemaphoreType.DMA((11,)),
+            pltpu.VMEM((4, 128, 128), F32),
+            pltpu.SemaphoreType.DMA((17,)),
         ],
         compiler_params=pltpu.CompilerParams(vmem_limit_bytes=VMEM_BYTES),
         name="experts",
@@ -1113,6 +1193,7 @@
     steps_beside = {
         3: lambda: next(row_task),
         9: lambda: next(gate_task),
+        10: lambda: next(out_task),
         12: lambda: next(row_task),
     }
 
@@ -1251,6 +1332,23 @@
     )
 
 
+def results_kernel(*refs):
+    half = len(refs) // 2
+    for src, dst in zip(refs[:half], refs[half:]):
+        dst[...] = src[...]
+
+
+def results_call(*arrays):
+    return pl.pallas_call(
+        results_kernel,
+        out_shape=[shape(a.shape, a.dtype) for a in arrays],
+        in_specs=[vm()] * len(arrays),
+        out_specs=[vm()] * len(arrays),
+        compiler_params=pltpu.CompilerParams(vmem_limit_bytes=VMEM_BYTES),
+        name="results",
+    )(*arrays)
+
+
 def tables():
     frequency = np.exp(
         np.arange(HEAD // 2, dtype=np.float32) * np.float32(-2.0 * math.log(10000.0) / HEAD)
@@ -1263,39 +1361,20 @@
     )
 
 
-def stage_weights(w_query, key_weight, value_weight, w_out, w_router, gain_attn, gain_ffn):
-    small = jnp.concatenate([w_router, gain_attn[:, None], gain_ffn[:, None]], 1)
-    small = jnp.pad(small, ((0, 0), (0, IN_H - COL_M - EXPERTS - 2)))
-    quarters = []
-    for i in range(2):
-        own_out = w_out[:, 768 * i : 768 * i + 768]
-        quarters.append([w_query[:, 768 * i : 768 * i + 768], own_out[:, :OUT_Q]])
-        quarters.append(
-            [
-                key_weight[:, 256 * i : 256 * i + 256],
-                value_weight[:, 256 * i : 256 * i + 256],
-                small,
-                own_out[:, OUT_Q:],
-            ]
-        )
-    stage = jnp.stack([jnp.concatenate(quarter, 1) for quarter in quarters])
-    return jnp.pad(stage, ((0, 0), (0, 4), (0, 0)))
-
-
 def body(
     block_in, routes, cotangent, gain_attn, w_query, key_weight, value_weight, w_out,
     gain_ffn, w_router, w_gate, w_up, w_down,
 ):
     cosine, sine = (jnp.asarray(table) for table in tables())
     x, dy = block_in[0], cotangent[0]
-    stage = stage_weights(
-        w_query, key_weight, value_weight, w_out, w_router, gain_attn, gain_ffn
-    )
+    small = jnp.concatenate([w_router, gain_attn[:, None], gain_ffn[:, None]], 1)
+    small = jnp.pad(small, ((0, 0), (0, 128 - EXPERTS - 2)))
     (
         rows, router, q, h1t, ot, lse, middle, gates,
         weights, wo, kv, tall, all_dy, gate_full, up_full, down_full,
     ) = forward_call(
-        stage, x, routes[0], cosine, sine, dy.reshape(2, 64, WIDTH), w_gate, w_up, w_down
+        w_query, key_weight, value_weight, w_out, small, x, routes[0], cosine, sine,
+        dy.reshape(2, 64, WIDTH), w_gate, w_up, w_down,
     )
     out_rows, d_rows, g_gate, g_up, g_down = expert_call(tall, all_dy, gate_full, up_full, down_full)
     d_mid, d_o, small, g_out, g_down = token_grad_call(
@@ -1304,6 +1383,9 @@
     grad_in, block_out, g_q, g_k, g_v, g_o, g_m, g_gate, g_up = backward_call(
         q, d_o, lse, middle, h1t, small, x, rows, kv, d_mid,
         out_rows, g_out, g_gate, g_up, weights, cosine, sine,
+    )
+    block_out, grad_in, g_q, g_k, g_v, g_o, g_gate, g_up, g_down = results_call(
+        block_out, grad_in, g_q, g_k, g_v, g_o, g_gate, g_up, g_down
     )
     return (
         block_out[None],

time: 410 us -> 386 us (0.941)
  local copies, waits for them, and re-layouts: 21 us -> 4.21 us
  Pallas kernels: 380 us -> 374 us
    unnamed x17 -> x4, local copies, waits for them, and re-layouts: 15 us -> 2.02 us
    pallas_call x1, Pallas kernels: 51 us -> 40.9 us  [expert_call(): pl.pallas_call(expert_kernel, out_shape=[shape((LENGTH, WIDTH)), shape((L...]
where the time goes in v5:
time: 386 us; the launch traced here: 381 us
  Pallas kernels  374 us (97%)
  local copies, waits for them, and re-layouts  4.21 us (1%)
    pallas_call x1, Pallas kernels, forward_call(): pl.pallas_call(forward_kernel, out_shape=[shape((8, WIDTH), F32), shape((...  157 us
    pallas_call x1, Pallas kernels, backward_call(): pl.pallas_call(backward_kernel, out_shape=[shape((ROWS, WIDTH), F32), sha...  118 us
    pallas_call x1, Pallas kernels, token_grad_call(): pl.pallas_call(token_grad_kernel, out_shape=[shape((ROWS, WIDTH), F32), s...  55.5 us
    pallas_call x1, Pallas kernels, expert_call(): pl.pallas_call(expert_kernel, out_shape=[shape((LENGTH, WIDTH)), shape((L...  40.9 us

profile of v5, /device:TPU:1, one launch (start us, length us, event | category | flops | bytes accessed | tf_op | source)
XLA Modules:
  0.0 380.9 jit_solution(11319287872839817664)
XLA Ops:
  0.6 0.7 copy.30
  1.4 0.8 copy.31
  2.1 1.4 fusion.4.w_small
  3.5 1.4 copy.32
  4.9 156.5 %forward.1 = (f32[8,1536]{1,0:T(8,128)}, bf16[1536,128]{1,0:T(8,128)(2,1)}, bf16[256,768]{1,0:T(8,128)(2,1)}, bf16[1536,256]{1,0:T(8,128)(2,1)}, bf16[768,256]{1...) custom-call(bf16[12,1536]{1,0:T(8,128)(2,1)} %w_query.1, ...), custom_call_target="tpu_custom_call" | custom-call | tf_op jit(solution)/shard_map/forward/pallas_call | solution.py:782
  161.5 40.9 %experts.1 = (bf16[2048,1536]{1,0:T(8,128)(2,1)}, bf16[2048,1664]{1,0:T(8,128)(2,1)}, bf16[2,1536,512]{2,1,0:T(8,128)(2,1)}, bf16[2,1536,512]{2,1,0:T(8,128)(2,1)}, bf16[2,512,1536]{2,1,0:T(8,128)(2,1)}) custom-call(bf16[2048,1664]{1,0:T(8,128)(2,1)} %bitcast.20, bf16[2048,1536]{1,0:T(8,128)(2,1)} %bitcast.22, bf16[2,1536,512]{2,1,0:T(8,128)(2,1)} %bitcast.26, ...), custom_call_target="tpu_custom_call" | custom-call | tf_op jit(solution)/shard_map/experts/pallas_call | solution.py:955
  202.3 55.5 %token_grad.1 = (f32[128,1536]{1,0:T(8,128)}, bf16[256,768]{1,0:T(8,128)(2,1)}, f32[40,1536]{1,0:T(8,128)}, bf16[2,4,4,3,16,768]{5,4,3,2,1,0:T(8,128)(2,1)}, f32[2,64,1536]{2,1,0:T(8,128)}) custom-call(bf16[4,2,2,2,64,1664]{5,4,3,2,1,0:T(8,128)(2,1)} %bitcast.19, f32[128,1536]{1,0:T(8,128)} %get-tuple-element.63.middle, f32[128,128]{1,0:T(8,128)} %get-tuple-element.64.gates, ...), custom_call_target="tpu_custom_call" | custom-call | tf_op jit(solution)/shard_map/token_grad/pallas_call | solution.py:1057
  257.9 117.6 %backward.1 = (f32[128,1536]{1,0:T(8,128)}, bf16[128,1536]{1,0:T(8,128)(2,1)}, f32[12,1536]{1,0:T(8,128)}, f32[12,512]{1,0:T(8,128)}, f32[12,512]{1,0:T(8,128)},...) custom-call(bf16[256,768]{1,0:T(8,128)(2,1)} %get-tuple-element.56.q, ...), custom_call_target="tpu_custom_call" | custom-call | tf_op jit(solution)/shard_map/backward/pallas_call | solution.py:1281
  375.4 0.0 copy-start
  375.4 4.0 %results.1 = (bf16[128,1536]{1,0:T(8,128)(2,1)}, f32[128,1536]{1,0:T(8,128)}, f32[12,1536]{1,0:T(8,128)}, f32[12,512]{1,0:T(8,128)}, f32[12,512]{1,0:T(8,128)}, ...) custom-call(bf16[128,1536]{1,0:T(8,128)(2,1)} %get-tuple-element.81.refs_0_, ...), custom_call_target="tpu_custom_call" | custom-call | tf_op jit(solution)/shard_map/results/pallas_call | solution.py:1342
  379.4 0.0 copy-done
  379.4 0.7 slice_reduce_fusion
  380.1 0.6 copy.34
Async XLA Ops:
  375.4 4.0 %copy-start = (f32[12,128]{1,0:T(8,128)S(1)}, f32[12,128]{1,0:T(8,128)}, u32[]{:S(2)}) copy-start(f32[12,128]{1,0:T(8,128)} %get-tuple-element.92) | copy-start | bytes 18436

commit v6 on v5

--- a/solution.py
+++ b/solution.py
@@ -558,13 +558,17 @@
     return values * inverse, inverse
 
 
-def attend(q, kv, o, ot, lse, scratch, chip, beside):
+def allowed_last(xh):
+    return iota((512, 768), 0) <= iota((512, 768), 1) % 256 + 256 * xh
+
+
+def attend(q, kv, o, ot, lse, scratch, place_of, beside):
     scores, vt, qt, qz, out_t = scratch
+    y, xh = place_of
     qt[...] = jnp.transpose(q[...].astype(F32) * 0.125).astype(BF)
-    for kb in range(8):
-        block = kv[kb // 2, kb % 2, :, :, 256:512].reshape(256, 256)
+    for kb in range(4):
+        block = kv[kb, :, :, :, 256:512].reshape(512, 256)
         vt[kb] = jnp.transpose(block.astype(F32)).astype(BF)
-    allowed = iota((256, 768), 0) <= iota((256, 768), 1) % 256
     for j in range(4):
         u, half = j // 2, j % 2
         qz[...] = jnp.zeros_like(qz)
@@ -573,40 +577,40 @@
             qz[64 * half : 64 * half + 64, 256 * g : 256 * g + 256] = qt[64 * h : 64 * h + 64]
 
         def score(kb):
-            rows = pl.ds(pl.multiple_of(kb * 256, 256), 256)
-            keys = kv[kb // 2, kb % 2, :, :, 128 * u : 128 * u + 128].reshape(256, 128)
+            rows = pl.ds(pl.multiple_of(kb * 512, 512), 512)
+            keys = kv[kb, :, :, :, 128 * u : 128 * u + 128].reshape(512, 128)
             return rows, dot(keys, qz[...])
 
         def top(kb, most):
             rows, s = score(kb)
             scores[rows] = s
-            return jnp.maximum(most, jnp.max(s.reshape(32, 8, 768), 0))
-
-        most = lax.fori_loop(0, chip, top, jnp.full((8, 768), -1e30, F32))
-        rows, s = score(chip)
-        s = jnp.where(allowed, s, -1e30)
+            return jnp.maximum(most, jnp.max(s.reshape(64, 8, 768), 0))
+
+        most = lax.fori_loop(0, y, top, jnp.full((8, 768), -1e30, F32))
+        rows, s = score(y)
+        s = jnp.where(allowed_last(xh), s, -1e30)
         scores[rows] = s
-        most = jnp.maximum(most, jnp.max(s.reshape(32, 8, 768), 0))
+        most = jnp.maximum(most, jnp.max(s.reshape(64, 8, 768), 0))
         most = jnp.max(most, 0, keepdims=True)
 
         def raise_(kb, total):
-            rows = pl.ds(pl.multiple_of(kb * 256, 256), 256)
+            rows = pl.ds(pl.multiple_of(kb * 512, 512), 512)
             e = jnp.exp(scores[rows] - most)
             scores[rows] = e
-            return total + jnp.sum(e.reshape(32, 8, 768), 0)
+            return total + jnp.sum(e.reshape(64, 8, 768), 0)
 
         beside[2 * j]()
-        total = lax.fori_loop(0, chip + 1, raise_, jnp.zeros((8, 768), F32))
+        total = lax.fori_loop(0, y + 1, raise_, jnp.zeros((8, 768), F32))
         total = jnp.sum(total, 0, keepdims=True)
         lse[j] = jnp.broadcast_to(most + jnp.log(total), (8, 768))
         inverse = 1.0 / total
 
         def mix(kb, acc):
-            rows = pl.ds(pl.multiple_of(kb * 256, 256), 256)
+            rows = pl.ds(pl.multiple_of(kb * 512, 512), 512)
             p = (scores[rows] * inverse).astype(BF)
             return acc + dot(vt[kb, 64 * j : 64 * j + 64], p)
 
-        acc = lax.fori_loop(0, chip + 1, mix, jnp.zeros((64, 768), F32))
+        acc = lax.fori_loop(0, y + 1, mix, jnp.zeros((64, 768), F32))
         for g in range(3):
             h = 3 * j + g
             out_t[64 * h : 64 * h + 64] = acc[:, 256 * g : 256 * g + 256]
@@ -708,6 +712,7 @@
     a = [wires.go(column, column, ring(at, 0, 2))]
     next(out_task)
     h1t[...] = jnp.transpose(hidden.astype(F32)).astype(BF)
+    chosen = jnp.transpose(routes[...].astype(F32))
     next(up_task)
     next(down_task)
     next(out_task)
@@ -735,7 +740,7 @@
         lambda: None,
         lambda: None,
     ]
-    attend(q, kv, o, ot, lse, (scores, vt, qt, qz, out_t), chip, beside)
+    attend(q, kv, o, ot, lse, (scores, vt, qt, qz, out_t), (y, xh), beside)
     got(swap)
     wo_kept = local(8, wo, wo_out)
 
@@ -744,9 +749,10 @@
     swap = wires.go(product.at[0], arrived, near)
     product[1] = dot(o[core], full)
     lane = iota((ROWS, 128), 1)
-    named = routes[:, 0:1] == lane
+    spots = lane.astype(F32)
+    named = chosen[:, 0:1] == spots
     for i in range(1, TOPK):
-        named = named | (routes[:, i : i + 1] == lane)
+        named = named | (chosen[:, i : i + 1] == spots)
     got([swap])
     mid = x[...].astype(F32) + product[1] + arrived[...]
     middle[...] = mid
@@ -815,7 +821,7 @@
             pltpu.VMEM((2, ROWS, WIDTH), F32),
             pltpu.VMEM((ROWS, WIDTH), F32),
             pltpu.VMEM((LENGTH, 768), F32),
-            pltpu.VMEM((8, 256, 256), BF),
+            pltpu.VMEM((4, 256, 512), BF),
             pltpu.VMEM((768, 256), BF),
             pltpu.VMEM((128, 768), BF),
             pltpu.VMEM((768, 256), F32),
@@ -1004,7 +1010,7 @@
 def token_grad_kernel(
     d_rows, middle, gates, dy, rows, router, wo, ot, g_down,
     d_mid, d_o, small, g_out, down_sum,
-    low, product, *rest,
+    low, *rest,
 ):
     scratch, expert_scratch, (ssem, rsem) = rest[:9], rest[9:15], rest[15:]
     at = place()
@@ -1017,9 +1023,10 @@
     down_task = expert_sum(g_down, down_sum, expert_scratch, wires, at)
     next(down_task)
     next(steps)
-    next(down_task)
     n, inverse = normed(middle[...])
     hidden = (n * rows[1:2]).astype(BF)
+    next(steps)
+    next(down_task)
     parts = final(steps)
     total = jnp.concatenate(parts, 0)
     d_hidden = total[:, 0:WIDTH]
@@ -1042,14 +1049,8 @@
     got([swap])
     chip_rows = low[...].reshape(256, WIDTH)
     d_o[...] = dot_t(chip_rows, wo[...].reshape(768, WIDTH)).astype(BF)
-    product[...] = dot(ot[...], chip_rows).astype(BF).reshape(4, 4, 3, 16, WIDTH)
-    lanes = pl.ds(pl.multiple_of((1 - core) * 768, 128), 768)
-    mine = pl.ds(pl.multiple_of(core * 768, 128), 768)
-    swap = wires.go(product.at[:, :, :, :, lanes], g_out.at[core], near)
-    for i in range(4):
-        g_out[core, i] = product[i, :, :, :, mine]
+    g_out[...] = dot(ot[...], chip_rows).astype(BF).reshape(4, 4, 3, 16, WIDTH)
     finish(down_task)
-    got([swap])
     wires.close()
 
 
@@ -1060,14 +1061,13 @@
             shape((ROWS, WIDTH), F32),
             shape((256, 768)),
             shape((40, WIDTH), F32),
-            shape((2, 4, 4, 3, 16, 768)),
+            shape((4, 4, 3, 16, WIDTH)),
             shape((2, 64, WIDTH), F32),
         ],
         in_specs=[hbm()] + [vm()] * 7 + [hbm()],
         out_specs=[vm()] * 5,
         scratch_shapes=[
             pltpu.VMEM((2, ROWS, WIDTH), BF),
-            pltpu.VMEM((4, 4, 3, 16, WIDTH), BF),
             *sum_rows_scratch(TALL),
             *expert_sum_scratch(64, WIDTH),
             *wire_sems(24),
@@ -1082,14 +1082,14 @@
     )
 
 
-def attend_back(q, kv, d_o, lse, dq, scratch, chip, turned_back, beside):
+def attend_back(q, kv, lse, dq, scratch, place_of, turned_back, beside):
     probs, acc, kt, qt, dot_, qz, oz, dqt = scratch
+    y, xh = place_of
     qt[...] = jnp.transpose(q[...].astype(F32) * 0.125).astype(BF)
-    dot_[...] = jnp.transpose(d_o[...].astype(F32)).astype(BF)
-    for kb in range(8):
-        block = kv[kb // 2, kb % 2, :, :, 0:256].reshape(256, 256)
+    dot_[...] = jnp.transpose(dq[...].astype(F32)).astype(BF)
+    for kb in range(4):
+        block = kv[kb, :, :, :, 0:256].reshape(512, 256)
         kt[kb] = jnp.transpose(block.astype(F32)).astype(BF)
-    allowed = iota((256, 768), 0) <= iota((256, 768), 1) % 256
     for j in range(4):
         u, half = j // 2, j % 2
         keys, values = slice(128 * u, 128 * u + 128), slice(256 + 128 * u, 384 + 128 * u)
@@ -1104,35 +1104,34 @@
         level = lse[j, 0:1]
 
         def d_share(kb):
-            return dot(kv[kb // 2, kb % 2, :, :, values].reshape(256, 128), oz[...])
+            return dot(kv[kb, :, :, :, values].reshape(512, 128), oz[...])
 
         def share_of(kb, centre, masked):
-            rows = pl.ds(pl.multiple_of(kb * 256, 256), 256)
-            block = kv[kb // 2, kb % 2, :, :, keys].reshape(256, 128)
-            p = jnp.exp(dot(block, qz[...]) - level)
+            rows = pl.ds(pl.multiple_of(kb * 512, 512), 512)
+            p = jnp.exp(dot(kv[kb, :, :, :, keys].reshape(512, 128), qz[...]) - level)
             if masked:
-                p = jnp.where(allowed, p, 0.0)
+                p = jnp.where(allowed_last(xh), p, 0.0)
             probs[rows] = p
             acc[rows, 128:256] += dot_t(p.astype(BF), oz[...])
-            return centre + jnp.sum((p * d_share(kb)).reshape(32, 8, 768), 0)
+            return centre + jnp.sum((p * d_share(kb)).reshape(64, 8, 768), 0)
 
         centre = lax.fori_loop(
-            0, chip, functools.partial(share_of, masked=False), jnp.zeros((8, 768), F32)
+            0, y, functools.partial(share_of, masked=False), jnp.zeros((8, 768), F32)
         )
         beside(4 * j)
-        centre = share_of(chip, centre, True)
+        centre = share_of(y, centre, True)
         centre = jnp.sum(centre, 0, keepdims=True)
         beside(4 * j + 1)
 
         def back(kb, total):
-            rows = pl.ds(pl.multiple_of(kb * 256, 256), 256)
+            rows = pl.ds(pl.multiple_of(kb * 512, 512), 512)
             ds = (probs[rows] * (d_share(kb) - centre)).astype(BF)
             acc[rows, 0:128] += dot_t(ds, qz[...])
             return total + dot(kt[kb, 64 * j : 64 * j + 64], ds)
 
-        total = lax.fori_loop(0, chip, back, jnp.zeros((64, 768), F32))
+        total = lax.fori_loop(0, y, back, jnp.zeros((64, 768), F32))
         beside(4 * j + 2)
-        total = back(chip, total)
+        total = back(y, total)
         for g in range(3):
             h = 3 * j + g
             dqt[64 * h : 64 * h + 64] = total[:, 256 * g : 256 * g + 256] * 0.125
@@ -1147,8 +1146,8 @@
 
 
 def backward_kernel(
-    q, d_o, lse, middle, h1t, small, x, rows,
-    kv_in, d_mid, out_rows, g_out, g_gate, g_up, weights, cosine, sine,
+    q, lse, h1t, small, x, rows,
+    d_o, middle, kv_in, d_mid, out_rows, g_out, g_gate, g_up, weights, cosine, sine,
     grad_in, block_out, g_q, g_k, g_v, g_o, g_m, gate_sum, up_sum,
     columns, whole, kv, dq, product, arrived, slots, taken, cos_v, sin_v, *rest,
 ):
@@ -1170,9 +1169,14 @@
         copy.start()
         return copy
 
-    columns_in = local(2, g_out, columns)
+    mine = pl.ds(pl.multiple_of(core * 768, 128), 768)
+    theirs = pl.ds(pl.multiple_of((1 - core) * 768, 128), 768)
+    columns_in = local(2, g_out.at[:, :, :, :, mine], columns.at[core])
+    columns_swap = wires.go(g_out.at[:, :, :, :, theirs], columns.at[core], near)
     kv_loaded = local(4, kv_in, kv)
     d_mid_in = local(5, d_mid, grad_in)
+    d_o_in = local(6, d_o, dq)
+    middle_in = local(7, middle, product.at[0])
     angle = pl.ds(pl.multiple_of(chip * 256, 256), 256)
     angles = [local(0, cosine.at[angle], cos_v), local(1, sine.at[angle], sin_v)]
     row_task = sum_rows(out_rows, row_scratch, wires, at)
@@ -1181,16 +1185,21 @@
     out_task = gather_sums(columns, OUT_Q, out_landings, wires, at)
     next(row_task)
     next(gate_task)
-    columns_in.wait()
-    next(out_task)
 
     def put_out():
         parts = final(row_task)
+        middle_in.wait()
         for part in range(2):
             cut = slice(64 * part, 64 * part + 64)
-            block_out[cut] = (middle[cut] + parts[part]).astype(BF)
+            block_out[cut] = (product[0, cut] + parts[part]).astype(BF)
+
+    def start_out():
+        columns_in.wait()
+        got([columns_swap])
+        next(out_task)
 
     steps_beside = {
+        1: start_out,
         3: lambda: next(row_task),
         9: lambda: next(gate_task),
         10: lambda: next(out_task),
@@ -1208,7 +1217,8 @@
 
     weights_in = local(3, weights, whole)
     kv_loaded.wait()
-    attend_back(q, kv, d_o, lse, dq, att_scratch, chip, turned_back, beside)
+    d_o_in.wait()
+    attend_back(q, kv, lse, dq, att_scratch, (y, xh), turned_back, beside)
     steps = sum_chips(kv, chips, wires, at)
     next(steps)
     n, inverse = normed(x[...].astype(F32))
@@ -1223,6 +1233,7 @@
     total = jnp.concatenate(parts, 0)
     dk = turn(total[:, 0:256], cos_v[...], -sin_v[...]).astype(BF)
     grads = jnp.concatenate([dq[...], dk, total[:, 256:512].astype(BF)], 1)
+    put_out()
     weights_in.wait()
     back = dot_t(grads, whole[:, :, :, :, :, 0:COL_M].reshape(WIDTH, COL_M))
     product[0] = back[0:128]
@@ -1232,7 +1243,6 @@
         made = dot(h1t[192 * i : 192 * i + 192], grads).astype(BF)
         whole[i // 4, i % 4, :, :, :, 0:COL_M] = made.reshape(4, 3, 16, COL_M)
     whole[:, :, :, :, :, COL_END:IN_H] = jnp.zeros((2, 4, 4, 3, 16, IN_H - COL_END), BF)
-    put_out()
     got([swap])
     d_hidden = product[core] + arrived[...]
     line = jnp.sum(d_hidden * n, 0, keepdims=True)
@@ -1275,7 +1285,7 @@
 
 
 def backward_call(
-    q, d_o, lse, middle, h1t, small, x, rows, kv, d_mid,
+    q, lse, h1t, small, x, rows, d_o, middle, kv, d_mid,
     out_rows, g_out, g_gate, g_up, weights, cosine, sine,
 ):
     return pl.pallas_call(
@@ -1291,7 +1301,7 @@
             shape((2, 192, FF), F32),
             shape((2, 192, FF), F32),
         ],
-        in_specs=[vm()] * 8 + [hbm()] * 9,
+        in_specs=[vm()] * 6 + [hbm()] * 11,
         out_specs=[vm()] * 9,
         scratch_shapes=[
             pltpu.VMEM((2, 4, 4, 3, 16, OUT_H), BF),
@@ -1306,7 +1316,7 @@
             pltpu.VMEM((256, 128), F32),
             pltpu.VMEM((LENGTH, 768), F32),
             pltpu.VMEM((LENGTH, 256), F32),
-            pltpu.VMEM((8, 256, 256), BF),
+            pltpu.VMEM((4, 256, 512), BF),
             pltpu.VMEM((768, 256), BF),
             pltpu.VMEM((768, 256), BF),
             pltpu.VMEM((128, 768), BF),
@@ -1319,14 +1329,14 @@
             *expert_sum_scratch(192, FF),
             *sum_scratch(128, 512),
             *wire_sems(112),
-            pltpu.SemaphoreType.DMA((6,)),
+            pltpu.SemaphoreType.DMA((8,)),
         ],
         compiler_params=pltpu.CompilerParams(
-            collective_id=5, has_side_effects=True, vmem_limit_bytes=VMEM_BYTES
+            collective_id=5, has_side_effects=True, vmem_limit_bytes=63 << 20
         ),
         name="backward",
     )(
-        q, d_o, lse, middle, h1t, small, x, rows, kv, d_mid,
+        q, lse, h1t, small, x, rows, d_o, middle, kv, d_mid,
         out_rows.reshape(4, 2, 2, 2, 64, WIDTH), g_out, g_gate.reshape(2, 2, 4, 192, FF),
         g_up.reshape(2, 2, 4, 192, FF), weights, cosine, sine,
     )
@@ -1373,7 +1383,7 @@
         rows, router, q, h1t, ot, lse, middle, gates,
         weights, wo, kv, tall, all_dy, gate_full, up_full, down_full,
     ) = forward_call(
-        w_query, key_weight, value_weight, w_out, small, x, routes[0], cosine, sine,
+        w_query, key_weight, value_weight, w_out, small, x, routes[0].T, cosine, sine,
         dy.reshape(2, 64, WIDTH), w_gate, w_up, w_down,
     )
     out_rows, d_rows, g_gate, g_up, g_down = expert_call(tall, all_dy, gate_full, up_full, down_full)
@@ -1381,7 +1391,7 @@
         d_rows, middle, gates, dy, rows, router, wo, ot, g_down
     )
     grad_in, block_out, g_q, g_k, g_v, g_o, g_m, g_gate, g_up = backward_call(
-        q, d_o, lse, middle, h1t, small, x, rows, kv, d_mid,
+        q, lse, h1t, small, x, rows, d_o, middle, kv, d_mid,
         out_rows, g_out, g_gate, g_up, weights, cosine, sine,
     )
     block_out, grad_in, g_q, g_k, g_v, g_o, g_gate, g_up, g_down = results_call(

time: 386 us -> 382 us (0.990)
  no operation moved by 1% of the time
where the time goes in v6:
time: 382 us; the launch traced here: 376 us
  Pallas kernels  371 us (97%)
    pallas_call x1, Pallas kernels, forward_call(): pl.pallas_call(forward_kernel, out_shape=[shape((8, WIDTH), F32), shape((...  155 us
    pallas_call x1, Pallas kernels, backward_call(): pl.pallas_call(backward_kernel, out_shape=[shape((ROWS, WIDTH), F32), sha...  116 us
    pallas_call x1, Pallas kernels, token_grad_call(): pl.pallas_call(token_grad_kernel, out_shape=[shape((ROWS, WIDTH), F32), s...  54.5 us
    pallas_call x1, Pallas kernels, expert_call(): pl.pallas_call(expert_kernel, out_shape=[shape((LENGTH, WIDTH)), shape((L...  41.1 us

profile of v6, /device:TPU:1, one launch (start us, length us, event | category | flops | bytes accessed | tf_op | source)
XLA Modules:
  0.0 376.2 jit_solution(1810805701169710912)
XLA Ops:
  0.6 0.7 copy.29
  1.4 0.8 copy.30
  2.1 1.4 fusion.4.w_small
  3.5 155.2 %forward.1 = (f32[8,1536]{1,0:T(8,128)}, bf16[1536,128]{1,0:T(8,128)(2,1)}, bf16[256,768]{1,0:T(8,128)(2,1)}, bf16[1536,256]{1,0:T(8,128)(2,1)}, bf16[768,256]{1...) custom-call(bf16[12,1536]{1,0:T(8,128)(2,1)} %w_query.1, ...), custom_call_target="tpu_custom_call" | custom-call | tf_op jit(solution)/shard_map/forward/pallas_call | solution.py:788
  158.7 41.1 %experts.1 = (bf16[2048,1536]{1,0:T(8,128)(2,1)}, bf16[2048,1664]{1,0:T(8,128)(2,1)}, bf16[2,1536,512]{2,1,0:T(8,128)(2,1)}, bf16[2,1536,512]{2,1,0:T(8,128)(2,1)}, bf16[2,512,1536]{2,1,0:T(8,128)(2,1)}) custom-call(bf16[2048,1664]{1,0:T(8,128)(2,1)} %bitcast.22, bf16[2048,1536]{1,0:T(8,128)(2,1)} %bitcast.24, bf16[2,1536,512]{2,1,0:T(8,128)(2,1)} %bitcast.28, ...), custom_call_target="tpu_custom_call" | custom-call | tf_op jit(solution)/shard_map/experts/pallas_call | solution.py:961
  199.8 54.5 %token_grad.1 = (f32[128,1536]{1,0:T(8,128)}, bf16[256,768]{1,0:T(8,128)(2,1)}, f32[40,1536]{1,0:T(8,128)}, bf16[4,4,3,16,1536]{4,3,2,1,0:T(8,128)(2,1)}, f32[2,64,1536]{2,1,0:T(8,128)}) custom-call(bf16[4,2,2,2,64,1664]{5,4,3,2,1,0:T(8,128)(2,1)} %bitcast.21, f32[128,1536]{1,0:T(8,128)} %get-tuple-element.65.middle, f32[128,128]{1,0:T(8,128)} %get-tuple-element.66.gates, ...), custom_call_target="tpu_custom_call" | custom-call | tf_op jit(solution)/shard_map/token_grad/pallas_call | solution.py:1058
  254.3 116.1 %backward.1 = (f32[128,1536]{1,0:T(8,128)}, bf16[128,1536]{1,0:T(8,128)(2,1)}, f32[12,1536]{1,0:T(8,128)}, f32[12,512]{1,0:T(8,128)}, f32[12,512]{1,0:T(8,128)},...) custom-call(bf16[256,768]{1,0:T(8,128)(2,1)} %get-tuple-element.56.q, ...), custom_call_target="tpu_custom_call" | custom-call | tf_op jit(solution)/shard_map/backward/pallas_call | solution.py:1291
  370.5 0.0 copy-start
  370.5 4.0 %results.1 = (bf16[128,1536]{1,0:T(8,128)(2,1)}, f32[128,1536]{1,0:T(8,128)}, f32[12,1536]{1,0:T(8,128)}, f32[12,512]{1,0:T(8,128)}, f32[12,512]{1,0:T(8,128)}, ...) custom-call(bf16[128,1536]{1,0:T(8,128)(2,1)} %get-tuple-element.81.refs_0_, ...), custom_call_target="tpu_custom_call" | custom-call | tf_op jit(solution)/shard_map/results/pallas_call | solution.py:1352
  374.5 0.0 copy-done
  374.5 0.7 slice_reduce_fusion
  375.2 0.6 copy.32
Async XLA Ops:
  370.5 4.0 %copy-start = (f32[12,128]{1,0:T(8,128)S(1)}, f32[12,128]{1,0:T(8,128)}, u32[]{:S(2)}) copy-start(f32[12,128]{1,0:T(8,128)} %get-tuple-element.92) | copy-start | bytes 18436
